TPU v7x, 32 devices: a whole 2x2x4 slice. The times are simulated.
32 devices in a mesh: seq: 8 (over z, y), mp: 4 (over x, core).
Axes of the slice: x: 2, y: 2, z: 4, core: 2. Of those that a mesh axis runs over, the one named last changes fastest.
Arguments:
- tokens: bfloat16 [2, 2048, 2048], P(None, 'seq'), may hold values from -6 to 6
- lengths: int32 [2, 3], replicated, may hold values from 1 to 2046, as said below
- norm1_gain: float32 [2048], replicated, may hold values from 0.5 to 1.5
- q_down: bfloat16 [2048, 1024], P(None, 'mp'), may hold values from -0.125 to 0.125
- latent_gain: float32 [1024], replicated, may hold values from 0.5 to 1.5
- q_up: bfloat16 [1024, 4096], P(None, 'mp'), may hold values from -0.25 to 0.25
- kv_proj: bfloat16 [2048, 512], replicated, may hold values from -0.125 to 0.125
- out_proj: bfloat16 [4096, 2048], P('mp'), may hold values from -0.75 to 0.75
- norm2_gain: float32 [2048], replicated, may hold values from 0.5 to 1.5
- w_gate: bfloat16 [2048, 5632], P(None, 'mp'), may hold values from -0.125 to 0.125
- w_up: bfloat16 [2048, 5632], P(None, 'mp'), may hold values from -0.125 to 0.125
- w_down: bfloat16 [5632, 2048], P('mp'), may hold values from -0.078125 to 0.078125
- cotangent: bfloat16 [2, 2048, 2048], P(None, 'seq'), may hold values from -6 to 6
Outputs:
- layer_out: bfloat16 [2, 2048, 2048], P(None, 'seq')
- grad_tokens: bfloat16 [2, 2048, 2048], P(None, 'seq')
- grad_norm1_gain: float32 [2048], P('seq')
- grad_q_down: float32 [2048, 1024], P('seq', 'mp')
- grad_latent_gain: float32 [1024], P('seq')
- grad_q_up: float32 [1024, 4096], P('seq', 'mp')
- grad_kv_proj: float32 [2048, 512], P(('seq', 'mp'))
- grad_out_proj: float32 [4096, 2048], P('mp', 'seq')
- grad_norm2_gain: float32 [2048], P('seq')
- grad_w_gate: float32 [2048, 5632], P('seq', 'mp')
- grad_w_up: float32 [2048, 5632], P('seq', 'mp')
- grad_w_down: float32 [5632, 2048], P('mp', 'seq')
Inputs may be any that keep to these rules, and one draw needn't show every extreme that they name: Row m holds the lengths of the three sequences of micro-batch m in order, summing to 2048; the first and the last are shorter than 256. In one micro-batch the first and the last both have length 1.
All inputs are finite; a program needn't handle non-finite values.
Results may differ from a plain program's by a relative error of at most 0.025.
Values may be sent and summed in bfloat16 or wider, within the bound.
A program may use at most 256 MiB of HBM per device.

v0:
```python
import math

import jax
import jax.numpy as jnp
from jax import lax
from jax.sharding import PartitionSpec as P

EPS = 1e-06
BASE = 10000.0
NEG_LARGE = -1e30


def normalize(values):
    return values * lax.rsqrt(jnp.mean(values * values, axis=-1, keepdims=True) + EPS)


def norm_backward(grad_hat, normed, values):
    inverse = lax.rsqrt(jnp.mean(values * values, axis=-1, keepdims=True) + EPS)
    return inverse * (grad_hat - normed * jnp.mean(grad_hat * normed, axis=-1, keepdims=True))


def inner_rows(left, right):
    return lax.dot_general(
        left, right, (((0,), (0,)), ((), ())), preferred_element_type=jnp.float32
    )


def inner_cols(left, right):
    return lax.dot_general(
        left, right, (((1,), (1,)), ((), ())), preferred_element_type=jnp.float32
    )


def documents(lengths_row, rows):
    first_end = lengths_row[0]
    second_end = first_end + lengths_row[1]
    doc_ids = (rows >= first_end).astype(jnp.int32) + (rows >= second_end).astype(jnp.int32)
    starts = jnp.where(rows >= second_end, second_end, jnp.where(rows >= first_end, first_end, 0))
    return (doc_ids, rows - starts)


def rotation(positions, head_dim):
    half = head_dim // 2
    freqs = BASE ** (-2.0 * jnp.arange(half, dtype=jnp.float32) / head_dim)
    angles = positions.astype(jnp.float32)[:, None] * freqs[None, :]
    return (jnp.cos(angles), jnp.sin(angles))


def rotate(values, cosine, sine):
    half = values.shape[-1] // 2
    first = values[..., :half]
    second = values[..., half:]
    return jnp.concatenate(
        [first * cosine - second * sine, second * cosine + first * sine], axis=-1
    )


def unrotate(grads, cosine, sine):
    half = grads.shape[-1] // 2
    first = grads[..., :half]
    second = grads[..., half:]
    return jnp.concatenate(
        [first * cosine + second * sine, second * cosine - first * sine], axis=-1
    )


def local(
    tokens,
    lengths,
    norm1_gain,
    q_down,
    latent_gain,
    q_up,
    kv_proj,
    out_proj,
    norm2_gain,
    w_gate,
    w_up,
    w_down,
    cotangent,
):
    micro_count, rows_local, width = tokens.shape
    seq_count = lax.axis_size("seq")
    seq_index = lax.axis_index("seq")
    part_index = lax.axis_index("mp")
    head_dim = kv_proj.shape[1] // 2
    heads_local = q_up.shape[1] // head_dim
    rank_local = q_down.shape[1]
    total_rows = rows_local * seq_count
    quarter = rows_local // lax.axis_size("mp")
    scale = head_dim ** (-0.5)
    key_block = rows_local * math.gcd(seq_count, max(1, 1024 // rows_local))
    block_count = total_rows // key_block
    local_rows = seq_index * rows_local + jnp.arange(rows_local, dtype=jnp.int32)
    layer_outs = []
    input_grads = []
    totals = None
    reduced = None
    reduced_proj = None
    for micro_index in range(micro_count):
        lengths_row = lengths[micro_index]
        query_docs, query_places = documents(lengths_row, local_rows)
        cosine, sine = rotation(query_places, head_dim)
        inputs = tokens[micro_index].astype(jnp.float32)
        normed_in = normalize(inputs)
        first_in = (normed_in * norm1_gain).astype(jnp.bfloat16)
        latent_part = jnp.dot(first_in, q_down, preferred_element_type=jnp.float32).astype(
            jnp.bfloat16
        )
        latent = lax.all_gather(latent_part, "mp", axis=1, tiled=True)
        latent_f = latent.astype(jnp.float32)
        latent_hat = normalize(latent_f)
        latent_in = (latent_hat * latent_gain).astype(jnp.bfloat16)
        query_pre = jnp.dot(latent_in, q_up, preferred_element_type=jnp.float32).reshape(
            rows_local, heads_local, head_dim
        )
        queries = rotate(query_pre, cosine[:, None, :], sine[:, None, :]).astype(jnp.bfloat16)
        key_value = jnp.dot(first_in, kv_proj, preferred_element_type=jnp.float32)
        keys_rotated = rotate(key_value[:, :head_dim], cosine, sine)
        packed = jnp.concatenate([keys_rotated, key_value[:, head_dim:]], axis=1).astype(
            jnp.bfloat16
        )
        piece = lax.all_gather(packed, "seq", axis=0, tiled=True)
        run_max = jnp.full((rows_local, heads_local, 1), NEG_LARGE, jnp.float32)
        key_rows = jnp.arange(piece.shape[0], dtype=jnp.int32)
        key_docs, key_places = documents(lengths_row, key_rows)
        visible = (key_docs[None, :] == query_docs[:, None]) & (
            key_rows[None, :] <= local_rows[:, None]
        )
        scores = (
            jnp.einsum(
                "thd,nd->thn", queries, piece[:, :head_dim], preferred_element_type=jnp.float32
            )
            * scale
        )
        scores = jnp.where(visible[:, None, :], scores, NEG_LARGE)
        new_max = jnp.maximum(run_max, jnp.max(scores, axis=-1, keepdims=True))
        probs = jnp.exp(scores - new_max)
        new_total = jnp.sum(probs, axis=-1, keepdims=True)
        new_acc = jnp.einsum(
            "thn,nd->thd",
            probs.astype(jnp.bfloat16),
            piece[:, head_dim:],
            preferred_element_type=jnp.float32,
        )
        run_max = new_max
        attn_f = new_acc / new_total
        log_total = run_max + jnp.log(new_total)
        attn_out = attn_f.astype(jnp.bfloat16).reshape(rows_local, heads_local * head_dim)
        branch = lax.psum(
            jnp.dot(attn_out, out_proj, preferred_element_type=jnp.float32).astype(jnp.bfloat16),
            "mp",
        ).astype(jnp.float32)
        middle = inputs + branch
        normed_mid = normalize(middle)
        second_in = (normed_mid * norm2_gain).astype(jnp.bfloat16)
        gate_pre = jnp.dot(second_in, w_gate, preferred_element_type=jnp.float32)
        up_pre = jnp.dot(second_in, w_up, preferred_element_type=jnp.float32)
        sigmoid = jax.nn.sigmoid(gate_pre)
        swish = gate_pre * sigmoid
        hidden = (swish * up_pre).astype(jnp.bfloat16)
        ffn_out = lax.psum(
            jnp.dot(hidden, w_down, preferred_element_type=jnp.float32).astype(jnp.bfloat16), "mp"
        ).astype(jnp.float32)
        layer_outs.append((middle + ffn_out).astype(jnp.bfloat16))
        grad_out = cotangent[micro_index]
        grad_down = inner_rows(hidden, grad_out)
        grad_hidden = inner_cols(grad_out, w_down)
        grad_gate = (grad_hidden * up_pre * sigmoid * (1.0 + gate_pre * (1.0 - sigmoid))).astype(
            jnp.bfloat16
        )
        grad_up = (grad_hidden * swish).astype(jnp.bfloat16)
        grad_gate_w = inner_rows(second_in, grad_gate)
        grad_up_w = inner_rows(second_in, grad_up)
        grad_second = lax.psum(
            (inner_cols(grad_gate, w_gate) + inner_cols(grad_up, w_up)).astype(jnp.bfloat16), "mp"
        ).astype(jnp.float32)
        grad_norm2 = jnp.sum(grad_second * normed_mid, axis=0)
        grad_middle = grad_out.astype(jnp.float32) + norm_backward(
            grad_second * norm2_gain, normed_mid, middle
        )
        grad_mid_low = grad_middle.astype(jnp.bfloat16)
        grad_out_w = inner_rows(attn_out, grad_mid_low)
        grad_attn_low = (
            inner_cols(grad_mid_low, out_proj)
            .reshape(rows_local, heads_local, head_dim)
            .astype(jnp.bfloat16)
        )
        delta = jnp.sum(grad_attn_low.astype(jnp.float32) * attn_f, axis=-1, keepdims=True)
        gathered = lax.all_gather(packed, "seq", axis=0, tiled=True)

        def backward_block(block_index, state):
            start = block_index * key_block
            query_grad, key_grads = state
            piece = lax.dynamic_slice_in_dim(gathered, start, key_block, 0)
            key_rows = start + jnp.arange(key_block, dtype=jnp.int32)
            key_docs, key_places = documents(lengths_row, key_rows)
            visible = (key_docs[None, :] == query_docs[:, None]) & (
                key_rows[None, :] <= local_rows[:, None]
            )
            scores = (
                jnp.einsum(
                    "thd,nd->thn", queries, piece[:, :head_dim], preferred_element_type=jnp.float32
                )
                * scale
            )
            probs = jnp.exp(jnp.where(visible[:, None, :], scores, NEG_LARGE) - log_total)
            grad_probs = jnp.einsum(
                "thd,nd->thn",
                grad_attn_low,
                piece[:, head_dim:],
                preferred_element_type=jnp.float32,
            )
            grad_scores = (probs * (grad_probs - delta)).astype(jnp.bfloat16)
            query_grad = (
                query_grad
                + jnp.einsum(
                    "thn,nd->thd",
                    grad_scores,
                    piece[:, :head_dim],
                    preferred_element_type=jnp.float32,
                )
                * scale
            )
            key_part = (
                jnp.einsum("thn,thd->nd", grad_scores, queries, preferred_element_type=jnp.float32)
                * scale
            )
            value_part = jnp.einsum(
                "thn,thd->nd",
                probs.astype(jnp.bfloat16),
                grad_attn_low,
                preferred_element_type=jnp.float32,
            )
            key_grads = lax.dynamic_update_slice_in_dim(
                key_grads, jnp.concatenate([key_part, value_part], axis=1), start, 0
            )
            return (query_grad, key_grads)

        query_grad, key_grads = lax.fori_loop(
            0,
            block_count,
            backward_block,
            (
                jnp.zeros((rows_local, heads_local, head_dim), jnp.float32),
                jnp.zeros((total_rows, 2 * head_dim), jnp.float32),
            ),
        )
        shared = lax.psum_scatter(key_grads, ("seq", "mp"), scatter_dimension=0, tiled=True)
        quarter_start = part_index * quarter
        quarter_places = lax.dynamic_slice_in_dim(query_places, quarter_start, quarter, 0)
        quarter_cos, quarter_sin = rotation(quarter_places, head_dim)
        proj_low = jnp.concatenate(
            [unrotate(shared[:, :head_dim], quarter_cos, quarter_sin), shared[:, head_dim:]], axis=1
        ).astype(jnp.bfloat16)
        first_quarter = lax.dynamic_slice_in_dim(first_in, quarter_start, quarter, 0)
        grad_proj = inner_rows(first_quarter, proj_low)
        from_keys = lax.dynamic_update_slice_in_dim(
            jnp.zeros((rows_local, width), jnp.float32),
            inner_cols(proj_low, kv_proj),
            quarter_start,
            0,
        )
        query_low = (
            unrotate(query_grad, cosine[:, None, :], sine[:, None, :])
            .astype(jnp.bfloat16)
            .reshape(rows_local, heads_local * head_dim)
        )
        grad_qup = inner_rows(latent_in, query_low)
        grad_latent = lax.psum(inner_cols(query_low, q_up).astype(jnp.bfloat16), "mp").astype(
            jnp.float32
        )
        grad_lgain = jnp.sum(grad_latent * latent_hat, axis=0)
        grad_latent_full = norm_backward(grad_latent * latent_gain, latent_hat, latent_f)
        latent_low = lax.dynamic_slice_in_dim(
            grad_latent_full, part_index * rank_local, rank_local, 1
        ).astype(jnp.bfloat16)
        grad_qdown = inner_rows(first_in, latent_low)
        grad_first = lax.psum(
            (inner_cols(latent_low, q_down) + from_keys).astype(jnp.bfloat16), "mp"
        ).astype(jnp.float32)
        grad_norm1 = jnp.sum(grad_first * normed_in, axis=0)
        input_grads.append(
            (grad_middle + norm_backward(grad_first * norm1_gain, normed_in, inputs)).astype(
                jnp.bfloat16
            )
        )
        pending = (
            grad_norm1,
            grad_qdown,
            grad_lgain,
            grad_qup,
            grad_out_w,
            grad_norm2,
            grad_gate_w,
            grad_up_w,
            grad_down,
        )
        totals = (
            (pending, grad_proj)
            if totals is None
            else jax.tree.map(jnp.add, totals, (pending, grad_proj))
        )
    summed, summed_proj = totals
    reduced = (
        lax.psum_scatter(
            summed[0].astype(jnp.bfloat16), "seq", scatter_dimension=0, tiled=True
        ).astype(jnp.float32),
        lax.psum_scatter(
            summed[1].astype(jnp.bfloat16), "seq", scatter_dimension=0, tiled=True
        ).astype(jnp.float32),
        lax.psum_scatter(
            summed[2].astype(jnp.bfloat16), "seq", scatter_dimension=0, tiled=True
        ).astype(jnp.float32),
        lax.psum_scatter(
            summed[3].astype(jnp.bfloat16), "seq", scatter_dimension=0, tiled=True
        ).astype(jnp.float32),
        lax.psum_scatter(
            summed[4].astype(jnp.bfloat16), "seq", scatter_dimension=1, tiled=True
        ).astype(jnp.float32),
        lax.psum_scatter(
            summed[5].astype(jnp.bfloat16), "seq", scatter_dimension=0, tiled=True
        ).astype(jnp.float32),
        lax.psum_scatter(
            summed[6].astype(jnp.bfloat16), "seq", scatter_dimension=0, tiled=True
        ).astype(jnp.float32),
        lax.psum_scatter(
            summed[7].astype(jnp.bfloat16), "seq", scatter_dimension=0, tiled=True
        ).astype(jnp.float32),
        lax.psum_scatter(
            summed[8].astype(jnp.bfloat16), "seq", scatter_dimension=1, tiled=True
        ).astype(jnp.float32),
    )
    reduced_proj = lax.psum_scatter(summed_proj, ("seq", "mp"), scatter_dimension=0, tiled=True)
    return (
        jnp.stack(layer_outs, axis=0),
        jnp.stack(input_grads, axis=0),
        reduced[0],
        reduced[1],
        reduced[2],
        reduced[3],
        reduced_proj,
        reduced[4],
        reduced[5],
        reduced[6],
        reduced[7],
        reduced[8],
    )


def solution(mesh):
    placed = (
        P(None, "seq", None),
        P(),
        P(),
        P(None, "mp"),
        P(),
        P(None, "mp"),
        P(),
        P("mp", None),
        P(),
        P(None, "mp"),
        P(None, "mp"),
        P("mp", None),
        P(None, "seq", None),
    )
    return jax.shard_map(
        local,
        mesh=mesh,
        in_specs=placed,
        out_specs=(
            P(None, "seq", None),
            P(None, "seq", None),
            P("seq"),
            P("seq", "mp"),
            P("seq"),
            P("seq", "mp"),
            P(("seq", "mp"), None),
            P("mp", "seq"),
            P("seq"),
            P("seq", "mp"),
            P("seq", "mp"),
            P("mp", "seq"),
        ),
        check_vma=False,
    )
```

profile of v0, /device:TPU:0, one launch (start us, length us, event | category | flops | bytes accessed | tf_op | source)
XLA Modules:
  0.0 1543.4 jit_solution(13968634985495141511)
XLA Ops:
  26.2 8.6 all_gather.14
  42.4 7.6 all_gather.16
  62.3 11.5 all-gather.3.cloned.1.call-done
  73.8 6.4 fusion.50
  80.2 44.1 %all-gather.5.cloned.1.call-done = bf16[2048,512]{1,0:T(8,128)(2,1)} async-done(((bf16[256,512]{1,0:T(8,128)(2,1)}), bf16[2048,512]{1,0:T(8,128)(2,1)}) %all-gather.5.cloned.1.call-update) | async-done | bytes 2097168 | tf_op jit(solution)/shard_map/all_gather | solution.py:123
  130.8 3.5 fusion.187
  138.7 3.4 fusion.186
  144.7 50.0 %all-reduce.19.cloned.1.call-done = (bf16[256,2048]{1,0:T(8,128)(2,1)}, bf16[256,2048]{1,0:T(8,128)(2,1)}) async-done(((bf16[256,2048]{1,0:T(8,128)(2,1)}, bf16[256,2048]{1,0:T(8,128)(2,1)}), (bf16[256,2048]{1,0:T(8,128)(2,1)}, bf16[256,2048]{1,0:T(8,128)(2,1)})) %all-reduce.19.cloned.1.call-update) | async-done | bytes 2097168 | tf_op jit(solution)/shard_map/psum | solution.py:150
  199.3 5.3 fusion.196
  211.5 4.6 multiply_convert_fusion.4
  217.9 3.5 multiply_convert_fusion.2
  233.3 47.4 %all-reduce.17.cloned.1.call-done = (bf16[256,2048]{1,0:T(8,128)(2,1)}, bf16[256,2048]{1,0:T(8,128)(2,1)}) async-done(((bf16[256,2048]{1,0:T(8,128)(2,1)}, bf16[256,2048]{1,0:T(8,128)(2,1)}), (bf16[256,2048]{1,0:T(8,128)(2,1)}, bf16[256,2048]{1,0:T(8,128)(2,1)})) %all-reduce.17.cloned.1.call-update) | async-done | bytes 2097168 | tf_op jit(solution)/shard_map/psum | solution.py:175
  280.7 5.1 fusion.93
  285.8 5.0 fusion.92
  300.3 48.4 %while.38 = (s32[]{:T(128)}, f32[256,4,256]{2,0,1:T(8,128)}, f32[2048,512]{1,0:T(8,128)}, s32[3]{0:T(128)S(1)}, s32[]{:T(128)}, /*index=5*/bf16[2048,512]{1,0:T(...) while((s32[]{:T(128)}, f32[256,4,256]{2,0,1:T(8,128)}, ...), condition=%wide.region_18.19_spmd.clone.clone.clone, body=%wide.region_17.18_spmd.clone.clone.clone.sunk | while | flops 2697207296 | bytes 67404128 | solution.py:240
  301.4 3.8 fusion.312
  305.1 3.8 fusion.314
  325.4 3.8 fusion.312
  329.2 3.8 fusion.314
  345.0 3.7 fusion.315
  348.7 4.9 convolution_convert_fusion.6
  358.8 49.4 %while.39 = (s32[]{:T(128)}, f32[256,4,256]{2,0,1:T(8,128)}, f32[2048,512]{1,0:T(8,128)}, s32[3]{0:T(128)S(1)}, s32[]{:T(128)}, /*index=5*/bf16[2048,512]{1,0:T(...) while((s32[]{:T(128)}, f32[256,4,256]{2,0,1:T(8,128)}, ...), condition=%wide.region_28.29_spmd.clone.clone.clone, body=%wide.region_27.28_spmd.clone.clone.clone.sunk | while | flops 2697207296 | bytes 65306948 | solution.py:240
  360.1 3.8 fusion.325
  363.8 3.7 fusion.327
  384.5 3.8 fusion.325
  388.3 3.7 fusion.327
  404.5 3.7 fusion.328
  419.9 35.0 %all-reduce.15.cloned.1.call-done = (bf16[256,1024]{1,0:T(8,128)(2,1)}, bf16[256,1024]{1,0:T(8,128)(2,1)}) async-done(((bf16[256,1024]{1,0:T(8,128)(2,1)}, bf16[256,1024]{1,0:T(8,128)(2,1)}), (bf16[256,1024]{1,0:T(8,128)(2,1)}, bf16[256,1024]{1,0:T(8,128)(2,1)})) %all-reduce.15.cloned.1.call-update) | async-done | bytes 1048592 | tf_op jit(solution)/shard_map/psum | solution.py:270
  468.9 3.4 add_convert_fusion.3
  476.7 4.4 add_convert_fusion.1
  484.2 4.3 add_convert_fusion.2
  492.7 4.2 add_convert_fusion
  499.5 5.4 convolution_convert_fusion.3
  504.9 5.5 convolution_convert_fusion.2
  516.2 82.2 %reduce-scatter.28.cloned.1.call-done = f32[64,512]{1,0:T(8,128)} async-done(((f32[2048,512]{1,0:T(8,128)}), f32[64,512]{1,0:T(8,128)}) %reduce-scatter.28.cloned.1.call-update) | async-done | bytes 131088 | tf_op jit(solution)/shard_map/reduce_scatter | solution.py:249
  598.4 139.1 %reduce-scatter.30.cloned.1.call-done = f32[64,512]{1,0:T(8,128)} async-done(((f32[2048,512]{1,0:T(8,128)}), f32[64,512]{1,0:T(8,128)}) %reduce-scatter.30.cloned.1.call-update) | async-done | bytes 131088 | tf_op jit(solution)/shard_map/reduce_scatter | solution.py:249
  750.4 3.7 convolution_add_fusion
  756.7 44.2 %reduce-scatter.14.cloned.1.call-done = bf16[256,256]{1,0:T(8,128)(2,1)} async-done(((bf16[2048,256]{1,0:T(8,128)(2,1)}), bf16[256,256]{1,0:T(8,128)(2,1)}) %reduce-scatter.14.cloned.1.call-update) | async-done | bytes 131088 | tf_op jit(solution)/shard_map/reduce_scatter | solution.py:309
  802.5 69.0 %reduce-scatter.16.cloned.1.call-done = bf16[128,1024]{1,0:T(8,128)(2,1)} async-done(((bf16[1024,1024]{1,0:T(8,128)(2,1)}), bf16[128,1024]{1,0:T(8,128)(2,1)}) %reduce-scatter.16.cloned.1.call-update) | async-done | bytes 262160 | tf_op jit(solution)/shard_map/reduce_scatter | solution.py:315
  873.3 89.2 %reduce-scatter.20.cloned.1.call-done = bf16[1024,256]{1,0:T(8,128)(2,1)} async-done(((bf16[1024,2048]{1,0:T(8,128)(2,1)}), bf16[1024,256]{1,0:T(8,128)(2,1)}) %reduce-scatter.20.cloned.1.call-update) | async-done | bytes 524304 | tf_op jit(solution)/shard_map/reduce_scatter | solution.py:318
  964.5 111.8 %reduce-scatter.24.cloned.1.call-done = bf16[256,1408]{1,0:T(8,128)(2,1)} async-done(((bf16[2048,1408]{1,0:T(8,128)(2,1)}), bf16[256,1408]{1,0:T(8,128)(2,1)}) %reduce-scatter.24.cloned.1.call-update) | async-done | bytes 720912 | tf_op jit(solution)/shard_map/reduce_scatter | solution.py:327
  1078.6 111.4 %reduce-scatter.22.cloned.1.call-done = bf16[256,1408]{1,0:T(8,128)(2,1)} async-done(((bf16[2048,1408]{1,0:T(8,128)(2,1)}), bf16[256,1408]{1,0:T(8,128)(2,1)}) %reduce-scatter.22.cloned.1.call-update) | async-done | bytes 720912 | tf_op jit(solution)/shard_map/reduce_scatter | solution.py:324
  1192.3 112.0 %reduce-scatter.26.cloned.1.call-done = bf16[1408,256]{1,0:T(8,128)(2,1)} async-done(((bf16[1408,2048]{1,0:T(8,128)(2,1)}), bf16[1408,256]{1,0:T(8,128)(2,1)}) %reduce-scatter.26.cloned.1.call-update) | async-done | bytes 720912 | tf_op jit(solution)/shard_map/reduce_scatter | solution.py:330
  1306.6 86.1 %all-reduce.13.cloned.1.call-done = (bf16[256,2048]{1,0:T(8,128)(2,1)}, bf16[256,2048]{1,0:T(8,128)(2,1)}, bf16[256,2048]{1,0:T(8,128)(2,1)}, bf16[256,2048]{1,0:T(8,128)(2,1)}) async-done(((bf16[256,2048]{1,0:T(8,128)(2,1)}, bf16[256,2048]{1,0:T(8,128)(2,1)}, bf16[256,2048]{1,0:T(8,128)(2,1)}, bf16[256,2048]{1,0:T(8,128)(2,1)}), (bf16[256,2048]{1,0:T(8,128)(2,1)}, bf16[256,2048]{1,0:T(8,128)(2,1)}, ...) | async-done | bytes 4194320 | tf_op jit(solution)/shard_map/psum | solution.py:162
  1392.8 3.5 fusion.97
  1396.3 37.3 %all-reduce.3 = (bf16[2048]{0:T(1024)(128)(2,1)S(1)}, bf16[1024]{0:T(1024)(128)(2,1)S(1)}, bf16[2048]{0:T(1024)(128)(2,1)S(1)}) all-reduce(bf16[2048]{0:T(1024)(128)(2,1)S(1)} %add_convert_fusion.14, bf16[1024]{0:T(1024)(128)(2,1)S(1)} %add_convert_fusion.15, ...), channel_id=4, replica_groups=mesh['seq'=8,'mp'=4] {'seq'}, use_global_device_ids=true, to_apply=%region_36.37.clone | all-reduce | flops 5120 | bytes 20480
  1435.5 5.7 fusion.115
  1444.1 92.4 %reduce-scatter.18.cloned.1.call-done = f32[64,512]{1,0:T(8,128)} async-done(((f32[2048,512]{1,0:T(8,128)}), f32[64,512]{1,0:T(8,128)}) %reduce-scatter.18.cloned.1.call-update) | async-done | bytes 131088 | tf_op jit(solution)/shard_map/reduce_scatter | solution.py:334
  (410 shorter events, 225.3 us)
Async XLA Ops:
  7.2 9.6 copy-start
  7.2 8.9 copy-start.78
  7.2 66.6 %all-gather.3.cloned.1.call-start = ((), (), s32[]{:S(2)}) async-start(), calls=%async_computation.9 | async-start | bytes 2359296 | tf_op jit(solution)/shard_map/all_gather | solution.py:123
  7.3 11.0 copy-start.91
  18.2 6.1 copy-start.13
  20.8 38.1 %copy-start.52 = (f32[256,128]{1,0:T(8,128)}, f32[256,128]{1,0:T(8,128)S(1)}, u32[]{:S(2)}) copy-start(f32[256,128]{1,0:T(8,128)S(1)} %get-tuple-element.947) | copy-start | bytes 393220
  20.8 39.6 %copy-start.48 = (f32[256,128]{1,0:T(8,128)}, f32[256,128]{1,0:T(8,128)S(1)}, u32[]{:S(2)}) copy-start(f32[256,128]{1,0:T(8,128)S(1)} %get-tuple-element.967) | copy-start | bytes 393220
  20.8 39.6 %copy-start.50 = (f32[256,128]{1,0:T(8,128)}, f32[256,128]{1,0:T(8,128)S(1)}, u32[]{:S(2)}) copy-start(f32[256,128]{1,0:T(8,128)S(1)} %get-tuple-element.968) | copy-start | bytes 393220
  21.6 102.7 %all-gather.5.cloned.1.call-start = ((), (), s32[]{:S(2)}) async-start(), calls=%async_computation.10 | async-start | bytes 2359296 | tf_op jit(solution)/shard_map/all_gather | solution.py:123
  22.6 13.5 copy-start.71
  24.3 170.4 %all-reduce.19.cloned.1.call-start = ((), (), s32[]{:S(2)}) async-start(), calls=%async_computation.23 | async-start | bytes 4194304 | tf_op jit(solution)/shard_map/psum | solution.py:150
  24.3 11.8 copy-start.33
  40.6 10.8 copy-start.34
  51.3 7.2 copy-start.36
  73.8 50.5 %copy-start.57 = (bf16[256,4,128]{2,0,1:T(8,128)(2,1)S(1)}, bf16[256,4,128]{2,0,1:T(8,128)(2,1)}, u32[]{:S(2)}) copy-start(bf16[256,4,128]{2,0,1:T(8,128)(2,1)} %get-tuple-element.925) | copy-start | bytes 786436
  144.5 136.3 %all-reduce.17.cloned.1.call-start = ((), (), s32[]{:S(2)}) async-start(), calls=%async_computation.22 | async-start | bytes 4194304 | tf_op jit(solution)/shard_map/psum | solution.py:175
  198.1 6.5 slice-start.2
  199.3 10.1 copy-start.26
  199.3 8.3 slice-start
  216.1 7.2 copy-start.65
  228.9 226.0 %all-reduce.15.cloned.1.call-start = ((), (), s32[]{:S(2)}) async-start(), calls=%async_computation.21 | async-start | bytes 2097152 | tf_op jit(solution)/shard_map/psum | solution.py:270
  285.8 6.3 copy-start.96
  358.8 49.4 %copy-start.53 = (f32[256,128]{1,0:T(8,128)S(1)}, f32[256,128]{1,0:T(8,128)}, u32[]{:S(2)}) copy-start(f32[256,128]{1,0:T(8,128)} %copy-done.52) | copy-start | bytes 393220
  409.9 7.0 copy-start.44
  418.5 179.9 %reduce-scatter.28.cloned.1.call-start = ((), (), s32[]{:S(2)}) async-start(), calls=%async_computation.18 | async-start | bytes 4325376 | tf_op jit(solution)/shard_map/reduce_scatter | solution.py:249
  419.1 318.4 %reduce-scatter.30.cloned.1.call-start = ((), (), s32[]{:S(2)}) async-start(), calls=%async_computation.19 | async-start | bytes 4325376 | tf_op jit(solution)/shard_map/reduce_scatter | solution.py:249
  419.2 35.8 %copy-start.16 = (bf16[256,1024]{1,0:T(8,128)(2,1)S(1)}, bf16[256,1024]{1,0:T(8,128)(2,1)}, u32[]{:S(2)}) copy-start(bf16[256,1024]{1,0:T(8,128)(2,1)} %copy-done.15) | copy-start | bytes 1572868
  419.2 35.8 %copy-start.18 = (bf16[256,1024]{1,0:T(8,128)(2,1)S(1)}, bf16[256,1024]{1,0:T(8,128)(2,1)}, u32[]{:S(2)}) copy-start(bf16[256,1024]{1,0:T(8,128)(2,1)} %copy-done.17) | copy-start | bytes 1572868
  419.2 35.8 %copy-start.72 = (f32[1024]{0:T(1024)S(1)}, f32[1024]{0:T(1024)}, u32[]{:S(2)}) copy-start(f32[1024]{0:T(1024)} %param.21) | copy-start | bytes 12292
  419.2 35.7 %copy-start.74 = (f32[256]{0:T(256)S(1)}, f32[256]{0:T(256)}, u32[]{:S(2)}) copy-start(f32[256]{0:T(256)} %copy-done.73) | copy-start | bytes 3076
  419.2 35.7 %copy-start.76 = (f32[256]{0:T(256)S(1)}, f32[256]{0:T(256)}, u32[]{:S(2)}) copy-start(f32[256]{0:T(256)} %copy-done.75) | copy-start | bytes 3076
  419.9 381.0 %reduce-scatter.14.cloned.1.call-start = ((), (), s32[]{:S(2)}) async-start(), calls=%async_computation.11 | async-start | bytes 1179648 | tf_op jit(solution)/shard_map/reduce_scatter | solution.py:309
  460.7 410.8 %reduce-scatter.16.cloned.1.call-start = ((), (), s32[]{:S(2)}) async-start(), calls=%async_computation.12 | async-start | bytes 2359296 | tf_op jit(solution)/shard_map/reduce_scatter | solution.py:315
  464.9 497.5 %reduce-scatter.20.cloned.1.call-start = ((), (), s32[]{:S(2)}) async-start(), calls=%async_computation.14 | async-start | bytes 4718592 | tf_op jit(solution)/shard_map/reduce_scatter | solution.py:318
  472.4 603.9 %reduce-scatter.24.cloned.1.call-start = ((), (), s32[]{:S(2)}) async-start(), calls=%async_computation.16 | async-start | bytes 6488064 | tf_op jit(solution)/shard_map/reduce_scatter | solution.py:327
  481.1 709.0 %reduce-scatter.22.cloned.1.call-start = ((), (), s32[]{:S(2)}) async-start(), calls=%async_computation.15 | async-start | bytes 6488064 | tf_op jit(solution)/shard_map/reduce_scatter | solution.py:324
  488.5 815.8 %reduce-scatter.26.cloned.1.call-start = ((), (), s32[]{:S(2)}) async-start(), calls=%async_computation.17 | async-start | bytes 6488064 | tf_op jit(solution)/shard_map/reduce_scatter | solution.py:330
  496.9 895.9 %all-reduce.13.cloned.1.call-start = ((), (), s32[]{:S(2)}) async-start(), calls=%async_computation.20 | async-start | bytes 8388608 | tf_op jit(solution)/shard_map/psum | solution.py:162
  504.9 5.5 copy-start.14
  504.9 5.5 copy-start.89
  513.4 224.2 %copy-start.92 = (f32[128]{0:T(128)S(1)}, f32[128]{0:T(128)}, u32[]{:S(2)}) copy-start(f32[128]{0:T(128)} %copy-done.91) | copy-start | bytes 1540
  513.4 224.2 %copy-start.93 = (f32[64]{0:T(128)S(1)}, f32[64]{0:T(128)}, u32[]{:S(2)}) copy-start(f32[64]{0:T(128)} %dynamic-slice_convert_fusion.4) | copy-start | bytes 772
  513.4 224.2 %copy-start.94 = (f32[64]{0:T(128)S(1)}, f32[64]{0:T(128)}, u32[]{:S(2)}) copy-start(f32[64]{0:T(128)} %dynamic-slice_convert_fusion.3) | copy-start | bytes 772
  748.6 787.8 %reduce-scatter.18.cloned.1.call-start = ((), (), s32[]{:S(2)}) async-start(), calls=%async_computation.13 | async-start | bytes 4325376 | tf_op jit(solution)/shard_map/reduce_scatter | solution.py:334
  1078.6 314.2 %copy-start.79 = (f32[2048]{0:T(1024)S(1)}, f32[2048]{0:T(1024)}, u32[]{:S(2)}) copy-start(f32[2048]{0:T(1024)} %param.19) | copy-start | bytes 24580
  1078.6 314.2 %copy-start.83 = (f32[256]{0:T(256)S(1)}, f32[256]{0:T(256)}, u32[]{:S(2)}) copy-start(f32[256]{0:T(256)} %copy-done.82) | copy-start | bytes 3076
  1078.6 314.2 %copy-start.85 = (f32[256]{0:T(256)S(1)}, f32[256]{0:T(256)}, u32[]{:S(2)}) copy-start(f32[256]{0:T(256)} %copy-done.84) | copy-start | bytes 3076
  1392.8 42.7 %copy-start.8 = (bf16[256,2048]{1,0:T(8,128)(2,1)S(1)}, bf16[256,2048]{1,0:T(8,128)(2,1)}, u32[]{:S(2)}) copy-start(bf16[256,2048]{1,0:T(8,128)(2,1)} %get-tuple-element.889) | copy-start | bytes 3145732
  (78 other events, 194.5 us)
Sparse Core Ops, SparseCore 0:
  21.7 52.0 all-gather.2
  76.5 47.7 all-gather.4
  144.6 50.0 all-reduce.18
  229.1 51.6 all-reduce.16
  418.7 36.2 all-reduce.14
  457.2 141.2 reduce-scatter.27
  600.8 136.6 reduce-scatter.29
  741.3 59.5 reduce-scatter.13
  804.4 67.0 reduce-scatter.15
  875.0 87.4 reduce-scatter.19
  966.5 109.7 reduce-scatter.23
  1080.2 109.7 reduce-scatter.21
  1194.1 110.1 reduce-scatter.25
  1306.9 85.8 all-reduce.12
  1395.5 140.9 reduce-scatter.17
where the time goes:
time: 1550 us; the launch traced here: 1540 us
  waiting for transfers between devices  1130 us (73%)
  matrix products  184 us (12%)
  other arithmetic  89.3 us (6%)
  local copies, waits for them, and re-layouts  69 us (4%)
  blocking collectives  53.5 us (3%)
  between operations  19.5 us (1%)
    reduce_scatter x2, waiting for transfers between devices, local(): lax.psum_scatter(key_grads, ('seq', 'mp'), scatter_dimension=0, tiled=True)  221 us
    reduce_scatter x1, waiting for transfers between devices, local(): lax.psum_scatter(summed[8].astype(jnp.bfloat16), 'seq', scatter_dimension...  112 us
    reduce_scatter x1, waiting for transfers between devices, local(): lax.psum_scatter(summed[7].astype(jnp.bfloat16), 'seq', scatter_dimension...  112 us
    reduce_scatter x1, waiting for transfers between devices, local(): lax.psum_scatter(summed[6].astype(jnp.bfloat16), 'seq', scatter_dimension...  111 us
    reduce_scatter x1, waiting for transfers between devices, local(): lax.psum_scatter(summed_proj, ('seq', 'mp'), scatter_dimension=0, tiled=T...  92.4 us
    reduce_scatter x1, waiting for transfers between devices, local(): lax.psum_scatter(summed[4].astype(jnp.bfloat16), 'seq', scatter_dimension...  89.2 us
    psum x1, waiting for transfers between devices, local(): lax.psum(jnp.dot(hidden, w_down, preferred_element_type=jnp.float32).asty...  86.1 us
    reduce_scatter x1, waiting for transfers between devices, local(): lax.psum_scatter(summed[3].astype(jnp.bfloat16), 'seq', scatter_dimension...  69 us
  transfers between devices with their start and end apart: 15, of which 15 were waited for; matrix products, arithmetic and copies ran while one was open for 8% of the time, Pallas kernels for 0%

commit v1 on v0

v1 whole, which is shorter than its diff:
```python
import jax
import jax.numpy as jnp
from jax import lax
from jax.sharding import PartitionSpec as P

EPS = 1e-06
BASE = 10000.0
NEG_LARGE = -1e30
LOW = jnp.bfloat16
F32 = jnp.float32
ORDER = (0, 2, 1, 3)
CORE = [(i, i ^ 1) for i in range(4)]
CROSS = [(i, i ^ 2) for i in range(4)]


def inverse_rms(values):
    return lax.rsqrt(jnp.mean(values * values, axis=-1, keepdims=True) + EPS)


def norm_backward(grad_hat, normed, inverse):
    return inverse * (grad_hat - normed * jnp.mean(grad_hat * normed, axis=-1, keepdims=True))


def dot(left, right):
    return jnp.dot(left, right, preferred_element_type=F32)


def inner_rows(left, right):
    return lax.dot_general(left, right, (((0,), (0,)), ((), ())), preferred_element_type=F32)


def inner_cols(left, right):
    return lax.dot_general(left, right, (((1,), (1,)), ((), ())), preferred_element_type=F32)


def documents(lengths_row, rows):
    first_end = lengths_row[0]
    second_end = first_end + lengths_row[1]
    doc_ids = (rows >= first_end).astype(jnp.int32) + (rows >= second_end).astype(jnp.int32)
    starts = jnp.where(rows >= second_end, second_end, jnp.where(rows >= first_end, first_end, 0))
    return (doc_ids, rows - starts)


def rotation(positions, head_dim):
    half = head_dim // 2
    freqs = BASE ** (-2.0 * jnp.arange(half, dtype=F32) / head_dim)
    angles = positions.astype(F32)[:, None] * freqs[None, :]
    return (jnp.cos(angles), jnp.sin(angles))


def rotate(values, cosine, sine):
    half = values.shape[-1] // 2
    first = values[..., :half]
    second = values[..., half:]
    return jnp.concatenate(
        [first * cosine - second * sine, second * cosine + first * sine], axis=-1
    )


def unrotate(grads, cosine, sine):
    return rotate(grads, cosine, -sine)


def local(
    tokens,
    lengths,
    norm1_gain,
    q_down,
    latent_gain,
    q_up,
    kv_proj,
    out_proj,
    norm2_gain,
    w_gate,
    w_up,
    w_down,
    cotangent,
):
    micro, rows, width = tokens.shape
    seq = lax.axis_size("seq")
    line = seq // 2
    at = lax.axis_index("seq")
    me = lax.axis_index("mp")
    place, side = at // 2, at % 2
    quarter = rows // 4
    head_dim = kv_proj.shape[1] // 2
    heads = q_up.shape[1] // head_dim
    part = q_down.shape[1]
    kv_part = kv_proj.shape[1] // 4
    scale = head_dim ** (-0.5)
    beside = [(i, i ^ 1) for i in range(seq)]

    def swap(index):
        return ((index & 1) << 1) | (index >> 1)

    def to_relative(array, axis):
        size = array.shape[axis] // 4
        return jnp.concatenate(
            [lax.dynamic_slice_in_dim(array, (me ^ k) * size, size, axis) for k in ORDER], axis
        )

    def to_natural(array, axis):
        size = array.shape[axis] // 4
        return jnp.concatenate(
            [lax.dynamic_slice_in_dim(array, swap(me ^ b) * size, size, axis) for b in range(4)],
            axis,
        )

    def sum_mp(partial):
        half = 2 * quarter
        got = lax.ppermute(partial[half:].astype(LOW), "mp", CORE)
        kept = partial[:half] + got.astype(F32)
        got = lax.ppermute(kept[quarter:].astype(LOW), "mp", CROSS)
        return kept[:quarter] + got.astype(F32)

    def gather_mp(piece, axis):
        pair = jnp.concatenate([piece, lax.ppermute(piece, "mp", CROSS)], axis)
        return jnp.concatenate([pair, lax.ppermute(pair, "mp", CORE)], axis)

    def gather_columns(piece):
        a, b, c, d = (lax.ppermute(piece, "mp", CROSS)[i * quarter : (i + 1) * quarter] for i in range(4))
        pair = jnp.concatenate([piece, jnp.concatenate([b, a, d, c], 0)], 1)
        got = lax.ppermute(pair, "mp", CORE)
        got = jnp.concatenate([got[2 * quarter :], got[: 2 * quarter]], 0)
        return jnp.concatenate([pair, got], 1)

    def halves(array):
        split = array.reshape(array.shape[0], line, 2, array.shape[1] // seq)
        mine = lax.dynamic_index_in_dim(split, side, 2, keepdims=False)
        theirs = lax.dynamic_index_in_dim(split, 1 - side, 2, keepdims=False)
        return jnp.swapaxes(mine, 0, 1), lax.ppermute(
            jnp.swapaxes(theirs, 0, 1), "seq", beside
        )

    def other(array):
        return lax.ppermute(array, "seq", beside)

    def reduce_line(block):
        up = down = None
        for step in range(1, line):
            goes_up = [(i, i + 2) for i in range(2 * step)]
            goes_down = [(seq - 1 - i, seq - 3 - i) for i in range(2 * step)]
            for_up, for_down = line - step + place, step - line + place
            if 2 * step < line + 1:
                which = jnp.where(
                    place <= step - 1, for_up, jnp.where(place >= line - step, for_down, 0)
                )
                term = block(which)
                if up is not None:
                    term = term + up.astype(F32) + down.astype(F32)
                term = term.astype(LOW)
                if step == 1 and line > 3:
                    up = lax.ppermute(term, "seq", goes_up + goes_down)
                    down = jnp.zeros_like(up)
                else:
                    up = lax.ppermute(term, "seq", goes_up)
                    down = lax.ppermute(term, "seq", goes_down)
            else:
                term_up = block(jnp.clip(for_up, 0, line - 1)) + up.astype(F32)
                term_down = block(jnp.clip(for_down, 0, line - 1)) + down.astype(F32)
                up = lax.ppermute(term_up.astype(LOW), "seq", goes_up)
                down = lax.ppermute(term_down.astype(LOW), "seq", goes_down)
        return block(place) + up.astype(F32) + down.astype(F32)

    def take(array, index):
        return lax.dynamic_index_in_dim(array, index, 0, keepdims=False)

    quarter_rows = jnp.arange(quarter, dtype=jnp.int32)
    row_ids = at * rows + jnp.concatenate([(me ^ k) * quarter + quarter_rows for k in ORDER])
    key_ids = (
        ((place - jnp.arange(line, dtype=jnp.int32)[None, None, :, None, None]) * 2
         + (side ^ jnp.arange(2, dtype=jnp.int32)[None, :, None, None, None])) * rows
        + (me ^ (jnp.arange(2, dtype=jnp.int32)[:, None, None, None, None]
                 + 2 * jnp.arange(2, dtype=jnp.int32)[None, None, None, :, None])) * quarter
        + quarter_rows[None, None, None, None, :]
    ).reshape(seq * rows)

    x_low = [to_relative(tokens[m], 0) for m in range(micro)]
    dz_low = [to_relative(cotangent[m], 0) for m in range(micro)]
    kv_cols = lax.dynamic_slice_in_dim(kv_proj, me * kv_part, kv_part, 1)
    first_weights = jnp.concatenate([q_down, kv_cols], axis=1)

    h1, kv, c_part, n1, inv1 = [], [], [], [], []
    tables, docs = [], []
    for m in range(micro):
        doc, places = documents(lengths[m], row_ids)
        docs.append(doc)
        cosine, sine = rotation(places, head_dim)
        tables.append((cosine, sine))
        x = x_low[m].astype(F32)
        inverse = inverse_rms(x)
        h1.append((x * inverse * norm1_gain).astype(LOW))
        inv1.append(inverse[:quarter])
        n1.append(x[:quarter] * inverse[:quarter])
        half = 2 * quarter
        pair = dot(h1[m][:half], kv_proj)
        packed = jnp.concatenate(
            [rotate(pair[:, :head_dim], cosine[:half], sine[:half]), pair[:, head_dim:]], axis=1
        ).astype(LOW)
        blocks = [packed] + [
            lax.ppermute(packed, "seq", [(i, i + 2 * d) for i in range(seq - 2 * d)])
            for d in range(1, line)
        ]
        near = jnp.stack(blocks, 0)
        near = jnp.stack([near, other(near)], 0)
        kv.append(
            jnp.stack([near, lax.ppermute(near, "mp", CORE)], 0).reshape(
                seq * rows, 2 * head_dim
            )
        )
        c_part.append(dot(h1[m], q_down).astype(LOW))

    dz_half, dz_half_other = halves(jnp.concatenate(dz_low, 0))
    h1_half, h1_half_other = halves(jnp.concatenate(h1, 0))

    state = []
    qn_list, o_list = [], []
    for m in range(micro):
        cosine, sine = tables[m]
        c = to_natural(gather_columns(c_part[m]), 1).astype(F32)
        inv_c = inverse_rms(c)
        chat = c * inv_c
        qn = (chat * latent_gain).astype(LOW)
        qp = dot(qn, q_up).reshape(rows, heads, head_dim)
        q = rotate(qp, cosine[:, None, :], sine[:, None, :]).astype(LOW)
        key_docs, _ = documents(lengths[m], key_ids)
        visible = (
            (key_docs[None, :] == docs[m][:, None])
            & (key_ids[None, :] <= row_ids[:, None])
            & (key_ids[None, :] >= 0)
        )
        keys, values = kv[m][:, :head_dim], kv[m][:, head_dim:]
        scores = jnp.einsum("thd,nd->thn", q, keys, preferred_element_type=F32) * scale
        scores = jnp.where(visible[:, None, :], scores, NEG_LARGE)
        top = jnp.max(scores, axis=-1, keepdims=True)
        probs = jnp.exp(scores - top)
        total = jnp.sum(probs, axis=-1, keepdims=True)
        attended = (
            jnp.einsum("thn,nd->thd", probs.astype(LOW), values, preferred_element_type=F32)
            / total
        )
        log_total = top + jnp.log(total)
        o = attended.astype(LOW).reshape(rows, heads * head_dim)
        branch = sum_mp(dot(o, out_proj))
        y = x_low[m][:quarter].astype(F32) + branch
        inv2 = inverse_rms(y)
        n2 = y * inv2
        h2 = gather_mp((n2 * norm2_gain).astype(LOW), 0)
        g = dot(h2, w_gate)
        u = dot(h2, w_up)
        sig = jax.nn.sigmoid(g)
        swish = g * sig
        hid = (swish * u).astype(LOW)
        dhid = inner_cols(dz_low[m], w_down)
        dg = (dhid * u * sig * (1.0 + g * (1.0 - sig))).astype(LOW)
        du = (dhid * swish).astype(LOW)
        qn_list.append(qn)
        o_list.append(o)
        state.append(
            dict(chat=chat, inv_c=inv_c, qn=qn, q=q, visible=visible, attended=attended,
                 log_total=log_total, o=o, y=y, n2=n2, inv2=inv2, h2=h2, hid=hid, dg=dg, du=du)
        )

    def tokens_of(name):
        own = [state[m][name] for m in range(micro)]
        return jnp.concatenate(own + [other(a) for a in own], 0)

    def halves_of(arrays):
        pairs = [halves(a) for a in arrays]
        return jnp.concatenate([p[0] for p in pairs] + [p[1] for p in pairs], 1)

    dz_all = jnp.concatenate([dz_half, dz_half_other], 1)
    h1_all = jnp.concatenate([h1_half, h1_half_other], 1)
    qn_all = halves_of(qn_list)
    o_all = tokens_of("o")
    hid_all = tokens_of("hid")
    h2_all = halves_of([st["h2"] for st in state])
    dg_all = tokens_of("dg")
    du_all = tokens_of("du")

    grad_down = reduce_line(lambda i: inner_rows(hid_all, take(dz_all, i)))
    grad_gate = reduce_line(lambda i: inner_rows(take(h2_all, i), dg_all))
    grad_up = reduce_line(lambda i: inner_rows(take(h2_all, i), du_all))

    dyl_list, gain2 = [], 0.0
    for m in range(micro):
        st = state[m]
        dh2 = sum_mp(inner_cols(st["dg"], w_gate) + inner_cols(st["du"], w_up))
        gain2 = gain2 + jnp.sum(dh2 * st["n2"], axis=0)
        dy = dz_low[m][:quarter].astype(F32) + norm_backward(
            dh2 * norm2_gain, st["n2"], st["inv2"]
        )
        st["dy"] = dy
        st["dyl"] = gather_mp(dy.astype(LOW), 0)
        dyl_list.append(st["dyl"])
    dyl_all = halves_of(dyl_list)
    grad_out = reduce_line(lambda i: inner_rows(o_all, take(dyl_all, i)))

    layer_out = []
    for m in range(micro):
        st = state[m]
        ffn = sum_mp(dot(st["hid"], w_down))
        layer_out.append(to_natural(gather_mp((st["y"] + ffn).astype(LOW), 0), 0))

    gain_c = 0.0
    for m in range(micro):
        st = state[m]
        cosine, sine = tables[m]
        keys, values = kv[m][:, :head_dim], kv[m][:, head_dim:]
        do = inner_cols(st["dyl"], out_proj).reshape(rows, heads, head_dim).astype(LOW)
        delta = jnp.sum(do.astype(F32) * st["attended"], axis=-1, keepdims=True)
        scores = jnp.einsum("thd,nd->thn", st["q"], keys, preferred_element_type=F32) * scale
        probs = jnp.exp(jnp.where(st["visible"][:, None, :], scores, NEG_LARGE) - st["log_total"])
        grad_probs = jnp.einsum("thd,nd->thn", do, values, preferred_element_type=F32)
        ds = (probs * (grad_probs - delta)).astype(LOW)
        dq = jnp.einsum("thn,nd->thd", ds, keys, preferred_element_type=F32) * scale
        dk = jnp.einsum("thn,thd->nd", ds, st["q"], preferred_element_type=F32) * scale
        dv = jnp.einsum("thn,thd->nd", probs.astype(LOW), do, preferred_element_type=F32)
        dkv = jnp.concatenate([dk, dv], 1).reshape(2, 2, line, 2, quarter, 2 * head_dim)
        mine = dkv[0] + lax.ppermute(dkv[1].astype(LOW), "mp", CORE).astype(F32)
        mine = mine[:, :, 0] + lax.ppermute(mine[:, :, 1].astype(LOW), "mp", CROSS).astype(F32)
        mine = mine[0] + other(mine[1].astype(LOW)).astype(F32)
        total = mine[0]
        for d in range(1, line):
            total = total + lax.ppermute(
                mine[d].astype(LOW), "seq", [(i + 2 * d, i) for i in range(seq - 2 * d)]
            ).astype(F32)
        dkv_low = jnp.concatenate(
            [
                unrotate(total[:, :head_dim], cosine[:quarter], sine[:quarter]),
                total[:, head_dim:],
            ],
            axis=1,
        ).astype(LOW)
        dkv_cols = lax.dynamic_slice_in_dim(gather_mp(dkv_low, 0), me * kv_part, kv_part, 1)
        dqp = (
            unrotate(dq, cosine[:, None, :], sine[:, None, :])
            .astype(LOW)
            .reshape(rows, heads * head_dim)
        )
        st["dqp"] = dqp
        dqn = sum_mp(inner_cols(dqp, q_up))
        chat, inv_c = st["chat"][:quarter], st["inv_c"][:quarter]
        gain_c = gain_c + jnp.sum(dqn * chat, axis=0)
        dc = norm_backward(dqn * latent_gain, chat, inv_c).astype(LOW)
        dc_cols = lax.dynamic_slice_in_dim(gather_mp(dc, 0), me * part, part, 1)
        st["dfirst"] = jnp.concatenate([dc_cols, dkv_cols], 1)

    dqp_all = tokens_of("dqp")
    grad_qup = reduce_line(lambda i: inner_rows(take(qn_all, i), dqp_all))
    dfirst_all = tokens_of("dfirst")
    grad_first = reduce_line(lambda i: inner_rows(take(h1_all, i), dfirst_all))
    grad_qdown = grad_first[:, :part]
    kv_cols_grad = grad_first[:, part:]
    pieces = []
    for k in ORDER:
        sent = lax.dynamic_slice_in_dim(
            kv_cols_grad, (me ^ k) * (kv_cols_grad.shape[0] // 4), kv_cols_grad.shape[0] // 4, 0
        )
        pieces.append(lax.ppermute(sent, "mp", [(i, i ^ k) for i in range(4)]) if k else sent)
    grad_kv = to_natural(jnp.concatenate(pieces, 1), 1)

    input_grads, gain1 = [], 0.0
    for m in range(micro):
        st = state[m]
        dh1 = sum_mp(inner_cols(st["dfirst"], first_weights))
        gain1 = gain1 + jnp.sum(dh1 * n1[m], axis=0)
        dx = (st["dy"] + norm_backward(dh1 * norm1_gain, n1[m], inv1[m])).astype(LOW)
        input_grads.append(to_natural(gather_mp(dx, 0), 0))

    gains = jnp.concatenate(
        [gain1.reshape(seq, -1), gain2.reshape(seq, -1), gain_c.reshape(seq, -1)], axis=1
    )
    gains = gains + lax.ppermute(gains, "mp", CORE)
    gains = gains + lax.ppermute(gains, "mp", CROSS)
    gain_sum = take(gains, at)
    for k in range(1, seq):
        gain_sum = gain_sum + lax.ppermute(
            take(gains, at ^ k), "seq", [(i, i ^ k) for i in range(seq)]
        )
    wide = width // seq
    return (
        jnp.stack(layer_out, axis=0),
        jnp.stack(input_grads, axis=0),
        gain_sum[:wide],
        grad_qdown,
        gain_sum[2 * wide :],
        grad_qup,
        grad_kv,
        grad_out,
        gain_sum[wide : 2 * wide],
        grad_gate,
        grad_up,
        grad_down,
    )


def solution(mesh):
    placed = (
        P(None, "seq", None),
        P(),
        P(),
        P(None, "mp"),
        P(),
        P(None, "mp"),
        P(),
        P("mp", None),
        P(),
        P(None, "mp"),
        P(None, "mp"),
        P("mp", None),
        P(None, "seq", None),
    )
    return jax.shard_map(
        local,
        mesh=mesh,
        in_specs=placed,
        out_specs=(
            P(None, "seq", None),
            P(None, "seq", None),
            P("seq"),
            P("seq", "mp"),
            P("seq"),
            P("seq", "mp"),
            P(("seq", "mp"), None),
            P("mp", "seq"),
            P("seq"),
            P("seq", "mp"),
            P("seq", "mp"),
            P("mp", "seq"),
        ),
        check_vma=False,
    )
```

time: 1550 us -> 906 us (0.58)
  waiting for transfers between devices: 1130 us -> 256 us
  starting transfers between devices: 1.25 us -> 195 us
  local copies, waits for them, and re-layouts: 69 us -> 143 us
  blocking collectives: 53.5 us -> 0 us
  other arithmetic: 89.3 us -> 130 us
  matrix products: 184 us -> 166 us
    reduce_scatter x9 -> x0, waiting for transfers between devices: 851 us -> none  [the longest x2 221 us: local(): lax.psum_scatter(key_grads, ('seq', 'mp'), scatter_dimension=0, tiled=True)]
    ppermute x0 -> x132, waiting for transfers between devices: none -> 256 us  [the longest x16 86.5 us: other(): return lax.ppermute(array, 'seq', beside)]
    psum x4 -> x0, waiting for transfers between devices: 219 us -> none  [the longest x1 86.1 us: local(): lax.psum(jnp.dot(hidden, w_down, preferred_element_type=jnp.float32).asty...]
    ppermute x0 -> x132, starting transfers between devices: none -> 195 us  [the longest x6 34.8 us: reduce_line(): up = lax.ppermute(term_up.astype(LOW), 'seq', goes_up)]
    all_gather x2 -> x0, waiting for transfers between devices: 55.6 us -> none  [local(): piece = lax.all_gather(packed, 'seq', axis=0, tiled=True)]
    unnamed x1 -> x0, blocking collectives: 37.3 us -> none
    dynamic_slice x0 -> x24, local copies, waits for them, and re-layouts: none -> 35.9 us  [the longest x3 14.9 us: halves(): theirs = lax.dynamic_index_in_dim(split, 1 - side, 2, keepdims=False)]
    concatenate x8 -> x43, other arithmetic: 9.08 us -> 42.3 us  [the longest x12 12.2 us: gather_mp(): return jnp.concatenate([pair, lax.ppermute(pair, 'mp', CORE)], axis)]
  transfers between devices with their start and end apart: 15 -> 132, of which waited for: 15 -> 43; matrix products, arithmetic and copies ran while one was open for 8% -> 45% of each run, Pallas kernels for 0% -> 0%
where the time goes in v1:
time: 906 us; the launch traced here: 899 us
  waiting for transfers between devices  256 us (28%)
  starting transfers between devices  195 us (22%)
  matrix products  166 us (18%)
  local copies, waits for them, and re-layouts  143 us (16%)
  other arithmetic  130 us (14%)
    ppermute x16, waiting for transfers between devices, other(): return lax.ppermute(array, 'seq', beside)  86.5 us
    dot_general x30, matrix products, inner_rows(): lax.dot_general(left, right, (((0,), (0,)), ((), ())), preferred_element_...  63.5 us
    unnamed x529, local copies, waits for them, and re-layouts  37.5 us
    ppermute x6, starting transfers between devices, reduce_line(): up = lax.ppermute(term_up.astype(LOW), 'seq', goes_up)  34.8 us
    dot_general x14, matrix products, dot(): return jnp.dot(left, right, preferred_element_type=F32)  34.3 us
    ppermute x10, waiting for transfers between devices, sum_mp(): got = lax.ppermute(kept[quarter:].astype(LOW), 'mp', CROSS)  29.6 us
    ppermute x6, waiting for transfers between devices, reduce_line(): up = lax.ppermute(term, 'seq', goes_up + goes_down)  29.5 us
    dot_general x12, matrix products, inner_cols(): lax.dot_general(left, right, (((1,), (1,)), ((), ())), preferred_element_...  26.5 us
  transfers between devices with their start and end apart: 132, of which 43 were waited for; matrix products, arithmetic and copies ran while one was open for 45% of the time, Pallas kernels for 0%

profile of v1, /device:TPU:0, one launch (start us, length us, event | category | flops | bytes accessed | tf_op | source)
XLA Modules:
  0.0 898.8 jit_solution(9307884954137005312)
XLA Ops:
  22.7 6.6 collective-permute-start.3
  89.3 8.7 constant_dynamic-slice_fusion
  98.1 15.8 %multiply_convert_fusion.3 = (bf16[256,4,2,256]{3,2,1,0:T(2,128)(2,1)S(1)}, bf16[256,4,2,256]{3,2,1,0:T(2,128)(2,1)S(1)}) fusion(f32[256]{0:T(256)S(1)} %copy-done.186, bf16[64,4,2,256]{3,2,1,0:T(2,128)(2,1)S(1)} %copy-done.130, bf16[64,4,2,256]{3,2,1,0:T(2,128)(2,1)S(1)} %copy-done.129, bf16[64,4,2,256]{3,2,1,0:T(2,128)(2,1)S(1)} %copy-done.128, ...), kind=kLoop, calls=%fused_computation.112 | loop fusion | flops 7340032 | bytes 4204544 | tf_op jit(solution)/shard_map/convert_element_type | solution.py:192
  114.0 7.0 dynamic-slice_maximum_fusion
  174.8 12.2 %collective-permute-done.5 = bf16[4,128,512]{2,1,0:T(8,128)(2,1)} collective-permute-done((bf16[4,128,512]{2,1,0:T(8,128)(2,1)}, bf16[4,128,512]{2,1,0:T(8,128)(2,1)}, u32[]{:S(2)}, u32[]{:S(2)}) %collective-permute-start.5) | collective-permute-done | bytes 524320 | tf_op jit(solution)/shard_map/ppermute | solution.py:136
  226.7 4.3 collective-permute-done.8
  233.6 7.0 collective-permute-done.9
  261.7 6.3 collective-permute-done.31
  268.3 4.4 collective-permute-done.12
  301.2 6.2 fusion.29
  307.5 6.0 multiply_convert_fusion.1
  336.2 4.7 fusion.273
  340.9 6.3 multiply_convert_fusion.6
  352.9 4.6 fusion.302
  374.0 5.8 collective-permute-done.35
  386.5 24.4 %collective-permute-done.109 = bf16[4,256,256]{2,1,0:T(8,128)(2,1)S(1)} collective-permute-done((bf16[4,256,256]{2,1,0:T(8,128)(2,1)S(1)}, bf16[4,256,256]{2,1,0:T(8,128)(2,1)S(1)}, u32[]{:S(2)}, u32[]{:S(2)}) %collective-permute-start.109) | collective-permute-done | bytes 524320 | tf_op jit(solution)/shard_map/ppermute | solution.py:131
  414.3 3.9 convolution_convert_fusion.1
  419.8 6.6 collective-permute-done.124
  427.9 13.9 %collective-permute-done.125 = bf16[256,1408]{1,0:T(8,128)(2,1)S(1)} collective-permute-done((bf16[256,1408]{1,0:T(8,128)(2,1)S(1)}, bf16[256,1408]{1,0:T(8,128)(2,1)S(1)}, u32[]{:S(2)}, u32[]{:S(2)}) %collective-permute-start.125) | collective-permute-done | bytes 720928 | tf_op jit(solution)/shard_map/ppermute | solution.py:136
  444.9 12.4 %collective-permute-done.110 = bf16[256,1408]{1,0:T(8,128)(2,1)S(1)} collective-permute-done((bf16[256,1408]{1,0:T(8,128)(2,1)S(1)}, bf16[256,1408]{1,0:T(8,128)(2,1)S(1)}, u32[]{:S(2)}, u32[]{:S(2)}) %collective-permute-start.110) | collective-permute-done | bytes 720928 | tf_op jit(solution)/shard_map/ppermute | solution.py:136
  458.8 13.9 %collective-permute-done.111 = bf16[256,1408]{1,0:T(8,128)(2,1)S(1)} collective-permute-done((bf16[256,1408]{1,0:T(8,128)(2,1)S(1)}, bf16[256,1408]{1,0:T(8,128)(2,1)S(1)}, u32[]{:S(2)}, u32[]{:S(2)}) %collective-permute-start.111) | collective-permute-done | bytes 720928 | tf_op jit(solution)/shard_map/ppermute | solution.py:136
  476.1 4.2 collective-permute-done.51
  502.1 11.7 %collective-permute-done.112 = bf16[256,1408]{1,0:T(8,128)(2,1)S(1)} collective-permute-done((bf16[256,1408]{1,0:T(8,128)(2,1)S(1)}, bf16[256,1408]{1,0:T(8,128)(2,1)S(1)}, u32[]{:S(2)}, u32[]{:S(2)}) %collective-permute-start.112) | collective-permute-done | bytes 720928 | tf_op jit(solution)/shard_map/ppermute | solution.py:153
  517.2 9.8 %collective-permute-done.127 = bf16[1408,256]{1,0:T(8,128)(2,1)S(1)} collective-permute-done((bf16[1408,256]{1,0:T(8,128)(2,1)S(1)}, bf16[1408,256]{1,0:T(8,128)(2,1)S(1)}, u32[]{:S(2)}, u32[]{:S(2)}) %collective-permute-start.127) | collective-permute-done | bytes 720928 | tf_op jit(solution)/shard_map/ppermute | solution.py:153
  542.5 6.8 multiply_convert_fusion
  557.7 6.0 fusion.32
  604.5 4.4 collective-permute-done.36
  627.1 8.1 collective-permute-done.89
  638.4 8.0 collective-permute-done.90
  648.0 4.2 collective-permute-start.113
  657.8 4.8 collective-permute-done.113
  663.6 5.0 collective-permute-start.103
  681.5 5.1 collective-permute-done.91
  688.7 5.0 collective-permute-start.92
  694.2 12.3 %collective-permute-done.92 = bf16[128,1024]{1,0:T(8,128)(2,1)S(1)} collective-permute-done((bf16[128,1024]{1,0:T(8,128)(2,1)S(1)}, bf16[128,1024]{1,0:T(8,128)(2,1)S(1)}, u32[]{:S(2)}, u32[]{:S(2)}) %collective-permute-start.92) | collective-permute-done | bytes 262176 | tf_op jit(solution)/shard_map/ppermute | solution.py:156
  708.0 12.0 %collective-permute-start.121 = (bf16[256,1408]{1,0:T(8,128)(2,1)S(1)}, bf16[256,1408]{1,0:T(8,128)(2,1)S(1)}, u32[]{:S(2)}, u32[]{:S(2)}) collective-permute-start(bf16[256,1408]{1,0:T(8,128)(2,1)S(1)} %fusion.40), channel_id=1, source_target_pairs={{0,8},{4,12},{8,16},{12,20},{16,24},{20,28},{1,9},{5,13},{9,17},{1... | collective-permute-start | bytes 2162696 | tf_op jit(solution)/shard_map/ppermute | solution.py:161
  730.8 4.6 collective-permute-start.114
  735.5 4.8 collective-permute-done.59
  747.6 7.0 collective-permute-done.60
  757.3 4.4 collective-permute-done.116
  772.6 10.9 %collective-permute-done.93 = bf16[128,1024]{1,0:T(8,128)(2,1)S(1)} collective-permute-done((bf16[128,1024]{1,0:T(8,128)(2,1)S(1)}, bf16[128,1024]{1,0:T(8,128)(2,1)S(1)}, u32[]{:S(2)}, u32[]{:S(2)}) %collective-permute-start.93) | collective-permute-done | bytes 262176 | tf_op jit(solution)/shard_map/ppermute | solution.py:161
  794.5 5.1 collective-permute-start.105
  820.6 4.4 collective-permute-start.83
  830.7 9.9 %collective-permute-start.84 = (bf16[256,384]{1,0:T(8,128)(2,1)S(1)}, bf16[256,384]{1,0:T(8,128)(2,1)S(1)}, u32[]{:S(2)}, u32[]{:S(2)}) collective-permute-start(bf16[256,384]{1,0:T(8,128)(2,1)S(1)} %fusion.63), channel_id=1, source_target_pairs={{0,8},{4,12},{8,16},{12,20},{16,24},{20,28},{1,9},{5,13},{9,17},{1... | collective-permute-start | bytes 589832 | tf_op jit(solution)/shard_map/ppermute | solution.py:161
  844.5 6.0 collective-permute-done.86
  862.6 9.5 %collective-permute-done.71 = f32[8,640]{1,0:T(8,128)S(1)} collective-permute-done((f32[8,640]{1,0:T(8,128)S(1)}, f32[8,640]{1,0:T(8,128)S(1)}, u32[]{:S(2)}, u32[]{:S(2)}) %collective-permute-start.71) | collective-permute-done | bytes 20512 | tf_op jit(solution)/shard_map/ppermute | solution.py:375
  882.7 5.7 collective-permute-start.78
  888.9 5.8 collective-permute-done.78
  (1081 shorter events, 524.2 us)
Async XLA Ops:
  22.7 123.9 %collective-permute-start.3 = (bf16[128,512]{1,0:T(8,128)(2,1)}, bf16[128,512]{1,0:T(8,128)(2,1)}, u32[]{:S(2)}, u32[]{:S(2)}) collective-permute-start(bf16[128,512]{1,0:T(8,128)(2,1)} %pad_maximum_fusion.52), channel_id=1, source_target_pairs={{0,16},{4,20},{8,24},{12,28},{1,17},{5,21},{9,25},{13,29},{2,18},{... | collective-permute-start | bytes 393224 | tf_op jit(solution)/shard_map/ppermute | solution.py:201
  29.3 120.0 %collective-permute-start.4 = (bf16[128,512]{1,0:T(8,128)(2,1)}, bf16[128,512]{1,0:T(8,128)(2,1)}, u32[]{:S(2)}, u32[]{:S(2)}) collective-permute-start(bf16[128,512]{1,0:T(8,128)(2,1)} %pad_maximum_fusion.52), channel_id=1, source_target_pairs={{0,24},{4,28},{1,25},{5,29},{2,26},{6,30},{3,27},{7,31}} | collective-permute-start | bytes 393224 | tf_op jit(solution)/shard_map/ppermute | solution.py:201
  31.6 119.3 %collective-permute-start.2 = (bf16[128,512]{1,0:T(8,128)(2,1)}, bf16[128,512]{1,0:T(8,128)(2,1)}, u32[]{:S(2)}, u32[]{:S(2)}) collective-permute-start(bf16[128,512]{1,0:T(8,128)(2,1)} %pad_maximum_fusion.52), channel_id=1, source_target_pairs={{0,8},{4,12},{8,16},{12,20},{16,24},{20,28},{1,9},{5,13},{9,17},{1... | collective-permute-start | bytes 393224 | tf_op jit(solution)/shard_map/ppermute | solution.py:201
  37.3 103.5 %collective-permute-start = (bf16[256,256]{0,1:T(8,128)(2,1)}, bf16[256,256]{0,1:T(8,128)(2,1)}, u32[]{:S(2)}, u32[]{:S(2)}) collective-permute-start(bf16[256,256]{0,1:T(8,128)(2,1)} %convolution_convert_fusion.9), channel_id=1, source_target_pairs={{0,2},{1,3},{2,0},{3,1},{4,6},{5,7},{6,4},{7,5},{8,10},{9,11},{10,... | collective-permute-start | bytes 393224 | tf_op jit(solution)/shard_map/ppermute | solution.py:121
  40.0 103.2 %collective-permute-start.15 = (bf16[256,256]{0,1:T(8,128)(2,1)}, bf16[256,256]{0,1:T(8,128)(2,1)}, u32[]{:S(2)}, u32[]{:S(2)}) collective-permute-start(bf16[256,256]{0,1:T(8,128)(2,1)} %convolution_convert_fusion.8), channel_id=1, source_target_pairs={{0,2},{1,3},{2,0},{3,1},{4,6},{5,7},{6,4},{7,5},{8,10},{9,11},{10,... | collective-permute-start | bytes 393224 | tf_op jit(solution)/shard_map/ppermute | solution.py:121
  149.3 268.9 %collective-permute-start.126 = (bf16[4,512,256]{2,1,0:T(8,128)(2,1)}, bf16[4,512,256]{2,1,0:T(8,128)(2,1)}, u32[]{:S(2)}, u32[]{:S(2)}) collective-permute-start(bf16[4,512,256]{2,1,0:T(8,128)(2,1)} %bitcast.375), channel_id=1, source_target_pairs={{0,4},{4,0},{8,12},{12,8},{16,20},{20,16},{24,28},{28,24},{1,5},{5... | collective-permute-start | bytes 3145736 | tf_op jit(solution)/shard_map/ppermute | solution.py:131
  152.8 34.2 %collective-permute-start.5 = (bf16[4,128,512]{2,1,0:T(8,128)(2,1)}, bf16[4,128,512]{2,1,0:T(8,128)(2,1)}, u32[]{:S(2)}, u32[]{:S(2)}) collective-permute-start(bf16[4,128,512]{2,1,0:T(8,128)(2,1)} %pad_maximum_fusion.30), channel_id=1, source_target_pairs={{0,4},{4,0},{8,12},{12,8},{16,20},{20,16},{24,28},{28,24},{1,5},{5... | collective-permute-start | bytes 1572872 | tf_op jit(solution)/shard_map/ppermute | solution.py:136
  154.4 43.9 %collective-permute-start.20 = (bf16[4,128,512]{2,1,0:T(8,128)(2,1)}, bf16[4,128,512]{2,1,0:T(8,128)(2,1)}, u32[]{:S(2)}, u32[]{:S(2)}) collective-permute-start(bf16[4,128,512]{2,1,0:T(8,128)(2,1)} %pad_maximum_fusion.35), channel_id=1, source_target_pairs={{0,4},{4,0},{8,12},{12,8},{16,20},{20,16},{24,28},{28,24},{1,5},{5... | collective-permute-start | bytes 1572872 | tf_op jit(solution)/shard_map/ppermute | solution.py:136
  172.0 68.7 %collective-permute-start.87 = (bf16[4,256,128]{1,2,0:T(8,128)(2,1)}, bf16[4,256,128]{1,2,0:T(8,128)(2,1)}, u32[]{:S(2)}, u32[]{:S(2)}) collective-permute-start(bf16[4,256,128]{1,2,0:T(8,128)(2,1)} %get-tuple-element.117), channel_id=1, source_target_pairs={{0,4},{4,0},{8,12},{12,8},{16,20},{20,16},{24,28},{28,24},{1,5},{5... | collective-permute-start | bytes 786440 | tf_op jit(solution)/shard_map/ppermute | solution.py:131
  190.4 50.4 %collective-permute-start.88 = (bf16[4,256,128]{1,2,0:T(8,128)(2,1)}, bf16[4,256,128]{1,2,0:T(8,128)(2,1)}, u32[]{:S(2)}, u32[]{:S(2)}) collective-permute-start(bf16[4,256,128]{1,2,0:T(8,128)(2,1)} %get-tuple-element.119), channel_id=1, source_target_pairs={{0,4},{4,0},{8,12},{12,8},{16,20},{20,16},{24,28},{28,24},{1,5},{5... | collective-permute-start | bytes 786440 | tf_op jit(solution)/shard_map/ppermute | solution.py:131
  275.5 108.8 %collective-permute-start.117 = (bf16[256,1408]{1,0:T(8,128)(2,1)}, bf16[256,1408]{1,0:T(8,128)(2,1)}, u32[]{:S(2)}, u32[]{:S(2)}) collective-permute-start(bf16[256,1408]{1,0:T(8,128)(2,1)} %get-tuple-element.46), channel_id=1, source_target_pairs={{0,4},{4,0},{8,12},{12,8},{16,20},{20,16},{24,28},{28,24},{1,5},{5... | collective-permute-start | bytes 2162696 | tf_op jit(solution)/shard_map/ppermute | solution.py:136
  289.4 91.3 %collective-permute-start.108 = (bf16[4,256,256]{2,1,0:T(8,128)(2,1)}, bf16[4,256,256]{2,1,0:T(8,128)(2,1)}, u32[]{:S(2)}, u32[]{:S(2)}) collective-permute-start(bf16[4,256,256]{2,1,0:T(8,128)(2,1)} %bitcast.380), channel_id=1, source_target_pairs={{0,4},{4,0},{8,12},{12,8},{16,20},{20,16},{24,28},{28,24},{1,5},{5... | collective-permute-start | bytes 1572872 | tf_op jit(solution)/shard_map/ppermute | solution.py:131
  292.8 26.8 %collective-permute-start.25 = (bf16[128,2048]{1,0:T(8,128)(2,1)}, bf16[128,2048]{1,0:T(8,128)(2,1)}, u32[]{:S(2)}, u32[]{:S(2)}) collective-permute-start(bf16[128,2048]{1,0:T(8,128)(2,1)} %pad_maximum_fusion.36), channel_id=1, source_target_pairs={{0,1},{1,0},{2,3},{3,2},{4,5},{5,4},{6,7},{7,6},{8,9},{9,8},{10,11... | collective-permute-start | bytes 1572872 | tf_op jit(solution)/shard_map/ppermute | solution.py:118
  293.7 63.8 %collective-permute-start.14 = (bf16[128,2048]{1,0:T(8,128)(2,1)}, bf16[128,2048]{1,0:T(8,128)(2,1)}, u32[]{:S(2)}, u32[]{:S(2)}) collective-permute-start(bf16[128,2048]{1,0:T(8,128)(2,1)} %pad_maximum_fusion.32), channel_id=1, source_target_pairs={{0,1},{1,0},{2,3},{3,2},{4,5},{5,4},{6,7},{7,6},{8,9},{9,8},{10,11... | collective-permute-start | bytes 1572872 | tf_op jit(solution)/shard_map/ppermute | solution.py:118
  350.1 32.2 %collective-permute-start.26 = (bf16[128,2048]{1,0:T(8,128)(2,1)}, bf16[128,2048]{1,0:T(8,128)(2,1)}, u32[]{:S(2)}, u32[]{:S(2)}) collective-permute-start(bf16[128,2048]{1,0:T(8,128)(2,1)} %slice.930), channel_id=1, source_target_pairs={{0,1},{1,0},{2,3},{3,2},{4,5},{5,4},{6,7},{7,6},{8,9},{9,8},{10,11... | collective-permute-start | bytes 1572872 | tf_op jit(solution)/shard_map/ppermute | solution.py:111
  380.8 31.7 %collective-permute-start.118 = (bf16[256,1408]{1,0:T(8,128)(2,1)S(1)}, bf16[256,1408]{1,0:T(8,128)(2,1)S(1)}, u32[]{:S(2)}, u32[]{:S(2)}) collective-permute-start(bf16[256,1408]{1,0:T(8,128)(2,1)S(1)} %copy-done.213), channel_id=1, source_target_pairs={{0,4},{4,0},{8,12},{12,8},{16,20},{20,16},{24,28},{28,24},{1,5},{5... | collective-permute-start | bytes 2162696 | tf_op jit(solution)/shard_map/ppermute | solution.py:136
  382.3 28.6 %collective-permute-start.109 = (bf16[4,256,256]{2,1,0:T(8,128)(2,1)S(1)}, bf16[4,256,256]{2,1,0:T(8,128)(2,1)S(1)}, u32[]{:S(2)}, u32[]{:S(2)}) collective-permute-start(bf16[4,256,256]{2,1,0:T(8,128)(2,1)S(1)} %bitcast.458), channel_id=1, source_target_pairs={{0,4},{4,0},{8,12},{12,8},{16,20},{20,16},{24,28},{28,24},{1,5},{5... | collective-permute-start | bytes 1572872 | tf_op jit(solution)/shard_map/ppermute | solution.py:131
  384.3 42.1 %collective-permute-start.124 = (bf16[256,1408]{1,0:T(8,128)(2,1)S(1)}, bf16[256,1408]{1,0:T(8,128)(2,1)S(1)}, u32[]{:S(2)}, u32[]{:S(2)}) collective-permute-start(bf16[256,1408]{1,0:T(8,128)(2,1)S(1)} %copy-done.205), channel_id=1, source_target_pairs={{0,4},{4,0},{8,12},{12,8},{16,20},{20,16},{24,28},{28,24},{1,5},{5... | collective-permute-start | bytes 2162696 | tf_op jit(solution)/shard_map/ppermute | solution.py:136
  385.7 56.1 %collective-permute-start.125 = (bf16[256,1408]{1,0:T(8,128)(2,1)S(1)}, bf16[256,1408]{1,0:T(8,128)(2,1)S(1)}, u32[]{:S(2)}, u32[]{:S(2)}) collective-permute-start(bf16[256,1408]{1,0:T(8,128)(2,1)S(1)} %copy-done.217), channel_id=1, source_target_pairs={{0,4},{4,0},{8,12},{12,8},{16,20},{20,16},{24,28},{28,24},{1,5},{5... | collective-permute-start | bytes 2162696 | tf_op jit(solution)/shard_map/ppermute | solution.py:136
  410.9 46.3 %collective-permute-start.110 = (bf16[256,1408]{1,0:T(8,128)(2,1)S(1)}, bf16[256,1408]{1,0:T(8,128)(2,1)S(1)}, u32[]{:S(2)}, u32[]{:S(2)}) collective-permute-start(bf16[256,1408]{1,0:T(8,128)(2,1)S(1)} %copy-done.201), channel_id=1, source_target_pairs={{0,4},{4,0},{8,12},{12,8},{16,20},{20,16},{24,28},{28,24},{1,5},{5... | collective-permute-start | bytes 2162696 | tf_op jit(solution)/shard_map/ppermute | solution.py:136
  412.5 60.2 %collective-permute-start.111 = (bf16[256,1408]{1,0:T(8,128)(2,1)S(1)}, bf16[256,1408]{1,0:T(8,128)(2,1)S(1)}, u32[]{:S(2)}, u32[]{:S(2)}) collective-permute-start(bf16[256,1408]{1,0:T(8,128)(2,1)S(1)} %copy-done.209), channel_id=1, source_target_pairs={{0,4},{4,0},{8,12},{12,8},{16,20},{20,16},{24,28},{28,24},{1,5},{5... | collective-permute-start | bytes 2162696 | tf_op jit(solution)/shard_map/ppermute | solution.py:136
  418.2 203.0 %collective-permute-start.99 = (bf16[256,1024]{0,1:T(8,128)(2,1)}, bf16[256,1024]{0,1:T(8,128)(2,1)}, u32[]{:S(2)}, u32[]{:S(2)}) collective-permute-start(bf16[256,1024]{0,1:T(8,128)(2,1)} %bitcast.19), channel_id=1, source_target_pairs={{0,4},{4,0},{8,12},{12,8},{16,20},{20,16},{24,28},{28,24},{1,5},{5... | collective-permute-start | bytes 1572872 | tf_op jit(solution)/shard_map/ppermute | solution.py:136
  426.4 186.7 %collective-permute-start.101 = (bf16[4,256,256]{2,1,0:T(8,128)(2,1)}, bf16[4,256,256]{2,1,0:T(8,128)(2,1)}, u32[]{:S(2)}, u32[]{:S(2)}) collective-permute-start(bf16[4,256,256]{2,1,0:T(8,128)(2,1)} %bitcast.384), channel_id=1, source_target_pairs={{0,4},{4,0},{8,12},{12,8},{16,20},{20,16},{24,28},{28,24},{1,5},{5... | collective-permute-start | bytes 1572872 | tf_op jit(solution)/shard_map/ppermute | solution.py:131
  441.8 43.5 %collective-permute-start.38 = (bf16[2,4,2,64,512]{4,3,2,1,0:T(8,128)(2,1)}, bf16[2,4,2,64,512]{4,3,2,1,0:T(8,128)(2,1)}, u32[]{:S(2)}, u32[]{:S(2)}) collective-permute-start(bf16[2,4,2,64,512]{4,3,2,1,0:T(8,128)(2,1)} %bitcast.54), channel_id=1, source_target_pairs={{0,1},{1,0},{2,3},{3,2},{4,5},{5,4},{6,7},{7,6},{8,9},{9,8},{10,11... | collective-permute-start | bytes 3145736 | tf_op jit(solution)/shard_map/ppermute | solution.py:320
  457.3 25.4 %collective-permute-start.27 = (bf16[64,2048]{1,0:T(8,128)(2,1)S(1)}, bf16[64,2048]{1,0:T(8,128)(2,1)S(1)}, u32[]{:S(2)}, u32[]{:S(2)}) collective-permute-start(bf16[64,2048]{1,0:T(8,128)(2,1)S(1)} %slice.942), channel_id=1, source_target_pairs={{0,2},{1,3},{2,0},{3,1},{4,6},{5,7},{6,4},{7,5},{8,10},{9,11},{10,... | collective-permute-start | bytes 786440 | tf_op jit(solution)/shard_map/ppermute | solution.py:113
  496.1 30.9 %collective-permute-start.127 = (bf16[1408,256]{1,0:T(8,128)(2,1)S(1)}, bf16[1408,256]{1,0:T(8,128)(2,1)S(1)}, u32[]{:S(2)}, u32[]{:S(2)}) collective-permute-start(bf16[1408,256]{1,0:T(8,128)(2,1)S(1)} %copy-done.238), channel_id=1, source_target_pairs={{0,8},{4,12},{28,20},{24,16},{1,9},{5,13},{29,21},{25,17},{2,10},{... | collective-permute-start | bytes 2162696 | tf_op jit(solution)/shard_map/ppermute | solution.py:153
  498.5 31.4 %collective-permute-start.53 = (bf16[128,2048]{1,0:T(8,128)(2,1)S(1)}, bf16[128,2048]{1,0:T(8,128)(2,1)S(1)}, u32[]{:S(2)}, u32[]{:S(2)}) collective-permute-start(bf16[128,2048]{1,0:T(8,128)(2,1)S(1)} %pad_maximum_fusion.41), channel_id=1, source_target_pairs={{0,1},{1,0},{2,3},{3,2},{4,5},{5,4},{6,7},{7,6},{8,9},{9,8},{10,11... | collective-permute-start | bytes 1572872 | tf_op jit(solution)/shard_map/ppermute | solution.py:118
  513.8 50.0 %collective-permute-start.39 = (bf16[2,4,64,512]{3,2,1,0:T(8,128)(2,1)}, bf16[2,4,64,512]{3,2,1,0:T(8,128)(2,1)}, u32[]{:S(2)}, u32[]{:S(2)}) collective-permute-start(bf16[2,4,64,512]{3,2,1,0:T(8,128)(2,1)} %fusion.98), channel_id=1, source_target_pairs={{0,2},{1,3},{2,0},{3,1},{4,6},{5,7},{6,4},{7,5},{8,10},{9,11},{10,... | collective-permute-start | bytes 1572872 | tf_op jit(solution)/shard_map/ppermute | solution.py:321
  527.0 51.4 %collective-permute-start.29 = (bf16[128,2048]{1,0:T(8,128)(2,1)}, bf16[128,2048]{1,0:T(8,128)(2,1)}, u32[]{:S(2)}, u32[]{:S(2)}) collective-permute-start(bf16[128,2048]{1,0:T(8,128)(2,1)} %pad_maximum_fusion.37), channel_id=1, source_target_pairs={{0,1},{1,0},{2,3},{3,2},{4,5},{5,4},{6,7},{7,6},{8,9},{9,8},{10,11... | collective-permute-start | bytes 1572872 | tf_op jit(solution)/shard_map/ppermute | solution.py:118
  557.2 28.9 %collective-permute-start.54 = (bf16[128,1024]{0,1:T(8,128)(2,1)}, bf16[128,1024]{0,1:T(8,128)(2,1)}, u32[]{:S(2)}, u32[]{:S(2)}) collective-permute-start(bf16[128,1024]{0,1:T(8,128)(2,1)} %slice.936), channel_id=1, source_target_pairs={{0,1},{1,0},{2,3},{3,2},{4,5},{5,4},{6,7},{7,6},{8,9},{9,8},{10,11... | collective-permute-start | bytes 786440 | tf_op jit(solution)/shard_map/ppermute | solution.py:111
  590.1 25.0 %collective-permute-start.102 = (bf16[4,256,256]{2,1,0:T(8,128)(2,1)}, bf16[4,256,256]{2,1,0:T(8,128)(2,1)}, u32[]{:S(2)}, u32[]{:S(2)}) collective-permute-start(bf16[4,256,256]{2,1,0:T(8,128)(2,1)} %bitcast.383), channel_id=1, source_target_pairs={{0,4},{4,0},{8,12},{12,8},{16,20},{20,16},{24,28},{28,24},{1,5},{5... | collective-permute-start | bytes 1572872 | tf_op jit(solution)/shard_map/ppermute | solution.py:131
  613.1 22.1 %collective-permute-start.89 = (bf16[256,1024]{0,1:T(8,128)(2,1)}, bf16[256,1024]{0,1:T(8,128)(2,1)S(1)}, u32[]{:S(2)}, u32[]{:S(2)}) collective-permute-start(bf16[256,1024]{0,1:T(8,128)(2,1)} %bitcast.460), channel_id=1, source_target_pairs={{0,4},{4,0},{8,12},{12,8},{16,20},{20,16},{24,28},{28,24},{1,5},{5... | collective-permute-start | bytes 1572872 | tf_op jit(solution)/shard_map/ppermute | solution.py:136
  615.1 32.9 %collective-permute-start.128 = (bf16[1408,256]{1,0:T(8,128)(2,1)}, bf16[1408,256]{1,0:T(8,128)(2,1)S(1)}, u32[]{:S(2)}, u32[]{:S(2)}) collective-permute-start(bf16[1408,256]{1,0:T(8,128)(2,1)} %fusion.44), channel_id=1, source_target_pairs={{0,8},{4,12},{8,16},{12,20},{1,9},{5,13},{9,17},{13,21},{2,10},{6,... | collective-permute-start | bytes 2162696 | tf_op jit(solution)/shard_map/ppermute | solution.py:156
  618.4 28.0 %collective-permute-start.90 = (bf16[256,1024]{0,1:T(8,128)(2,1)}, bf16[256,1024]{0,1:T(8,128)(2,1)S(1)}, u32[]{:S(2)}, u32[]{:S(2)}) collective-permute-start(bf16[256,1024]{0,1:T(8,128)(2,1)} %bitcast.467), channel_id=1, source_target_pairs={{0,4},{4,0},{8,12},{12,8},{16,20},{20,16},{24,28},{28,24},{1,5},{5... | collective-permute-start | bytes 1572872 | tf_op jit(solution)/shard_map/ppermute | solution.py:136
  621.3 185.9 %collective-permute-start.79 = (bf16[4,512,256]{2,1,0:T(8,128)(2,1)}, bf16[4,512,256]{2,1,0:T(8,128)(2,1)}, u32[]{:S(2)}, u32[]{:S(2)}) collective-permute-start(bf16[4,512,256]{2,1,0:T(8,128)(2,1)} %bitcast.377), channel_id=1, source_target_pairs={{0,4},{4,0},{8,12},{12,8},{16,20},{20,16},{24,28},{28,24},{1,5},{5... | collective-permute-start | bytes 3145736 | tf_op jit(solution)/shard_map/ppermute | solution.py:131
  624.0 47.0 %collective-permute-start.130 = (bf16[1408,256]{1,0:T(8,128)(2,1)S(1)}, bf16[1408,256]{1,0:T(8,128)(2,1)S(1)}, u32[]{:S(2)}, u32[]{:S(2)}) collective-permute-start(bf16[1408,256]{1,0:T(8,128)(2,1)S(1)} %copy-done.237), channel_id=1, source_target_pairs={{28,20},{24,16},{20,12},{16,8},{29,21},{25,17},{21,13},{17,9},{30,... | collective-permute-start | bytes 2162696 | tf_op jit(solution)/shard_map/ppermute | solution.py:157
  662.6 26.1 %collective-permute-start.58 = (bf16[2,4,2,64,512]{4,3,2,1,0:T(8,128)(2,1)S(1)}, bf16[2,4,2,64,512]{4,3,2,1,0:T(8,128)(2,1)S(1)}, u32[]{:S(2)}, u32[]{:S(2)}) collective-permute-start(bf16[2,4,2,64,512]{4,3,2,1,0:T(8,128)(2,1)S(1)} %bitcast.455), channel_id=1, source_target_pairs={{0,1},{1,0},{2,3},{3,2},{4,5},{5,4},{6,7},{7,6},{8,9},{9,8},{10,11... | collective-permute-start | bytes 3145736 | tf_op jit(solution)/shard_map/ppermute | solution.py:320
  663.6 57.2 %collective-permute-start.103 = (bf16[1024,256]{1,0:T(8,128)(2,1)S(1)}, bf16[1024,256]{1,0:T(8,128)(2,1)S(1)}, u32[]{:S(2)}, u32[]{:S(2)}) collective-permute-start(bf16[1024,256]{1,0:T(8,128)(2,1)S(1)} %convolution_convert_fusion.3), channel_id=1, source_target_pairs={{0,8},{4,12},{28,20},{24,16},{1,9},{5,13},{29,21},{25,17},{2,10},{... | collective-permute-start | bytes 1572872 | tf_op jit(solution)/shard_map/ppermute | solution.py:153
  678.5 46.8 %collective-permute-start.129 = (bf16[1408,256]{1,0:T(8,128)(2,1)S(1)}, bf16[1408,256]{1,0:T(8,128)(2,1)S(1)}, u32[]{:S(2)}, u32[]{:S(2)}) collective-permute-start(bf16[1408,256]{1,0:T(8,128)(2,1)S(1)} %fusion.43), channel_id=1, source_target_pairs={{0,8},{4,12},{8,16},{12,20},{16,24},{20,28},{1,9},{5,13},{9,17},{1... | collective-permute-start | bytes 2162696 | tf_op jit(solution)/shard_map/ppermute | solution.py:161
  686.6 38.7 %collective-permute-start.131 = (bf16[1408,256]{1,0:T(8,128)(2,1)S(1)}, bf16[1408,256]{1,0:T(8,128)(2,1)S(1)}, u32[]{:S(2)}, u32[]{:S(2)}) collective-permute-start(bf16[1408,256]{1,0:T(8,128)(2,1)S(1)} %fusion.45), channel_id=1, source_target_pairs={{28,20},{24,16},{20,12},{16,8},{12,4},{8,0},{29,21},{25,17},{21,13... | collective-permute-start | bytes 2162696 | tf_op jit(solution)/shard_map/ppermute | solution.py:162
  708.0 34.0 %collective-permute-start.121 = (bf16[256,1408]{1,0:T(8,128)(2,1)S(1)}, bf16[256,1408]{1,0:T(8,128)(2,1)S(1)}, u32[]{:S(2)}, u32[]{:S(2)}) collective-permute-start(bf16[256,1408]{1,0:T(8,128)(2,1)S(1)} %fusion.40), channel_id=1, source_target_pairs={{0,8},{4,12},{8,16},{12,20},{16,24},{20,28},{1,9},{5,13},{9,17},{1... | collective-permute-start | bytes 2162696 | tf_op jit(solution)/shard_map/ppermute | solution.py:161
  730.8 25.2 %collective-permute-start.114 = (bf16[256,1408]{1,0:T(8,128)(2,1)S(1)}, bf16[256,1408]{1,0:T(8,128)(2,1)S(1)}, u32[]{:S(2)}, u32[]{:S(2)}) collective-permute-start(bf16[256,1408]{1,0:T(8,128)(2,1)S(1)} %fusion.37), channel_id=1, source_target_pairs={{0,8},{4,12},{8,16},{12,20},{16,24},{20,28},{1,9},{5,13},{9,17},{1... | collective-permute-start | bytes 2162696 | tf_op jit(solution)/shard_map/ppermute | solution.py:161
  742.0 65.2 %collective-permute-start.80 = (bf16[256,384]{0,1:T(8,128)(2,1)}, bf16[256,384]{0,1:T(8,128)(2,1)}, u32[]{:S(2)}, u32[]{:S(2)}) collective-permute-start(bf16[256,384]{0,1:T(8,128)(2,1)} %pad_maximum_fusion.50), channel_id=1, source_target_pairs={{0,4},{4,0},{8,12},{12,8},{16,20},{20,16},{24,28},{28,24},{1,5},{5... | collective-permute-start | bytes 589832 | tf_op jit(solution)/shard_map/ppermute | solution.py:136
  765.1 26.2 %collective-permute-start.104 = (bf16[1024,256]{1,0:T(8,128)(2,1)}, bf16[1024,256]{1,0:T(8,128)(2,1)S(1)}, u32[]{:S(2)}, u32[]{:S(2)}) collective-permute-start(bf16[1024,256]{1,0:T(8,128)(2,1)} %fusion.56), channel_id=1, source_target_pairs={{0,8},{4,12},{8,16},{12,20},{1,9},{5,13},{9,17},{13,21},{2,10},{6,... | collective-permute-start | bytes 1572872 | tf_op jit(solution)/shard_map/ppermute | solution.py:156
  794.5 30.5 %collective-permute-start.105 = (bf16[1024,256]{1,0:T(8,128)(2,1)}, bf16[1024,256]{1,0:T(8,128)(2,1)}, u32[]{:S(2)}, u32[]{:S(2)}) collective-permute-start(bf16[1024,256]{1,0:T(8,128)(2,1)} %fusion.55), channel_id=1, source_target_pairs={{0,8},{4,12},{8,16},{12,20},{16,24},{20,28},{1,9},{5,13},{9,17},{1... | collective-permute-start | bytes 1572872 | tf_op jit(solution)/shard_map/ppermute | solution.py:161
  816.1 27.3 %collective-permute-start.66 = (bf16[128,2048]{1,0:T(8,128)(2,1)S(1)}, bf16[128,2048]{1,0:T(8,128)(2,1)S(1)}, u32[]{:S(2)}, u32[]{:S(2)}) collective-permute-start(bf16[128,2048]{1,0:T(8,128)(2,1)S(1)} %slice.926), channel_id=1, source_target_pairs={{0,1},{1,0},{2,3},{3,2},{4,5},{5,4},{6,7},{7,6},{8,9},{9,8},{10,11... | collective-permute-start | bytes 1572872 | tf_op jit(solution)/shard_map/ppermute | solution.py:111
  857.3 25.4 %collective-permute-start.48 = (bf16[64,2048]{1,0:T(8,128)(2,1)S(1)}, bf16[64,2048]{1,0:T(8,128)(2,1)S(1)}, u32[]{:S(2)}, u32[]{:S(2)}) collective-permute-start(bf16[64,2048]{1,0:T(8,128)(2,1)S(1)} %get-tuple-element.168), channel_id=1, source_target_pairs={{0,2},{1,3},{2,0},{3,1},{4,6},{5,7},{6,4},{7,5},{8,10},{9,11},{10,... | collective-permute-start | bytes 786440 | tf_op jit(solution)/shard_map/ppermute | solution.py:117
  859.6 35.1 %collective-permute-start.68 = (bf16[64,2048]{1,0:T(8,128)(2,1)S(1)}, bf16[64,2048]{1,0:T(8,128)(2,1)S(1)}, u32[]{:S(2)}, u32[]{:S(2)}) collective-permute-start(bf16[64,2048]{1,0:T(8,128)(2,1)S(1)} %add_convert_fusion), channel_id=1, source_target_pairs={{0,2},{1,3},{2,0},{3,1},{4,6},{5,7},{6,4},{7,5},{8,10},{9,11},{10,... | collective-permute-start | bytes 786440 | tf_op jit(solution)/shard_map/ppermute | solution.py:117
  (342 other events, 3981.5 us)

commit v2 on v1

v2 whole, which is shorter than its diff:
```python
import jax
import jax.numpy as jnp
from jax import lax
from jax.experimental import pallas as pl
from jax.experimental.pallas import tpu as pltpu
from jax.sharding import PartitionSpec as P

EPS = 1e-06
BASE = 10000.0
NEG_LARGE = -1e30
LOW = jnp.bfloat16
F32 = jnp.float32
ORDER = (0, 2, 1, 3)
CORE = [(i, i ^ 1) for i in range(4)]
CROSS = [(i, i ^ 2) for i in range(4)]


def inverse_rms(values):
    return lax.rsqrt(jnp.mean(values * values, axis=-1, keepdims=True) + EPS)


def norm_backward(grad_hat, normed, inverse):
    return inverse * (grad_hat - normed * jnp.mean(grad_hat * normed, axis=-1, keepdims=True))


def dot(left, right):
    return jnp.dot(left, right, preferred_element_type=F32)


def inner_rows(left, right):
    return lax.dot_general(left, right, (((0,), (0,)), ((), ())), preferred_element_type=F32)


def inner_cols(left, right):
    return lax.dot_general(left, right, (((1,), (1,)), ((), ())), preferred_element_type=F32)


def documents(lengths_row, rows):
    first_end = lengths_row[0]
    second_end = first_end + lengths_row[1]
    doc_ids = (rows >= first_end).astype(jnp.int32) + (rows >= second_end).astype(jnp.int32)
    starts = jnp.where(rows >= second_end, second_end, jnp.where(rows >= first_end, first_end, 0))
    return (doc_ids, rows - starts)


def rotation(positions, head_dim):
    half = head_dim // 2
    freqs = BASE ** (-2.0 * jnp.arange(half, dtype=F32) / head_dim)
    angles = positions.astype(F32)[:, None] * freqs[None, :]
    return (jnp.cos(angles), jnp.sin(angles))


def rotate(values, cosine, sine):
    half = values.shape[-1] // 2
    first = values[..., :half]
    second = values[..., half:]
    return jnp.concatenate(
        [first * cosine - second * sine, second * cosine + first * sine], axis=-1
    )


def unrotate(grads, cosine, sine):
    return rotate(grads, cosine, -sine)


def in_vmem():
    return pl.BlockSpec(memory_space=pltpu.VMEM)


def whole(shape, dtype):
    return jax.ShapeDtypeStruct(shape, dtype)


def run(body, ids, args, outs, flops, scratch=(), name=None, limit=40):
    return pl.pallas_call(
        body,
        grid_spec=pltpu.PrefetchScalarGridSpec(
            num_scalar_prefetch=1,
            grid=(1,),
            in_specs=[in_vmem()] * len(args),
            out_specs=[in_vmem()] * len(outs),
            scratch_shapes=list(scratch),
        ),
        out_shape=list(outs),
        cost_estimate=pl.CostEstimate(flops=flops, bytes_accessed=1 << 20, transcendentals=0),
        compiler_params=pltpu.CompilerParams(vmem_limit_bytes=limit << 20),
        name=name,
    )(ids, *args)


def side_columns(source, mine, theirs, side):
    line, _, wide = mine.shape
    for z in range(line):
        mine[z] = source[:, pl.ds(pl.multiple_of((2 * z + side) * wide, wide), wide)]
        theirs[z] = source[:, pl.ds(pl.multiple_of((2 * z + 1 - side) * wide, wide), wide)]


def first_body(m, quarter, ids, x_ref, gain, q_down, kv_proj, cos, sin, c, kv, h1, mine, theirs):
    blocks = [
        x_ref[m, pl.ds(pl.multiple_of((ids[0] ^ k) * quarter, quarter), quarter), :] for k in ORDER
    ]
    x = jnp.concatenate(blocks, 0).astype(F32)
    low = (x * inverse_rms(x) * gain[...]).astype(LOW)
    h1[...] = low
    half = 2 * quarter
    pair = dot(low[:half], kv_proj[...])
    wide = kv_proj.shape[1] // 2
    kv[:, :wide] = rotate(pair[:, :wide], cos[:half], sin[:half]).astype(LOW)
    kv[:, wide:] = pair[:, wide:].astype(LOW)
    c[...] = dot(low, q_down[...]).astype(LOW)
    if mine is not None:
        side_columns(h1, mine, theirs, ids[1])


def cotangent_body(m, quarter, ids, z_ref, w_down, dhid, dz, mine, theirs):
    blocks = [
        z_ref[m, pl.ds(pl.multiple_of((ids[0] ^ k) * quarter, quarter), quarter), :] for k in ORDER
    ]
    dz[...] = jnp.concatenate(blocks, 0)
    if mine is not None:
        side_columns(dz, mine, theirs, ids[1])
    dhid[...] = inner_cols(dz[...], w_down[...])


def attend_body(
    scale, ids, c0, c1, c2, gain, q_up, cos, sin, kv, key_ids, row_ids, row_starts, out_proj,
    qn, q, o, lse, send, keep, mine, theirs,
):
    rows = qn.shape[0]
    quarter = rows // 4
    part = c0.shape[1]
    wide = q.shape[2]
    got = c1[...]
    pair = jnp.concatenate(
        [got[quarter : 2 * quarter], got[:quarter], got[3 * quarter :], got[2 * quarter : 3 * quarter]],
        0,
    )
    far = jnp.concatenate([c2[2 * quarter :], c2[: 2 * quarter]], 0)
    c = jnp.concatenate([c0[...], pair, far], 1).astype(F32)
    chat = c * inverse_rms(c)
    for k, xor in enumerate(ORDER):
        columns = pl.ds(pl.multiple_of((ids[0] ^ xor) * part, part), part)
        qn[:, columns] = (chat[:, k * part : (k + 1) * part] * gain[:, columns]).astype(LOW)
    if mine is not None:
        side_columns(qn, mine, theirs, ids[1])
    bias = jnp.where(
        (key_ids[...] >= row_starts[...]) & (key_ids[...] <= row_ids[...]), 0.0, NEG_LARGE
    )
    low = qn[...]
    keys, values = kv[:, :wide], kv[:, wide:]
    for h in range(q.shape[0]):
        pre = dot(low, q_up[:, h * wide : (h + 1) * wide])
        q_h = (rotate(pre, cos[...], sin[...]) * scale).astype(LOW)
        q[h] = q_h
        scores = inner_cols(q_h, keys) + bias
        top = jnp.max(scores, axis=-1, keepdims=True)
        probs = jnp.exp(scores - top)
        total = jnp.sum(probs, axis=-1, keepdims=True)
        out = dot(probs.astype(LOW), values) / total
        o[:, h * wide : (h + 1) * wide] = out.astype(LOW)
        log_total = jnp.broadcast_to(top + jnp.log(total), (rows, 128))
        lse[h : h + 1, :] = jnp.transpose(log_total)[:1]
    half = 2 * quarter
    send[...] = dot(o[half:, :], out_proj[...]).astype(LOW)
    keep[...] = dot(o[:half, :], out_proj[...])


def forward_body(ids, a0, a1, a2, w_gate, w_up, dhid, h2, hid, dgu, mine, theirs):
    h2[...] = jnp.concatenate([a0[...], a1[...], a2[...]], 0)
    if mine is not None:
        side_columns(h2, mine, theirs, ids[1])
    low = h2[...]
    wide = hid.shape[1]
    g = dot(low, w_gate[...])
    u = dot(low, w_up[...])
    sig = jax.nn.sigmoid(g)
    swish = g * sig
    hid[...] = (swish * u).astype(LOW)
    back = dhid[...]
    dgu[:, :wide] = (back * u * sig * (1.0 + g * (1.0 - sig))).astype(LOW)
    dgu[:, wide:] = (back * swish).astype(LOW)


def hidden_back_body(ids, dgu, w_gate, w_up, send, keep):
    wide = w_gate.shape[1]
    half = dgu.shape[0] // 2
    for rows, out in ((slice(half, None), send), (slice(0, half), keep)):
        out[...] = (
            inner_cols(dgu[rows, :wide], w_gate[...]) + inner_cols(dgu[rows, wide:], w_up[...])
        ).astype(out.dtype)


def block_body(count, extra, final, ids, *refs):
    lefts, rights = refs[:count], refs[count : 2 * count]
    added, outs = refs[2 * count : 2 * count + extra], refs[2 * count + extra :]
    total = None
    for a, b in zip(lefts, rights):
        term = inner_rows(a[ids[0]], b[...])
        total = term if total is None else total + term
    for ref in added:
        total = total + ref[...].astype(F32)
    if final == "turned":
        outs[0][...] = jnp.transpose(total)
    elif final == "split":
        wide = outs[0].shape[1]
        outs[0][...] = total[:, :wide]
        outs[1][...] = total[:, wide:]
    else:
        outs[0][...] = total.astype(outs[0].dtype)


def attend_back_body(
    scale, micro, chunk, ids, a0, a1, a2, out_proj, q_up, key_ids, *refs
):
    per = 7
    groups = [refs[m * per : (m + 1) * per] for m in range(micro)]
    dyl_out, dqp, send, keep, kv_send, kv_keep = refs[micro * per : micro * per + 6]
    dq_acc, do_acc, delta_acc = refs[-3:]
    sides = refs[micro * per + 6 : -3]
    for m in range(micro):
        q, kv, o, lse, row_ids, cos, sin = groups[m]
        heads, rows, wide = q.shape
        half_rows = rows // 2
        dyl = jnp.concatenate([a0[m], a1[m], a2[m]], 0)
        dyl_out[m] = dyl
        if sides:
            side_columns(dyl_out.at[m], sides[2 * m], sides[2 * m + 1], ids[1])
        for h in range(heads):
            do = inner_cols(dyl, out_proj[h * wide : (h + 1) * wide, :]).astype(LOW)
            do_acc[h] = do
            delta = jnp.sum(
                do.astype(F32) * o[:, h * wide : (h + 1) * wide].astype(F32), axis=-1, keepdims=True
            )
            delta_acc[h] = jnp.transpose(jnp.broadcast_to(delta, (rows, 128)))[:8]
            dq_acc[h] = jnp.zeros((rows, wide), F32)
        count = kv.shape[0] // 2 // chunk
        for part, out in ((0, kv_keep), (1, kv_send)):

            def one(i, carry):
                base = pl.multiple_of((part * count + i) * chunk, chunk)
                keys = kv[pl.ds(base, chunk), :wide]
                values = kv[pl.ds(base, chunk), wide:]
                at = key_ids[pl.ds(base, chunk), :]
                bias = jnp.where((at >= row_ids[1:2, :]) & (at <= row_ids[0:1, :]), 0.0, NEG_LARGE)

                def head(h, sums):
                    dk, dv = sums
                    q_h, do_h = q[h], do_acc[h]
                    probs = jnp.exp(inner_cols(keys, q_h) + bias - lse[pl.ds(h, 1), :])
                    back = inner_cols(values, do_h) - delta_acc[h][:1]
                    ds = (probs * back).astype(LOW)
                    dv = dv + dot(probs.astype(LOW), do_h)
                    dk = dk + dot(ds, q_h)
                    dq_acc[h] = dq_acc[h] + inner_rows(ds, keys)
                    return dk, dv

                zero = jnp.zeros((chunk, wide), F32)
                dk, dv = lax.fori_loop(0, heads, head, (zero, zero))
                place = pl.ds(pl.multiple_of(i * chunk, chunk), chunk)
                out[m, place, :wide] = dk.astype(out.dtype)
                out[m, place, wide:] = dv.astype(out.dtype)
                return carry

            if count == 1:
                one(0, 0)
            else:
                lax.fori_loop(0, count, one, 0)
        for h in range(heads):
            dq = unrotate(dq_acc[h] * scale, cos[...], sin[...])
            dqp[m, :, h * wide : (h + 1) * wide] = dq.astype(LOW)
        low = dqp[m]
        send[m] = inner_cols(low[half_rows:], q_up[...]).astype(LOW)
        keep[m] = inner_cols(low[:half_rows], q_up[...])


def natural_body(micro, quarter, ids, a0, a1, a2, out):
    for m in range(micro):
        pieces = (a0[m], a1[m], a2[m, :quarter, :], a2[m, quarter:, :])
        for k, piece in zip(ORDER, pieces):
            out[m, pl.ds(pl.multiple_of((ids[0] ^ k) * quarter, quarter), quarter), :] = piece


def local(
    tokens,
    lengths,
    norm1_gain,
    q_down,
    latent_gain,
    q_up,
    kv_proj,
    out_proj,
    norm2_gain,
    w_gate,
    w_up,
    w_down,
    cotangent,
):
    micro, rows, width = tokens.shape
    seq = lax.axis_size("seq")
    line = seq // 2
    at = lax.axis_index("seq").astype(jnp.int32)
    me = lax.axis_index("mp").astype(jnp.int32)
    place, side = at // 2, at % 2
    ids = jnp.stack([me, side])
    quarter, half = rows // 4, rows // 2
    head_dim = kv_proj.shape[1] // 2
    heads = q_up.shape[1] // head_dim
    part = q_down.shape[1]
    rank = q_up.shape[0]
    hidden = w_gate.shape[1]
    kv_part = kv_proj.shape[1] // 4
    wide = width // seq
    scale = head_dim ** (-0.5)
    key_count = seq * rows
    beside = [(i, i ^ 1) for i in range(seq)]

    def swap(index):
        return ((index & 1) << 1) | (index >> 1)

    def to_natural(array, axis):
        size = array.shape[axis] // 4
        return jnp.concatenate(
            [lax.dynamic_slice_in_dim(array, swap(me ^ b) * size, size, axis) for b in range(4)],
            axis,
        )

    def other(array):
        return lax.ppermute(array, "seq", beside)

    def sum_mp(send, keep):
        kept = keep + lax.ppermute(send, "mp", CORE).astype(F32)
        got = lax.ppermute(kept[..., quarter:, :].astype(LOW), "mp", CROSS)
        return kept[..., :quarter, :] + got.astype(F32)

    def gather_mp(piece):
        near = lax.ppermute(piece, "mp", CROSS)
        pair = jnp.concatenate([piece, near], -2)
        return piece, near, lax.ppermute(pair, "mp", CORE)

    def sides_shape(columns):
        if columns // seq % 128:
            return []
        return [whole((line, rows, columns // seq), LOW)] * 2

    def sides(made, full):
        if made:
            mine, theirs = made
        else:
            split = full.reshape(rows, line, 2, full.shape[1] // seq)
            mine = jnp.swapaxes(lax.dynamic_index_in_dim(split, side, 2, keepdims=False), 0, 1)
            theirs = jnp.swapaxes(
                lax.dynamic_index_in_dim(split, 1 - side, 2, keepdims=False), 0, 1
            )
        return mine, other(theirs)

    def without_sides(body, count):
        return body if count else lambda *refs: body(*refs, None, None)

    def reduce_line(lefts, rights, final):
        w, columns = lefts[0].shape[2], rights[0].shape[1]
        flops = 2 * w * columns * rows * len(lefts)

        def block(index, added, outs, kind):
            return run(
                lambda *refs: block_body(len(lefts), len(added), kind, *refs),
                index.reshape(1),
                [*lefts, *rights, *added],
                outs,
                flops,
                name="block",
            )

        low = [whole((w, columns), LOW)]
        up = down = None
        for step in range(1, line):
            goes_up = [(i, i + 2) for i in range(2 * step)]
            goes_down = [(seq - 1 - i, seq - 3 - i) for i in range(2 * step)]
            for_up, for_down = line - step + place, step - line + place
            if 2 * step < line + 1:
                which = jnp.where(
                    place <= step - 1, for_up, jnp.where(place >= line - step, for_down, 0)
                )
                (term,) = block(which, [a for a in (up, down) if a is not None], low, None)
                if step == 1 and line > 3:
                    up = lax.ppermute(term, "seq", goes_up + goes_down)
                else:
                    up = lax.ppermute(term, "seq", goes_up)
                    down = lax.ppermute(term, "seq", goes_down)
            else:
                (term_up,) = block(jnp.clip(for_up, 0, line - 1), [up], low, None)
                (term_down,) = block(jnp.clip(for_down, 0, line - 1), [down], low, None)
                up = lax.ppermute(term_up, "seq", goes_up)
                down = lax.ppermute(term_down, "seq", goes_down)
        if final == "turned":
            outs = [whole((columns, w), F32)]
        elif final == "split":
            outs = [whole((w, columns // 2), F32)] * 2
        else:
            outs = [whole((w, columns), F32)]
        return block(place, [up, down], outs, final)

    def with_other(arrays):
        return list(arrays) + [other(a) for a in arrays]

    def two_sides(pairs):
        return [p[0] for p in pairs] + [p[1] for p in pairs]

    quarter_rows = jnp.arange(quarter, dtype=jnp.int32)
    row_ids = at * rows + jnp.concatenate([(me ^ k) * quarter + quarter_rows for k in ORDER])
    key_ids = (
        ((place - jnp.arange(line, dtype=jnp.int32)[None, None, :, None, None]) * 2
         + (side ^ jnp.arange(2, dtype=jnp.int32)[None, :, None, None, None])) * rows
        + (me ^ (jnp.arange(2, dtype=jnp.int32)[:, None, None, None, None]
                 + 2 * jnp.arange(2, dtype=jnp.int32)[None, None, None, :, None])) * quarter
        + quarter_rows[None, None, None, None, :]
    ).reshape(key_count)

    gain1_row, gain2_row, gain_c_row = norm1_gain[None, :], norm2_gain[None, :], latent_gain[None, :]
    kv_cols = lax.dynamic_slice_in_dim(kv_proj, me * kv_part, kv_part, 1)
    first_weights = jnp.concatenate([q_down, kv_cols], axis=1)
    width_sides = sides_shape(width)
    rank_sides = sides_shape(rank)

    tables, starts, kv, c_part, h1_pairs = [], [], [], [], []
    for m in range(micro):
        _, places = documents(lengths[m], row_ids)
        starts.append(row_ids - places)
        tables.append(rotation(places, head_dim))
        c, packed, h1, *made = run(
            without_sides(lambda *refs: first_body(m, quarter, *refs), len(width_sides)),
            ids,
            [tokens, gain1_row, q_down, kv_proj, *tables[m]],
            [whole((rows, part), LOW), whole((half, 2 * head_dim), LOW), whole((rows, width), LOW),
             *width_sides],
            2 * width * (rows * part + half * 2 * head_dim),
            name="first",
        )
        blocks = [packed] + [
            lax.ppermute(packed, "seq", [(i, i + 2 * d) for i in range(seq - 2 * d)])
            for d in range(1, line)
        ]
        near = jnp.stack(blocks, 0)
        near = jnp.stack([near, other(near)], 0)
        kv.append(
            jnp.stack([near, lax.ppermute(near, "mp", CORE)], 0).reshape(key_count, 2 * head_dim)
        )
        c_part.append(c)
        h1_pairs.append(sides(made, h1))

    dhid, dz_pairs, dz_rows = [], [], []
    for m in range(micro):
        back, dz, *made = run(
            without_sides(lambda *refs: cotangent_body(m, quarter, *refs), len(width_sides)),
            ids,
            [cotangent, w_down],
            [whole((rows, hidden), F32), whole((rows, width), LOW), *width_sides],
            2 * rows * width * hidden,
            name="cotangent",
        )
        dhid.append(back)
        dz_rows.append(dz)
        dz_pairs.append(sides(made, dz))

    qn_pairs, h2_pairs, hid, dgu, qs, os, lses, state = [], [], [], [], [], [], [], []
    for m in range(micro):
        near = lax.ppermute(c_part[m], "mp", CROSS)
        swapped = jnp.concatenate(
            [near[quarter : 2 * quarter], near[:quarter], near[3 * quarter :], near[2 * quarter : 3 * quarter]], 0
        )
        far = lax.ppermute(jnp.concatenate([c_part[m], swapped], 1), "mp", CORE)
        qn, q, o, lse, send, keep, *made = run(
            without_sides(lambda *refs: attend_body(scale, *refs), len(rank_sides)),
            ids,
            [c_part[m], near, far, gain_c_row, q_up, *tables[m], kv[m], key_ids[None, :],
             row_ids[:, None], starts[m][:, None], out_proj],
            [whole((rows, rank), LOW), whole((heads, rows, head_dim), LOW),
             whole((rows, heads * head_dim), LOW), whole((heads, rows), F32),
             whole((half, width), LOW), whole((half, width), F32), *rank_sides],
            2 * rows * heads * head_dim * (rank + 2 * key_count + width),
            name="attend",
        )
        qn_pairs.append(sides(made, qn))
        x = lax.dynamic_slice_in_dim(tokens[m], me * quarter, quarter, 0).astype(F32)
        inv1 = inverse_rms(x)
        y = x + sum_mp(send, keep)
        inv2 = inverse_rms(y)
        n2 = y * inv2
        pieces = gather_mp((n2 * gain2_row).astype(LOW))
        h2, hid_m, dgu_m, *made = run(
            without_sides(forward_body, len(width_sides)),
            ids,
            [*pieces, w_gate, w_up, dhid[m]],
            [whole((rows, width), LOW), whole((rows, hidden), LOW), whole((rows, 2 * hidden), LOW),
             *width_sides],
            4 * rows * width * hidden,
            name="forward",
        )
        h2_pairs.append(sides(made, h2))
        hid.append(hid_m)
        dgu.append(dgu_m)
        qs.append(q)
        os.append(o)
        lses.append(lse)
        c_rows = jnp.concatenate(
            [c_part[m][:quarter], swapped[:quarter], far[half : half + quarter]], 1
        )
        state.append(dict(x=x, n1=x * inv1, inv1=inv1, y=y, n2=n2, inv2=inv2, c=c_rows))

    (grad_down,) = reduce_line(two_sides(dz_pairs), with_other(hid), "turned")
    grad_gate, grad_up = reduce_line(two_sides(h2_pairs), with_other(dgu), "split")

    def stacked(name):
        return jnp.stack([st[name] for st in state], 0)

    back = [
        run(
            hidden_back_body,
            ids,
            [dgu[m], w_gate, w_up],
            [whole((half, width), LOW), whole((half, width), F32)],
            4 * rows * width * hidden,
            name="hidden_back",
        )
        for m in range(micro)
    ]
    dh2 = sum_mp(jnp.stack([b[0] for b in back], 0), jnp.stack([b[1] for b in back], 0))
    y, n2, inv2, n1, inv1 = (stacked(k) for k in ("y", "n2", "inv2", "n1", "inv1"))
    dz_own = jnp.stack([dz[:quarter] for dz in dz_rows], 0).astype(F32)
    gain2 = jnp.sum(dh2 * n2, axis=(0, 1))
    dy = dz_own + norm_backward(dh2 * gain2_row, n2, inv2)

    def attend_back(which, pieces):
        args = [*pieces, out_proj, q_up, key_ids[:, None]]
        for m in which:
            args += [qs[m], kv[m], os[m], lses[m], jnp.stack([row_ids, starts[m]], 0), *tables[m]]
        n = len(which)
        return run(
            lambda *refs: attend_back_body(scale, n, min(1024, key_count // 2), *refs),
            ids,
            args,
            [whole((n, rows, width), LOW), whole((n, rows, heads * head_dim), LOW),
             whole((n, half, rank), LOW), whole((n, half, rank), F32),
             whole((n, key_count // 2, 2 * head_dim), LOW),
             whole((n, key_count // 2, 2 * head_dim), F32), *(width_sides * n)],
            2 * n * rows * heads * head_dim * (5 * key_count + width + rank),
            scratch=[pltpu.VMEM((heads, rows, head_dim), F32),
                     pltpu.VMEM((heads, rows, head_dim), LOW),
                     pltpu.VMEM((heads, 8, rows), F32)],
            name="attend_back",
            limit=56,
        )

    pieces = gather_mp(dy.astype(LOW))
    if key_count <= 2048:
        dyl, dqp, send, keep, kv_send, kv_keep, *made = attend_back(range(micro), pieces)
    else:
        each = [attend_back([m], [p[m : m + 1] for p in pieces]) for m in range(micro)]
        dyl, dqp, send, keep, kv_send, kv_keep = (
            jnp.concatenate([e[i] for e in each], 0) for i in range(6)
        )
        made = [a for e in each for a in e[6:]]
    dyl_pairs = [sides(made[2 * m : 2 * m + 2], dyl[m]) for m in range(micro)]
    (grad_out,) = reduce_line(two_sides(dyl_pairs), with_other(os), "turned")
    (grad_qup,) = reduce_line(two_sides(qn_pairs), with_other([dqp[m] for m in range(micro)]), None)

    dqn = sum_mp(send, keep)
    c = stacked("c").astype(F32)
    inv_c = inverse_rms(c)
    chat = c * inv_c
    chat = to_natural(chat, 2)
    gain_c = jnp.sum(dqn * chat, axis=(0, 1))
    dc = norm_backward(dqn * gain_c_row, chat, inv_c).astype(LOW)

    dkv = kv_keep + lax.ppermute(kv_send, "mp", CORE).astype(F32)
    dkv = dkv.reshape(micro, 2, line, 2, quarter, 2 * head_dim)
    dkv = dkv[:, :, :, 0] + lax.ppermute(dkv[:, :, :, 1].astype(LOW), "mp", CROSS).astype(F32)
    dkv = dkv[:, 0] + other(dkv[:, 1].astype(LOW)).astype(F32)
    total = dkv[:, 0]
    for d in range(1, line):
        total = total + lax.ppermute(
            dkv[:, d].astype(LOW), "seq", [(i + 2 * d, i) for i in range(seq - 2 * d)]
        ).astype(F32)
    cosine = jnp.stack([t[0][:quarter] for t in tables], 0)
    sine = jnp.stack([t[1][:quarter] for t in tables], 0)
    dkv_low = jnp.concatenate(
        [unrotate(total[..., :head_dim], cosine, sine), total[..., head_dim:]], axis=-1
    ).astype(LOW)
    both = jnp.concatenate(gather_mp(jnp.concatenate([dc, dkv_low], -1)), -2)
    dfirst = jnp.concatenate(
        [lax.dynamic_slice_in_dim(both, me * part, part, 2),
         lax.dynamic_slice_in_dim(both, rank + me * kv_part, kv_part, 2)], -1
    )
    dfirst_list = [dfirst[m] for m in range(micro)]
    (grad_first,) = reduce_line(two_sides(h1_pairs), with_other(dfirst_list), None)
    grad_qdown = grad_first[:, :part]
    kv_cols_grad = grad_first[:, part:]
    pieces = []
    for k in ORDER:
        size = kv_cols_grad.shape[0] // 4
        sent = lax.dynamic_slice_in_dim(kv_cols_grad, (me ^ k) * size, size, 0)
        pieces.append(lax.ppermute(sent, "mp", [(i, i ^ k) for i in range(4)]) if k else sent)
    grad_kv = to_natural(jnp.concatenate(pieces, 1), 1)

    def put_natural(pieces):
        return run(
            lambda *refs: natural_body(micro, quarter, *refs),
            ids,
            pieces,
            [whole((micro, rows, width), LOW)],
            0,
            name="natural",
        )[0]

    part_sum = inner_cols(dfirst.reshape(micro * rows, -1), first_weights).reshape(micro, rows, width)
    dh1 = sum_mp(part_sum[:, half:].astype(LOW), part_sum[:, :half])
    gain1 = jnp.sum(dh1 * n1, axis=(0, 1))
    dx = (dy + norm_backward(dh1 * gain1_row, n1, inv1)).astype(LOW)
    input_grads = put_natural(gather_mp(dx))

    ffn = [dot(hid[m], w_down) for m in range(micro)]
    ffn = sum_mp(
        jnp.stack([f[half:] for f in ffn], 0).astype(LOW), jnp.stack([f[:half] for f in ffn], 0)
    )
    layer_out = put_natural(gather_mp((y + ffn).astype(LOW)))

    gains = jnp.concatenate(
        [gain1.reshape(seq, -1), gain2.reshape(seq, -1), gain_c.reshape(seq, -1)], axis=1
    )
    gains = gains + lax.ppermute(gains, "mp", CORE)
    gains = gains + lax.ppermute(gains, "mp", CROSS)
    gain_sum = lax.dynamic_index_in_dim(gains, at, 0, keepdims=False)
    for k in range(1, seq):
        gain_sum = gain_sum + lax.ppermute(
            lax.dynamic_index_in_dim(gains, at ^ k, 0, keepdims=False),
            "seq",
            [(i, i ^ k) for i in range(seq)],
        )
    return (
        layer_out,
        input_grads,
        gain_sum[:wide],
        grad_qdown,
        gain_sum[2 * wide :],
        grad_qup,
        grad_kv,
        grad_out,
        gain_sum[wide : 2 * wide],
        grad_gate,
        grad_up,
        grad_down,
    )


def solution(mesh):
    placed = (
        P(None, "seq", None),
        P(),
        P(),
        P(None, "mp"),
        P(),
        P(None, "mp"),
        P(),
        P("mp", None),
        P(),
        P(None, "mp"),
        P(None, "mp"),
        P("mp", None),
        P(None, "seq", None),
    )
    return jax.shard_map(
        local,
        mesh=mesh,
        in_specs=placed,
        out_specs=(
            P(None, "seq", None),
            P(None, "seq", None),
            P("seq"),
            P("seq", "mp"),
            P("seq"),
            P("seq", "mp"),
            P(("seq", "mp"), None),
            P("mp", "seq"),
            P("seq"),
            P("seq", "mp"),
            P("seq", "mp"),
            P("mp", "seq"),
        ),
        check_vma=False,
    )
```

time: 906 us -> 748 us (0.83)
  matrix products: 166 us -> 6.06 us
  Pallas kernels: 0 us -> 149 us
  other arithmetic: 130 us -> 52.5 us
  local copies, waits for them, and re-layouts: 143 us -> 78.9 us
    pallas_call x0 -> x38, Pallas kernels: none -> 149 us  [run(): pl.pallas_call(body, grid_spec=pltpu.PrefetchScalarGridSpec(num_scalar_pr...]
    dot_general x42 -> x0, matrix products: 105 us -> none  [the longest x30 63.5 us: inner_rows(): lax.dot_general(left, right, (((0,), (0,)), ((), ())), preferred_element_...]
    ppermute x16 -> x23, waiting for transfers between devices: 86.5 us -> 138 us  [other(): return lax.ppermute(array, 'seq', beside)]
    ppermute x85 -> x50, waiting for transfers between devices: 113 us -> 72.8 us  [the longest x6 21.9 us: sum_mp(): got = lax.ppermute(kept[..., quarter:, :].astype(LOW), 'mp', CROSS)]
    concatenate x42 -> x15, other arithmetic: 41.8 us -> 7.92 us  [the longest x6 4.3 us: gather_mp(): pair = jnp.concatenate([piece, near], -2)]
    dynamic_slice x16 -> x4, local copies, waits for them, and re-layouts: 33.4 us -> 0.12 us  [the longest x1 0.06 us: local(): lax.dynamic_index_in_dim(gains, at ^ k, 0, keepdims=False)]
    dot_general x14 -> x2, matrix products: 34.3 us -> 4.77 us  [dot(): return jnp.dot(left, right, preferred_element_type=F32)]
    concatenate x21 -> x1, local copies, waits for them, and re-layouts: 26.5 us -> 0.14 us  [local(): jnp.concatenate([(me ^ k) * quarter + quarter_rows for k in ORDER])]
  transfers between devices with their start and end apart: 132 -> 101, of which waited for: 43 -> 36; matrix products, arithmetic and copies ran while one was open for 45% -> 11% of each run, Pallas kernels for 0% -> 19%
where the time goes in v2:
time: 748 us; the launch traced here: 740 us
  waiting for transfers between devices  257 us (34%)
  starting transfers between devices  191 us (26%)
  Pallas kernels  149 us (20%)
  local copies, waits for them, and re-layouts  78.9 us (11%)
  other arithmetic  52.5 us (7%)
    pallas_call x38, Pallas kernels, run(): pl.pallas_call(body, grid_spec=pltpu.PrefetchScalarGridSpec(num_scalar_pr...  149 us
    ppermute x23, waiting for transfers between devices, other(): return lax.ppermute(array, 'seq', beside)  138 us
    unnamed x476, local copies, waits for them, and re-layouts  53.2 us
    ppermute x5, starting transfers between devices, reduce_line(): up = lax.ppermute(term_up, 'seq', goes_up)  50.6 us
    ppermute x5, starting transfers between devices, reduce_line(): up = lax.ppermute(term, 'seq', goes_up)  38 us
    ppermute x23, starting transfers between devices, other(): return lax.ppermute(array, 'seq', beside)  24.2 us
    ppermute x5, waiting for transfers between devices, reduce_line(): up = lax.ppermute(term, 'seq', goes_up + goes_down)  22.6 us
    ppermute x6, waiting for transfers between devices, sum_mp(): got = lax.ppermute(kept[..., quarter:, :].astype(LOW), 'mp', CROSS)  21.9 us
  transfers between devices with their start and end apart: 101, of which 36 were waited for; matrix products, arithmetic and copies ran while one was open for 11% of the time, Pallas kernels for 19%

profile of v2, /device:TPU:0, one launch (start us, length us, event | category | flops | bytes accessed | tf_op | source)
XLA Modules:
  0.0 740.5 jit_solution(873437232812242782)
XLA Ops:
  15.9 7.6 %collective-permute-start.4 = (bf16[128,512]{1,0:T(8,128)(2,1)}, bf16[128,512]{1,0:T(8,128)(2,1)}, u32[]{:S(2)}, u32[]{:S(2)}) collective-permute-start(bf16[128,512]{1,0:T(8,128)(2,1)} %get-tuple-element.66), channel_id=1, source_target_pairs={{0,24},{4,28},{1,25},{5,29},{2,26},{6,30},{3,27},{7,31}} | collective-permute-start | bytes 393224 | tf_op jit(solution)/shard_map/ppermute | solution.py:439
  67.3 12.3 %collective-permute-done.5 = bf16[4,128,512]{2,1,0:T(8,128)(2,1)} collective-permute-done((bf16[4,128,512]{2,1,0:T(8,128)(2,1)}, bf16[4,128,512]{2,1,0:T(8,128)(2,1)}, u32[]{:S(2)}, u32[]{:S(2)}) %collective-permute-start.5) | collective-permute-done | bytes 524320 | tf_op jit(solution)/shard_map/ppermute | solution.py:328
  87.9 8.4 %attend.3 = (bf16[256,1024]{1,0:T(8,128)(2,1)}, bf16[4,256,256]{2,1,0:T(8,128)(2,1)S(1)}, bf16[256,1024]{1,0:T(8,128)(2,1)S(1)}, f32[4,256]{1,0:T(4,128)S(1)}, b...) custom-call(s32[2]{0:T(128)S(1)} %pad_add_fusion.3.refs_0_.ids, ...), custom_call_target="tpu_custom_call" | custom-call | flops 3758096384 | bytes 1048576 | tf_op jit(solution)/shard_map/attend/pallas_call | solution.py:75
  97.5 9.5 %attend.2 = (bf16[256,1024]{1,0:T(8,128)(2,1)}, bf16[4,256,256]{2,1,0:T(8,128)(2,1)S(1)}, bf16[256,1024]{1,0:T(8,128)(2,1)S(1)}, f32[4,256]{1,0:T(4,128)S(1)}, b...) custom-call(s32[2]{0:T(128)S(1)} %pad_add_fusion.3.refs_0_.ids, ...), custom_call_target="tpu_custom_call" | custom-call | flops 3758096384 | bytes 1048576 | tf_op jit(solution)/shard_map/attend/pallas_call | solution.py:75
  115.6 6.9 collective-permute-done.17
  147.5 8.5 %forward.3 = (bf16[256,2048]{1,0:T(8,128)(2,1)}, bf16[256,1408]{1,0:T(8,128)(2,1)}, bf16[256,2816]{1,0:T(8,128)(2,1)S(1)}, bf16[4,256,256]{2,1,0:T(8,128)(2,1)S(1)}, bf16[4,256,256]{2,1,0:T(8,128)(2,1)S(1)}) custom-call(s32[2]{0:T(128)S(1)} %pad_add_fusion.3.refs_0_.ids, bf16[64,2048]{1,0:T(8,128)(2,1)S(1)} %copy-done.102, bf16[64,2048]{1,0:T(8,128)(2,1)S(1)} %copy-done.118, ...), custom_call_target="tpu_custom_call" | custom-call | flops 2952790016 | bytes 1048576 | tf_op jit(solution)/shard_map/forward/pallas_call | solution.py:75
  159.0 8.1 %hidden_back.3 = (bf16[128,2048]{1,0:T(8,128)(2,1)S(1)}, f32[128,2048]{1,0:T(8,128)S(1)}) custom-call(s32[2]{0:T(128)S(1)} %pad_add_fusion.3.refs_0_.ids, bf16[256,2816]{1,0:T(8,128)(2,1)S(1)} %get-tuple-element.81.dgu.refs_6_, bf16[2048,1408]{1,0:T(8,128)(2,1)S(1)} %bitcast.158, bf16[2048,1408]{1,0:T(8,128)(2,1)S(1)} %copy-done.1), custom_call_target="tpu_custom_call" | custom-call | flops 2952790016 | bytes 1048576 | tf_op jit(solution)/shard_map/hidden_back/pallas_call | solution.py:75
  167.3 7.2 forward.2
  175.3 3.6 copy-done.2
  178.9 7.9 %hidden_back.2 = (bf16[128,2048]{1,0:T(8,128)(2,1)S(1)}, f32[128,2048]{1,0:T(8,128)S(1)}) custom-call(s32[2]{0:T(128)S(1)} %pad_add_fusion.3.refs_0_.ids, bf16[256,2816]{1,0:T(8,128)(2,1)S(1)} %get-tuple-element.79.dgu.refs_5_, bf16[2048,1408]{1,0:T(8,128)(2,1)S(1)} %bitcast.158, bf16[2048,1408]{1,0:T(8,128)(2,1)S(1)} %copy-done.2), custom_call_target="tpu_custom_call" | custom-call | flops 2952790016 | bytes 1048576 | tf_op jit(solution)/shard_map/hidden_back/pallas_call | solution.py:75
  194.0 12.8 %collective-permute-done.27 = bf16[2,64,2048]{2,1,0:T(8,128)(2,1)S(1)} collective-permute-done((bf16[2,64,2048]{2,1,0:T(8,128)(2,1)S(1)}, bf16[2,64,2048]{2,1,0:T(8,128)(2,1)S(1)}, u32[]{:S(2)}, u32[]{:S(2)}) %collective-permute-start.27) | collective-permute-done | bytes 524320 | tf_op jit(solution)/shard_map/ppermute | solution.py:332
  214.0 8.8 %collective-permute-done.28.refs_2_ = bf16[2,64,2048]{2,1,0:T(8,128)(2,1)S(1)} collective-permute-done((bf16[2,64,2048]{2,1,0:T(8,128)(2,1)S(1)}, bf16[2,64,2048]{2,1,0:T(8,128)(2,1)S(1)}, u32[]{:S(2)}, u32[]{:S(2)}) %collective-permute-start.28) | collective-permute-done | bytes 524320 | tf_op jit(solution)/shard_map/ppermute | solution.py:336
  227.2 35.1 %attend_back.1 = (bf16[2,256,2048]{2,1,0:T(8,128)(2,1)}, bf16[2,256,1024]{2,1,0:T(8,128)(2,1)}, bf16[2,128,1024]{2,1,0:T(8,128)(2,1)}, f32[2,128,1024]{2,1,0:T(8...) custom-call(s32[2]{0:T(128)} %copy-done.156, ...), custom_call_target="tpu_custom_call" | custom-call | flops 13958643712 | bytes 1048576 | tf_op jit(solution)/shard_map/attend_back/pallas_call | solution.py:75
  276.5 8.0 %collective-permute-done.94.refs_7_ = bf16[256,1408]{1,0:T(8,128)(2,1)S(1)} collective-permute-done((bf16[256,1408]{1,0:T(8,128)(2,1)S(1)}, bf16[256,1408]{1,0:T(8,128)(2,1)S(1)}, u32[]{:S(2)}, u32[]{:S(2)}) %collective-permute-start.94) | collective-permute-done | bytes 720928 | tf_op jit(solution)/shard_map/ppermute | solution.py:328
  289.6 7.3 collective-permute-done.33
  299.5 58.0 %collective-permute-done.84.refs_4_ = bf16[4,256,256]{2,1,0:T(8,128)(2,1)S(1)} collective-permute-done((bf16[4,256,256]{2,1,0:T(8,128)(2,1)S(1)}, bf16[4,256,256]{2,1,0:T(8,128)(2,1)S(1)}, u32[]{:S(2)}, u32[]{:S(2)}) %collective-permute-start.84) | collective-permute-done | bytes 524320 | tf_op jit(solution)/shard_map/ppermute | solution.py:328
  358.6 10.2 %collective-permute-done.83.refs_3_ = bf16[4,256,256]{2,1,0:T(8,128)(2,1)S(1)} collective-permute-done((bf16[4,256,256]{2,1,0:T(8,128)(2,1)S(1)}, bf16[4,256,256]{2,1,0:T(8,128)(2,1)S(1)}, u32[]{:S(2)}, u32[]{:S(2)}) %collective-permute-start.83) | collective-permute-done | bytes 524320 | tf_op jit(solution)/shard_map/ppermute | solution.py:328
  371.9 18.7 %collective-permute-done.34 = bf16[2,4,64,512]{3,2,0,1:T(8,128)(2,1)S(1)} collective-permute-done((bf16[2,4,64,512]{3,2,0,1:T(8,128)(2,1)S(1)}, bf16[2,4,64,512]{3,2,0,1:T(8,128)(2,1)S(1)}, u32[]{:S(2)}, u32[]{:S(2)}) %collective-permute-start.34) | collective-permute-done | bytes 524320 | tf_op jit(solution)/shard_map/ppermute | solution.py:328
  395.2 4.2 collective-permute-done.35
  400.4 6.5 collective-permute-done.37
  415.6 9.1 %collective-permute-done.96.refs_9_ = bf16[256,1408]{1,0:T(8,128)(2,1)S(1)} collective-permute-done((bf16[256,1408]{1,0:T(8,128)(2,1)S(1)}, bf16[256,1408]{1,0:T(8,128)(2,1)S(1)}, u32[]{:S(2)}, u32[]{:S(2)}) %collective-permute-start.96) | collective-permute-done | bytes 720928 | tf_op jit(solution)/shard_map/ppermute | solution.py:385
  439.7 12.0 %collective-permute-done.87.refs_9_ = bf16[256,2816]{1,0:T(8,128)(2,1)S(1)} collective-permute-done((bf16[256,2816]{1,0:T(8,128)(2,1)S(1)}, bf16[256,2816]{1,0:T(8,128)(2,1)S(1)}, u32[]{:S(2)}, u32[]{:S(2)}) %collective-permute-start.87) | collective-permute-done | bytes 1441824 | tf_op jit(solution)/shard_map/ppermute | solution.py:385
  457.5 3.9 collective-permute-done.75.refs_4_
  468.7 3.9 collective-permute-done.65.refs_8_
  472.6 5.0 collective-permute-start.97
  477.6 6.2 collective-permute-done.64.refs_7_
  488.6 6.5 collective-permute-done.53.refs_3_
  496.9 7.2 collective-permute-done.54.refs_4_
  504.1 5.0 collective-permute-start.78
  513.1 17.9 %collective-permute-start.88 = (bf16[256,2816]{1,0:T(8,128)(2,1)}, bf16[256,2816]{1,0:T(8,128)(2,1)}, u32[]{:S(2)}, u32[]{:S(2)}) collective-permute-start(bf16[256,2816]{1,0:T(8,128)(2,1)} %block.41), channel_id=1, source_target_pairs={{0,8},{4,12},{8,16},{12,20},{1,9},{5,13},{9,17},{13,21},{2,10},{6,... | collective-permute-start | bytes 4325384 | tf_op jit(solution)/shard_map/ppermute | solution.py:387
  538.8 9.4 %collective-permute-start.67 = (bf16[128,1024]{1,0:T(8,128)(2,1)S(1)}, bf16[128,1024]{1,0:T(8,128)(2,1)S(1)}, u32[]{:S(2)}, u32[]{:S(2)}) collective-permute-start(bf16[128,1024]{1,0:T(8,128)(2,1)S(1)} %block.31), channel_id=1, source_target_pairs={{0,8},{4,12},{8,16},{12,20},{1,9},{5,13},{9,17},{13,21},{2,10},{6,... | collective-permute-start | bytes 786440 | tf_op jit(solution)/shard_map/ppermute | solution.py:387
  549.3 3.6 block.47
  554.7 5.7 collective-permute-done.67.refs_9_
  560.4 29.6 %collective-permute-start.98 = (bf16[256,1408]{1,0:T(8,128)(2,1)}, bf16[256,1408]{1,0:T(8,128)(2,1)S(1)}, u32[]{:S(2)}, u32[]{:S(2)}) collective-permute-start(bf16[256,1408]{1,0:T(8,128)(2,1)} %block.47), channel_id=1, source_target_pairs={{0,8},{4,12},{8,16},{12,20},{16,24},{20,28},{1,9},{5,13},{9,17},{1... | collective-permute-start | bytes 2162696 | tf_op jit(solution)/shard_map/ppermute | solution.py:392
  596.3 4.9 collective-permute-start.57
  601.9 4.3 block.43
  606.2 4.2 block.42
  610.4 7.4 %collective-permute-done.79.refs_9_ = bf16[256,1024]{1,0:T(8,128)(2,1)S(1)} collective-permute-done((bf16[256,1024]{1,0:T(8,128)(2,1)S(1)}, bf16[256,1024]{1,0:T(8,128)(2,1)S(1)}, u32[]{:S(2)}, u32[]{:S(2)}) %collective-permute-start.79) | collective-permute-done | bytes 524320 | tf_op jit(solution)/shard_map/ppermute | solution.py:387
  621.5 5.5 collective-permute-start.89
  635.3 4.6 collective-permute-start.68
  642.5 17.1 %collective-permute-done.70.refs_10_ = bf16[128,1024]{1,0:T(8,128)(2,1)S(1)} collective-permute-done((bf16[128,1024]{1,0:T(8,128)(2,1)S(1)}, bf16[128,1024]{1,0:T(8,128)(2,1)S(1)}, u32[]{:S(2)}, u32[]{:S(2)}) %collective-permute-start.70) | collective-permute-done | bytes 262176 | tf_op jit(solution)/shard_map/ppermute | solution.py:393
  662.2 5.8 collective-permute-start.80
  673.5 7.5 %collective-permute-done.58.refs_9_ = bf16[256,384]{1,0:T(8,128)(2,1)S(1)} collective-permute-done((bf16[256,384]{1,0:T(8,128)(2,1)S(1)}, bf16[256,384]{1,0:T(8,128)(2,1)S(1)}, u32[]{:S(2)}, u32[]{:S(2)}) %collective-permute-start.58) | collective-permute-done | bytes 196640 | tf_op jit(solution)/shard_map/ppermute | solution.py:387
  688.7 4.1 block.49
  698.2 5.2 collective-permute-start.59
  704.9 3.3 block.39
  708.2 5.1 block.44
  724.8 3.3 collective-permute-start.51
  (808 shorter events, 277.1 us)
Async XLA Ops:
  15.9 37.2 %collective-permute-start.4 = (bf16[128,512]{1,0:T(8,128)(2,1)}, bf16[128,512]{1,0:T(8,128)(2,1)}, u32[]{:S(2)}, u32[]{:S(2)}) collective-permute-start(bf16[128,512]{1,0:T(8,128)(2,1)} %get-tuple-element.66), channel_id=1, source_target_pairs={{0,24},{4,28},{1,25},{5,29},{2,26},{6,30},{3,27},{7,31}} | collective-permute-start | bytes 393224 | tf_op jit(solution)/shard_map/ppermute | solution.py:439
  23.5 30.1 %collective-permute-start.3 = (bf16[128,512]{1,0:T(8,128)(2,1)}, bf16[128,512]{1,0:T(8,128)(2,1)}, u32[]{:S(2)}, u32[]{:S(2)}) collective-permute-start(bf16[128,512]{1,0:T(8,128)(2,1)} %get-tuple-element.66), channel_id=1, source_target_pairs={{0,16},{4,20},{8,24},{12,28},{1,17},{5,21},{9,25},{13,29},{2,18},{... | collective-permute-start | bytes 393224 | tf_op jit(solution)/shard_map/ppermute | solution.py:439
  40.2 43.2 %collective-permute-start = (bf16[256,256]{1,0:T(8,128)(2,1)S(1)}, bf16[256,256]{1,0:T(8,128)(2,1)}, u32[]{:S(2)}, u32[]{:S(2)}) collective-permute-start(bf16[256,256]{1,0:T(8,128)(2,1)S(1)} %get-tuple-element.65.refs_1_), channel_id=1, source_target_pairs={{0,2},{1,3},{2,0},{3,1},{4,6},{5,7},{6,4},{7,5},{8,10},{9,11},{10,... | collective-permute-start | bytes 393224 | tf_op jit(solution)/shard_map/ppermute | solution.py:466
  53.0 29.4 %collective-permute-start.9 = (bf16[256,256]{1,0:T(8,128)(2,1)S(1)}, bf16[256,256]{1,0:T(8,128)(2,1)}, u32[]{:S(2)}, u32[]{:S(2)}) collective-permute-start(bf16[256,256]{1,0:T(8,128)(2,1)S(1)} %get-tuple-element.69.refs_1_), channel_id=1, source_target_pairs={{0,2},{1,3},{2,0},{3,1},{4,6},{5,7},{6,4},{7,5},{8,10},{9,11},{10,... | collective-permute-start | bytes 393224 | tf_op jit(solution)/shard_map/ppermute | solution.py:466
  53.6 219.8 %collective-permute-start.93 = (bf16[4,256,256]{2,1,0:T(8,128)(2,1)}, bf16[4,256,256]{2,1,0:T(8,128)(2,1)}, u32[]{:S(2)}, u32[]{:S(2)}) collective-permute-start(bf16[4,256,256]{2,1,0:T(8,128)(2,1)} %get-tuple-element.117), channel_id=1, source_target_pairs={{0,4},{4,0},{8,12},{12,8},{16,20},{20,16},{24,28},{28,24},{1,5},{5... | collective-permute-start | bytes 1572872 | tf_op jit(solution)/shard_map/ppermute | solution.py:328
  56.2 23.4 %collective-permute-start.5 = (bf16[4,128,512]{2,1,0:T(8,128)(2,1)}, bf16[4,128,512]{2,1,0:T(8,128)(2,1)}, u32[]{:S(2)}, u32[]{:S(2)}) collective-permute-start(bf16[4,128,512]{2,1,0:T(8,128)(2,1)} %get-tuple-element.168), channel_id=1, source_target_pairs={{0,4},{4,0},{8,12},{12,8},{16,20},{20,16},{24,28},{28,24},{1,5},{5... | collective-permute-start | bytes 1572872 | tf_op jit(solution)/shard_map/ppermute | solution.py:328
  79.6 194.8 %collective-permute-start.92 = (bf16[4,256,256]{2,1,0:T(8,128)(2,1)}, bf16[4,256,256]{2,1,0:T(8,128)(2,1)}, u32[]{:S(2)}, u32[]{:S(2)}) collective-permute-start(bf16[4,256,256]{2,1,0:T(8,128)(2,1)} %get-tuple-element.116), channel_id=1, source_target_pairs={{0,4},{4,0},{8,12},{12,8},{16,20},{20,16},{24,28},{28,24},{1,5},{5... | collective-permute-start | bytes 1572872 | tf_op jit(solution)/shard_map/ppermute | solution.py:328
  140.9 26.3 %collective-permute-start.19 = (bf16[128,2048]{1,0:T(8,128)(2,1)S(1)}, bf16[128,2048]{1,0:T(8,128)(2,1)S(1)}, u32[]{:S(2)}, u32[]{:S(2)}) collective-permute-start(bf16[128,2048]{1,0:T(8,128)(2,1)S(1)} %pad_maximum_fusion.16), channel_id=1, source_target_pairs={{0,1},{1,0},{2,3},{3,2},{4,5},{5,4},{6,7},{7,6},{8,9},{9,8},{10,11... | collective-permute-start | bytes 1572872 | tf_op jit(solution)/shard_map/ppermute | solution.py:338
  225.2 50.2 %collective-permute-start.95 = (bf16[256,1408]{1,0:T(8,128)(2,1)}, bf16[256,1408]{1,0:T(8,128)(2,1)}, u32[]{:S(2)}, u32[]{:S(2)}) collective-permute-start(bf16[256,1408]{1,0:T(8,128)(2,1)} %get-tuple-element.76.refs_6_), channel_id=1, source_target_pairs={{0,4},{4,0},{8,12},{12,8},{16,20},{20,16},{24,28},{28,24},{1,5},{5... | collective-permute-start | bytes 2162696 | tf_op jit(solution)/shard_map/ppermute | solution.py:328
  271.7 25.2 %collective-permute-start.33 = (bf16[2,2,4,64,512]{4,3,0,2,1:T(8,128)(2,1)S(1)}, bf16[2,2,4,64,512]{4,3,0,2,1:T(8,128)(2,1)S(1)}, u32[]{:S(2)}, u32[]{:S(2)}) collective-permute-start(bf16[2,2,4,64,512]{4,3,0,2,1:T(8,128)(2,1)S(1)} %fusion.4), channel_id=1, source_target_pairs={{0,2},{1,3},{2,0},{3,1},{4,6},{5,7},{6,4},{7,5},{8,10},{9,11},{10,... | collective-permute-start | bytes 3145736 | tf_op jit(solution)/shard_map/ppermute | solution.py:576
  273.4 95.4 %collective-permute-start.86 = (bf16[256,2816]{1,0:T(8,128)(2,1)S(1)}, bf16[256,2816]{1,0:T(8,128)(2,1)S(1)}, u32[]{:S(2)}, u32[]{:S(2)}) collective-permute-start(bf16[256,2816]{1,0:T(8,128)(2,1)S(1)} %get-tuple-element.81.dgu.refs_6_), channel_id=1, source_target_pairs={{0,4},{4,0},{8,12},{12,8},{16,20},{20,16},{24,28},{28,24},{1,5},{5... | collective-permute-start | bytes 4325384 | tf_op jit(solution)/shard_map/ppermute | solution.py:328
  274.3 95.6 %collective-permute-start.85 = (bf16[256,2816]{1,0:T(8,128)(2,1)S(1)}, bf16[256,2816]{1,0:T(8,128)(2,1)S(1)}, u32[]{:S(2)}, u32[]{:S(2)}) collective-permute-start(bf16[256,2816]{1,0:T(8,128)(2,1)S(1)} %copy-done.4), channel_id=1, source_target_pairs={{0,4},{4,0},{8,12},{12,8},{16,20},{20,16},{24,28},{28,24},{1,5},{5... | collective-permute-start | bytes 4325384 | tf_op jit(solution)/shard_map/ppermute | solution.py:328
  284.5 73.0 %collective-permute-start.84 = (bf16[4,256,256]{2,1,0:T(8,128)(2,1)S(1)}, bf16[4,256,256]{2,1,0:T(8,128)(2,1)S(1)}, u32[]{:S(2)}, u32[]{:S(2)}) collective-permute-start(bf16[4,256,256]{2,1,0:T(8,128)(2,1)S(1)} %copy-done.166), channel_id=1, source_target_pairs={{0,4},{4,0},{8,12},{12,8},{16,20},{20,16},{24,28},{28,24},{1,5},{5... | collective-permute-start | bytes 1572872 | tf_op jit(solution)/shard_map/ppermute | solution.py:328
  288.3 80.4 %collective-permute-start.83 = (bf16[4,256,256]{2,1,0:T(8,128)(2,1)S(1)}, bf16[4,256,256]{2,1,0:T(8,128)(2,1)S(1)}, u32[]{:S(2)}, u32[]{:S(2)}) collective-permute-start(bf16[4,256,256]{2,1,0:T(8,128)(2,1)S(1)} %copy-done.168), channel_id=1, source_target_pairs={{0,4},{4,0},{8,12},{12,8},{16,20},{20,16},{24,28},{28,24},{1,5},{5... | collective-permute-start | bytes 1572872 | tf_op jit(solution)/shard_map/ppermute | solution.py:328
  296.9 74.8 %collective-permute-start.31 = (bf16[2,64,1024]{2,1,0:T(8,128)(2,1)S(1)}, bf16[2,64,1024]{2,1,0:T(8,128)(2,1)S(1)}, u32[]{:S(2)}, u32[]{:S(2)}) collective-permute-start(bf16[2,64,1024]{2,1,0:T(8,128)(2,1)S(1)} %slice.422), channel_id=1, source_target_pairs={{0,2},{1,3},{2,0},{3,1},{4,6},{5,7},{6,4},{7,5},{8,10},{9,11},{10,... | collective-permute-start | bytes 786440 | tf_op jit(solution)/shard_map/ppermute | solution.py:332
  357.5 72.5 %collective-permute-start.77 = (bf16[256,1024]{1,0:T(8,128)(2,1)S(1)}, bf16[256,1024]{1,0:T(8,128)(2,1)S(1)}, u32[]{:S(2)}, u32[]{:S(2)}) collective-permute-start(bf16[256,1024]{1,0:T(8,128)(2,1)S(1)} %copy-done.41), channel_id=1, source_target_pairs={{0,4},{4,0},{8,12},{12,8},{16,20},{20,16},{24,28},{28,24},{1,5},{5... | collective-permute-start | bytes 1572872 | tf_op jit(solution)/shard_map/ppermute | solution.py:328
  368.7 43.7 %collective-permute-start.22 = (bf16[2,128,2048]{2,1,0:T(8,128)(2,1)}, bf16[2,128,2048]{2,1,0:T(8,128)(2,1)}, u32[]{:S(2)}, u32[]{:S(2)}) collective-permute-start(bf16[2,128,2048]{2,1,0:T(8,128)(2,1)} %pad_maximum_fusion.5), channel_id=1, source_target_pairs={{0,1},{1,0},{2,3},{3,2},{4,5},{5,4},{6,7},{7,6},{8,9},{9,8},{10,11... | collective-permute-start | bytes 3145736 | tf_op jit(solution)/shard_map/ppermute | solution.py:331
  368.8 21.9 %collective-permute-start.34 = (bf16[2,4,64,512]{3,2,0,1:T(8,128)(2,1)S(1)}, bf16[2,4,64,512]{3,2,0,1:T(8,128)(2,1)S(1)}, u32[]{:S(2)}, u32[]{:S(2)}) collective-permute-start(bf16[2,4,64,512]{3,2,0,1:T(8,128)(2,1)S(1)} %fusion.17), channel_id=1, source_target_pairs={{0,4},{4,0},{8,12},{12,8},{16,20},{20,16},{24,28},{28,24},{1,5},{5... | collective-permute-start | bytes 1572872 | tf_op jit(solution)/shard_map/ppermute | solution.py:328
  399.4 29.1 %collective-permute-start.63 = (bf16[4,256,128]{2,1,0:T(8,128)(2,1)S(1)}, bf16[4,256,128]{2,1,0:T(8,128)(2,1)S(1)}, u32[]{:S(2)}, u32[]{:S(2)}) collective-permute-start(bf16[4,256,128]{2,1,0:T(8,128)(2,1)S(1)} %copy-done.172), channel_id=1, source_target_pairs={{0,4},{4,0},{8,12},{12,8},{16,20},{20,16},{24,28},{28,24},{1,5},{5... | collective-permute-start | bytes 786440 | tf_op jit(solution)/shard_map/ppermute | solution.py:328
  409.8 41.9 %collective-permute-start.87 = (bf16[256,2816]{1,0:T(8,128)(2,1)S(1)}, bf16[256,2816]{1,0:T(8,128)(2,1)S(1)}, u32[]{:S(2)}, u32[]{:S(2)}) collective-permute-start(bf16[256,2816]{1,0:T(8,128)(2,1)S(1)} %block.40), channel_id=1, source_target_pairs={{0,8},{4,12},{28,20},{24,16},{1,9},{5,13},{29,21},{25,17},{2,10},{... | collective-permute-start | bytes 4325384 | tf_op jit(solution)/shard_map/ppermute | solution.py:385
  430.9 21.7 %collective-permute-start.74 = (bf16[4,256,256]{2,1,0:T(8,128)(2,1)}, bf16[4,256,256]{2,1,0:T(8,128)(2,1)S(1)}, u32[]{:S(2)}, u32[]{:S(2)}) collective-permute-start(bf16[4,256,256]{2,1,0:T(8,128)(2,1)} %get-tuple-element.106), channel_id=1, source_target_pairs={{0,4},{4,0},{8,12},{12,8},{16,20},{20,16},{24,28},{28,24},{1,5},{5... | collective-permute-start | bytes 1572872 | tf_op jit(solution)/shard_map/ppermute | solution.py:328
  436.7 49.1 %collective-permute-start.39 = (bf16[2,128,1536]{2,1,0:T(8,128)(2,1)}, bf16[2,128,1536]{2,1,0:T(8,128)(2,1)}, u32[]{:S(2)}, u32[]{:S(2)}) collective-permute-start(bf16[2,128,1536]{2,1,0:T(8,128)(2,1)} %pad_maximum_fusion.12), channel_id=1, source_target_pairs={{0,1},{1,0},{2,3},{3,2},{4,5},{5,4},{6,7},{7,6},{8,9},{9,8},{10,11... | collective-permute-start | bytes 2359304 | tf_op jit(solution)/shard_map/ppermute | solution.py:338
  437.7 29.9 %collective-permute-start.62 = (bf16[4,256,128]{2,1,0:T(8,128)(2,1)S(1)}, bf16[4,256,128]{2,1,0:T(8,128)(2,1)S(1)}, u32[]{:S(2)}, u32[]{:S(2)}) collective-permute-start(bf16[4,256,128]{2,1,0:T(8,128)(2,1)S(1)} %copy-done.170), channel_id=1, source_target_pairs={{0,4},{4,0},{8,12},{12,8},{16,20},{20,16},{24,28},{28,24},{1,5},{5... | collective-permute-start | bytes 786440 | tf_op jit(solution)/shard_map/ppermute | solution.py:328
  438.7 22.7 %collective-permute-start.75 = (bf16[4,256,256]{2,1,0:T(8,128)(2,1)}, bf16[4,256,256]{2,1,0:T(8,128)(2,1)S(1)}, u32[]{:S(2)}, u32[]{:S(2)}) collective-permute-start(bf16[4,256,256]{2,1,0:T(8,128)(2,1)} %get-tuple-element.107), channel_id=1, source_target_pairs={{0,4},{4,0},{8,12},{12,8},{16,20},{20,16},{24,28},{28,24},{1,5},{5... | collective-permute-start | bytes 1572872 | tf_op jit(solution)/shard_map/ppermute | solution.py:328
  452.7 31.2 %collective-permute-start.64 = (bf16[256,1024]{1,0:T(8,128)(2,1)S(1)}, bf16[256,1024]{1,0:T(8,128)(2,1)S(1)}, u32[]{:S(2)}, u32[]{:S(2)}) collective-permute-start(bf16[256,1024]{1,0:T(8,128)(2,1)S(1)} %get-tuple-element.149.refs_5_), channel_id=1, source_target_pairs={{0,4},{4,0},{8,12},{12,8},{16,20},{20,16},{24,28},{28,24},{1,5},{5... | collective-permute-start | bytes 1572872 | tf_op jit(solution)/shard_map/ppermute | solution.py:328
  461.4 33.7 %collective-permute-start.53 = (bf16[4,256,256]{2,1,0:T(8,128)(2,1)}, bf16[4,256,256]{2,1,0:T(8,128)(2,1)S(1)}, u32[]{:S(2)}, u32[]{:S(2)}) collective-permute-start(bf16[4,256,256]{2,1,0:T(8,128)(2,1)} %get-tuple-element.97), channel_id=1, source_target_pairs={{0,4},{4,0},{8,12},{12,8},{16,20},{20,16},{24,28},{28,24},{1,5},{5... | collective-permute-start | bytes 1572872 | tf_op jit(solution)/shard_map/ppermute | solution.py:328
  467.9 36.2 %collective-permute-start.54 = (bf16[4,256,256]{2,1,0:T(8,128)(2,1)S(1)}, bf16[4,256,256]{2,1,0:T(8,128)(2,1)S(1)}, u32[]{:S(2)}, u32[]{:S(2)}) collective-permute-start(bf16[4,256,256]{2,1,0:T(8,128)(2,1)S(1)} %copy-done.164), channel_id=1, source_target_pairs={{0,4},{4,0},{8,12},{12,8},{16,20},{20,16},{24,28},{28,24},{1,5},{5... | collective-permute-start | bytes 1572872 | tf_op jit(solution)/shard_map/ppermute | solution.py:328
  472.6 40.2 %collective-permute-start.97 = (bf16[256,1408]{1,0:T(8,128)(2,1)S(1)}, bf16[256,1408]{1,0:T(8,128)(2,1)S(1)}, u32[]{:S(2)}, u32[]{:S(2)}) collective-permute-start(bf16[256,1408]{1,0:T(8,128)(2,1)S(1)} %copy-done.122), channel_id=1, source_target_pairs={{0,8},{4,12},{8,16},{12,20},{1,9},{5,13},{9,17},{13,21},{2,10},{6,... | collective-permute-start | bytes 2162696 | tf_op jit(solution)/shard_map/ppermute | solution.py:387
  483.9 27.7 %collective-permute-start.24 = (bf16[2,64,2048]{2,1,0:T(8,128)(2,1)S(1)}, bf16[2,64,2048]{2,1,0:T(8,128)(2,1)S(1)}, u32[]{:S(2)}, u32[]{:S(2)}) collective-permute-start(bf16[2,64,2048]{2,1,0:T(8,128)(2,1)S(1)} %copy-done.99), channel_id=1, source_target_pairs={{0,2},{1,3},{2,0},{3,1},{4,6},{5,7},{6,4},{7,5},{8,10},{9,11},{10,... | collective-permute-start | bytes 1572872 | tf_op jit(solution)/shard_map/ppermute | solution.py:336
  485.7 27.3 %collective-permute-start.100 = (bf16[256,1408]{1,0:T(8,128)(2,1)S(1)}, bf16[256,1408]{1,0:T(8,128)(2,1)S(1)}, u32[]{:S(2)}, u32[]{:S(2)}) collective-permute-start(bf16[256,1408]{1,0:T(8,128)(2,1)S(1)} %block.48), channel_id=1, source_target_pairs={{28,20},{24,16},{20,12},{16,8},{12,4},{8,0},{29,21},{25,17},{21,13... | collective-permute-start | bytes 2162696 | tf_op jit(solution)/shard_map/ppermute | solution.py:393
  495.1 94.9 %collective-permute-start.90 = (bf16[256,2816]{1,0:T(8,128)(2,1)}, bf16[256,2816]{1,0:T(8,128)(2,1)}, u32[]{:S(2)}, u32[]{:S(2)}) collective-permute-start(bf16[256,2816]{1,0:T(8,128)(2,1)} %block.41), channel_id=1, source_target_pairs={{28,20},{24,16},{20,12},{16,8},{29,21},{25,17},{21,13},{17,9},{30,... | collective-permute-start | bytes 4325384 | tf_op jit(solution)/shard_map/ppermute | solution.py:388
  504.1 27.9 %collective-permute-start.78 = (bf16[256,1024]{1,0:T(8,128)(2,1)S(1)}, bf16[256,1024]{1,0:T(8,128)(2,1)S(1)}, u32[]{:S(2)}, u32[]{:S(2)}) collective-permute-start(bf16[256,1024]{1,0:T(8,128)(2,1)S(1)} %block.35), channel_id=1, source_target_pairs={{0,8},{4,12},{28,20},{24,16},{1,9},{5,13},{29,21},{25,17},{2,10},{... | collective-permute-start | bytes 1572872 | tf_op jit(solution)/shard_map/ppermute | solution.py:385
  512.9 77.8 %collective-permute-start.40 = (bf16[2,128,2048]{2,1,0:T(8,128)(2,1)}, bf16[2,128,2048]{2,1,0:T(8,128)(2,1)}, u32[]{:S(2)}, u32[]{:S(2)}) collective-permute-start(bf16[2,128,2048]{2,1,0:T(8,128)(2,1)} %slice.418), channel_id=1, source_target_pairs={{0,1},{1,0},{2,3},{3,2},{4,5},{5,4},{6,7},{7,6},{8,9},{9,8},{10,11... | collective-permute-start | bytes 3145736 | tf_op jit(solution)/shard_map/ppermute | solution.py:331
  513.1 83.3 %collective-permute-start.88 = (bf16[256,2816]{1,0:T(8,128)(2,1)}, bf16[256,2816]{1,0:T(8,128)(2,1)}, u32[]{:S(2)}, u32[]{:S(2)}) collective-permute-start(bf16[256,2816]{1,0:T(8,128)(2,1)} %block.41), channel_id=1, source_target_pairs={{0,8},{4,12},{8,16},{12,20},{1,9},{5,13},{9,17},{13,21},{2,10},{6,... | collective-permute-start | bytes 4325384 | tf_op jit(solution)/shard_map/ppermute | solution.py:387
  554.6 87.3 %collective-permute-start.25 = (bf16[2,128,2048]{2,1,0:T(8,128)(2,1)}, bf16[2,128,2048]{2,1,0:T(8,128)(2,1)S(1)}, u32[]{:S(2)}, u32[]{:S(2)}) collective-permute-start(bf16[2,128,2048]{2,1,0:T(8,128)(2,1)} %pad_maximum_fusion.6), channel_id=1, source_target_pairs={{0,1},{1,0},{2,3},{3,2},{4,5},{5,4},{6,7},{7,6},{8,9},{9,8},{10,11... | collective-permute-start | bytes 3145736 | tf_op jit(solution)/shard_map/ppermute | solution.py:338
  560.4 73.3 %collective-permute-start.98 = (bf16[256,1408]{1,0:T(8,128)(2,1)}, bf16[256,1408]{1,0:T(8,128)(2,1)S(1)}, u32[]{:S(2)}, u32[]{:S(2)}) collective-permute-start(bf16[256,1408]{1,0:T(8,128)(2,1)} %block.47), channel_id=1, source_target_pairs={{0,8},{4,12},{8,16},{12,20},{16,24},{20,28},{1,9},{5,13},{9,17},{1... | collective-permute-start | bytes 2162696 | tf_op jit(solution)/shard_map/ppermute | solution.py:392
  590.7 27.1 %collective-permute-start.79 = (bf16[256,1024]{1,0:T(8,128)(2,1)S(1)}, bf16[256,1024]{1,0:T(8,128)(2,1)S(1)}, u32[]{:S(2)}, u32[]{:S(2)}) collective-permute-start(bf16[256,1024]{1,0:T(8,128)(2,1)S(1)} %block.36), channel_id=1, source_target_pairs={{0,8},{4,12},{8,16},{12,20},{1,9},{5,13},{9,17},{13,21},{2,10},{6,... | collective-permute-start | bytes 1572872 | tf_op jit(solution)/shard_map/ppermute | solution.py:387
  596.3 25.2 %collective-permute-start.57 = (bf16[256,384]{1,0:T(8,128)(2,1)S(1)}, bf16[256,384]{1,0:T(8,128)(2,1)S(1)}, u32[]{:S(2)}, u32[]{:S(2)}) collective-permute-start(bf16[256,384]{1,0:T(8,128)(2,1)S(1)} %block.25), channel_id=1, source_target_pairs={{0,8},{4,12},{28,20},{24,16},{1,9},{5,13},{29,21},{25,17},{2,10},{... | collective-permute-start | bytes 589832 | tf_op jit(solution)/shard_map/ppermute | solution.py:385
  601.3 34.0 %collective-permute-start.41 = (bf16[2,64,2048]{2,1,0:T(8,128)(2,1)}, bf16[2,64,2048]{2,1,0:T(8,128)(2,1)}, u32[]{:S(2)}, u32[]{:S(2)}) collective-permute-start(bf16[2,64,2048]{2,1,0:T(8,128)(2,1)} %slice.419), channel_id=1, source_target_pairs={{0,2},{1,3},{2,0},{3,1},{4,6},{5,7},{6,4},{7,5},{8,10},{9,11},{10,... | collective-permute-start | bytes 1572872 | tf_op jit(solution)/shard_map/ppermute | solution.py:332
  618.7 89.5 %collective-permute-start.91 = (bf16[256,2816]{1,0:T(8,128)(2,1)}, bf16[256,2816]{1,0:T(8,128)(2,1)}, u32[]{:S(2)}, u32[]{:S(2)}) collective-permute-start(bf16[256,2816]{1,0:T(8,128)(2,1)} %block.43), channel_id=1, source_target_pairs={{28,20},{24,16},{20,12},{16,8},{12,4},{8,0},{29,21},{25,17},{21,13... | collective-permute-start | bytes 4325384 | tf_op jit(solution)/shard_map/ppermute | solution.py:393
  621.5 86.7 %collective-permute-start.89 = (bf16[256,2816]{1,0:T(8,128)(2,1)}, bf16[256,2816]{1,0:T(8,128)(2,1)}, u32[]{:S(2)}, u32[]{:S(2)}) collective-permute-start(bf16[256,2816]{1,0:T(8,128)(2,1)} %block.42), channel_id=1, source_target_pairs={{0,8},{4,12},{8,16},{12,20},{16,24},{20,28},{1,9},{5,13},{9,17},{1... | collective-permute-start | bytes 4325384 | tf_op jit(solution)/shard_map/ppermute | solution.py:392
  633.7 26.0 %collective-permute-start.70 = (bf16[128,1024]{1,0:T(8,128)(2,1)S(1)}, bf16[128,1024]{1,0:T(8,128)(2,1)S(1)}, u32[]{:S(2)}, u32[]{:S(2)}) collective-permute-start(bf16[128,1024]{1,0:T(8,128)(2,1)S(1)} %block.33), channel_id=1, source_target_pairs={{28,20},{24,16},{20,12},{16,8},{12,4},{8,0},{29,21},{25,17},{21,13... | collective-permute-start | bytes 786440 | tf_op jit(solution)/shard_map/ppermute | solution.py:393
  635.3 27.0 %collective-permute-start.68 = (bf16[128,1024]{1,0:T(8,128)(2,1)S(1)}, bf16[128,1024]{1,0:T(8,128)(2,1)S(1)}, u32[]{:S(2)}, u32[]{:S(2)}) collective-permute-start(bf16[128,1024]{1,0:T(8,128)(2,1)S(1)} %block.32), channel_id=1, source_target_pairs={{0,8},{4,12},{8,16},{12,20},{16,24},{20,28},{1,9},{5,13},{9,17},{1... | collective-permute-start | bytes 786440 | tf_op jit(solution)/shard_map/ppermute | solution.py:392
  641.9 26.1 %collective-permute-start.60 = (bf16[256,384]{1,0:T(8,128)(2,1)S(1)}, bf16[256,384]{1,0:T(8,128)(2,1)S(1)}, u32[]{:S(2)}, u32[]{:S(2)}) collective-permute-start(bf16[256,384]{1,0:T(8,128)(2,1)S(1)} %block.26), channel_id=1, source_target_pairs={{28,20},{24,16},{20,12},{16,8},{29,21},{25,17},{21,13},{17,9},{30,... | collective-permute-start | bytes 589832 | tf_op jit(solution)/shard_map/ppermute | solution.py:388
  659.7 37.0 %collective-permute-start.82 = (bf16[256,1024]{1,0:T(8,128)(2,1)}, bf16[256,1024]{1,0:T(8,128)(2,1)}, u32[]{:S(2)}, u32[]{:S(2)}) collective-permute-start(bf16[256,1024]{1,0:T(8,128)(2,1)} %block.38), channel_id=1, source_target_pairs={{28,20},{24,16},{20,12},{16,8},{12,4},{8,0},{29,21},{25,17},{21,13... | collective-permute-start | bytes 1572872 | tf_op jit(solution)/shard_map/ppermute | solution.py:393
  662.2 36.0 %collective-permute-start.80 = (bf16[256,1024]{1,0:T(8,128)(2,1)}, bf16[256,1024]{1,0:T(8,128)(2,1)}, u32[]{:S(2)}, u32[]{:S(2)}) collective-permute-start(bf16[256,1024]{1,0:T(8,128)(2,1)} %block.37), channel_id=1, source_target_pairs={{0,8},{4,12},{8,16},{12,20},{16,24},{20,28},{1,9},{5,13},{9,17},{1... | collective-permute-start | bytes 1572872 | tf_op jit(solution)/shard_map/ppermute | solution.py:392
  681.7 32.4 %collective-permute-start.42 = (bf16[2,64,2048]{2,1,0:T(8,128)(2,1)}, bf16[2,64,2048]{2,1,0:T(8,128)(2,1)}, u32[]{:S(2)}, u32[]{:S(2)}) collective-permute-start(bf16[2,64,2048]{2,1,0:T(8,128)(2,1)} %add_convert_fusion.refs_1_), channel_id=1, source_target_pairs={{0,2},{1,3},{2,0},{3,1},{4,6},{5,7},{6,4},{7,5},{8,10},{9,11},{10,... | collective-permute-start | bytes 1572872 | tf_op jit(solution)/shard_map/ppermute | solution.py:336
  715.3 21.8 %collective-permute-start.43 = (bf16[2,128,2048]{2,1,0:T(8,128)(2,1)S(1)}, bf16[2,128,2048]{2,1,0:T(8,128)(2,1)S(1)}, u32[]{:S(2)}, u32[]{:S(2)}) collective-permute-start(bf16[2,128,2048]{2,1,0:T(8,128)(2,1)S(1)} %pad_maximum_fusion.11), channel_id=1, source_target_pairs={{0,1},{1,0},{2,3},{3,2},{4,5},{5,4},{6,7},{7,6},{8,9},{9,8},{10,11... | collective-permute-start | bytes 3145736 | tf_op jit(solution)/shard_map/ppermute | solution.py:338
  (293 other events, 6623.0 us)

commit v3 on v2

--- a/solution.py
+++ b/solution.py
@@ -1,3 +1,5 @@
+import functools
+
 import jax
 import jax.numpy as jnp
 from jax import lax
@@ -71,28 +73,34 @@
     return jax.ShapeDtypeStruct(shape, dtype)
 
 
-def run(body, ids, args, outs, flops, scratch=(), name=None, limit=40):
+def run(body, ids, args, outs, after=(), scratch=(), name=None, limit=40):
+    args, after = list(args), list(after)
+
+    def without(*refs):
+        body(*refs[: 1 + len(args)], *refs[1 + len(args) + len(after) :])
+
     return pl.pallas_call(
-        body,
+        without,
         grid_spec=pltpu.PrefetchScalarGridSpec(
             num_scalar_prefetch=1,
             grid=(1,),
-            in_specs=[in_vmem()] * len(args),
+            in_specs=[in_vmem()] * len(args) + [pl.BlockSpec(memory_space=pl.ANY)] * len(after),
             out_specs=[in_vmem()] * len(outs),
             scratch_shapes=list(scratch),
         ),
         out_shape=list(outs),
-        cost_estimate=pl.CostEstimate(flops=flops, bytes_accessed=1 << 20, transcendentals=0),
+        cost_estimate=pl.CostEstimate(flops=1000, bytes_accessed=1000, transcendentals=0),
         compiler_params=pltpu.CompilerParams(vmem_limit_bytes=limit << 20),
         name=name,
-    )(ids, *args)
+    )(ids, *args, *after)
 
 
 def side_columns(source, mine, theirs, side):
     line, _, wide = mine.shape
+    rows = theirs.shape[1]
     for z in range(line):
         mine[z] = source[:, pl.ds(pl.multiple_of((2 * z + side) * wide, wide), wide)]
-        theirs[z] = source[:, pl.ds(pl.multiple_of((2 * z + 1 - side) * wide, wide), wide)]
+        theirs[z] = source[:rows, pl.ds(pl.multiple_of((2 * z + 1 - side) * wide, wide), wide)]
 
 
 def first_body(m, quarter, ids, x_ref, gain, q_down, kv_proj, cos, sin, c, kv, h1, mine, theirs):
@@ -112,14 +120,16 @@
         side_columns(h1, mine, theirs, ids[1])
 
 
-def cotangent_body(m, quarter, ids, z_ref, w_down, dhid, dz, mine, theirs):
-    blocks = [
-        z_ref[m, pl.ds(pl.multiple_of((ids[0] ^ k) * quarter, quarter), quarter), :] for k in ORDER
-    ]
-    dz[...] = jnp.concatenate(blocks, 0)
-    if mine is not None:
-        side_columns(dz, mine, theirs, ids[1])
-    dhid[...] = inner_cols(dz[...], w_down[...])
+def cotangent_body(micro, quarter, ids, z_ref, w_down, dhid, dz, *sides):
+    for m in range(micro):
+        blocks = [
+            z_ref[m, pl.ds(pl.multiple_of((ids[0] ^ k) * quarter, quarter), quarter), :]
+            for k in ORDER
+        ]
+        dz[m] = jnp.concatenate(blocks, 0)
+        if sides:
+            side_columns(dz.at[m], sides[0].at[m], sides[1].at[m], ids[1])
+        dhid[m] = inner_cols(dz[m], w_down[...])
 
 
 def attend_body(
@@ -165,48 +175,59 @@
     keep[...] = dot(o[:half, :], out_proj[...])
 
 
-def forward_body(ids, a0, a1, a2, w_gate, w_up, dhid, h2, hid, dgu, mine, theirs):
+def forward_body(m, ids, a0, a1, a2, w_gate, w_up, dhid, h2, hid, dg, du, mine, theirs):
     h2[...] = jnp.concatenate([a0[...], a1[...], a2[...]], 0)
     if mine is not None:
         side_columns(h2, mine, theirs, ids[1])
     low = h2[...]
-    wide = hid.shape[1]
     g = dot(low, w_gate[...])
     u = dot(low, w_up[...])
     sig = jax.nn.sigmoid(g)
     swish = g * sig
     hid[...] = (swish * u).astype(LOW)
-    back = dhid[...]
-    dgu[:, :wide] = (back * u * sig * (1.0 + g * (1.0 - sig))).astype(LOW)
-    dgu[:, wide:] = (back * swish).astype(LOW)
-
-
-def hidden_back_body(ids, dgu, w_gate, w_up, send, keep):
-    wide = w_gate.shape[1]
-    half = dgu.shape[0] // 2
-    for rows, out in ((slice(half, None), send), (slice(0, half), keep)):
-        out[...] = (
-            inner_cols(dgu[rows, :wide], w_gate[...]) + inner_cols(dgu[rows, wide:], w_up[...])
-        ).astype(out.dtype)
-
-
-def block_body(count, extra, final, ids, *refs):
-    lefts, rights = refs[:count], refs[count : 2 * count]
-    added, outs = refs[2 * count : 2 * count + extra], refs[2 * count + extra :]
+    back = dhid[m]
+    dg[...] = (back * u * sig * (1.0 + g * (1.0 - sig))).astype(LOW)
+    du[...] = (back * swish).astype(LOW)
+
+
+def hidden_back_body(micro, ids, *refs):
+    dgs, dus = refs[:micro], refs[micro : 2 * micro]
+    w_gate, w_up, send, keep = refs[2 * micro :]
+    half = send.shape[1]
+    for m in range(micro):
+        for rows, out in ((slice(half, None), send), (slice(0, half), keep)):
+            out[m] = (
+                inner_cols(dgs[m][rows, :], w_gate[...]) + inner_cols(dus[m][rows, :], w_up[...])
+            ).astype(out.dtype)
+
+
+def pick(ref, lead):
+    return ref if lead is None else ref.at[lead]
+
+
+def block_body(terms, lefts, rights, extra, from_side, turned, ids, *refs):
+    left, refs = refs[:lefts], refs[lefts:]
+    right, refs = refs[:rights], refs[rights:]
+    added, out = refs[: extra + from_side], refs[-1]
     total = None
-    for a, b in zip(lefts, rights):
-        term = inner_rows(a[ids[0]], b[...])
+    for a, a_lead, b, b_lead, first, count in terms:
+        rows = pick(right[b], b_lead)[first : first + count, :]
+        term = inner_rows(pick(left[a], a_lead)[ids[0]], rows)
         total = term if total is None else total + term
-    for ref in added:
-        total = total + ref[...].astype(F32)
-    if final == "turned":
-        outs[0][...] = jnp.transpose(total)
-    elif final == "split":
-        wide = outs[0].shape[1]
-        outs[0][...] = total[:, :wide]
-        outs[1][...] = total[:, wide:]
-    else:
-        outs[0][...] = total.astype(outs[0].dtype)
+    for i, ref in enumerate(added):
+        total = total + (ref[ids[0]] if i >= extra else ref[...]).astype(F32)
+    out[...] = jnp.transpose(total) if turned else total.astype(out.dtype)
+
+
+def side_sum_body(terms, lefts, ids, *refs):
+    left, right, out = refs[:lefts], refs[lefts:-1], refs[-1]
+    for z in range(out.shape[0]):
+        total = None
+        for a, a_lead, b, b_lead, first, count in terms:
+            rows = pick(right[b], b_lead)[first : first + count, :]
+            term = inner_rows(pick(left[a], a_lead)[z], rows)
+            total = term if total is None else total + term
+        out[z] = total.astype(out.dtype)
 
 
 def attend_back_body(
@@ -224,7 +245,7 @@
         dyl = jnp.concatenate([a0[m], a1[m], a2[m]], 0)
         dyl_out[m] = dyl
         if sides:
-            side_columns(dyl_out.at[m], sides[2 * m], sides[2 * m + 1], ids[1])
+            side_columns(dyl_out.at[m], sides[0].at[m], sides[1].at[m], ids[1])
         for h in range(heads):
             do = inner_cols(dyl, out_proj[h * wide : (h + 1) * wide, :]).astype(LOW)
             do_acc[h] = do
@@ -337,42 +358,67 @@
         pair = jnp.concatenate([piece, near], -2)
         return piece, near, lax.ppermute(pair, "mp", CORE)
 
-    def sides_shape(columns):
+    def sides_shape(columns, their_rows, lead=()):
         if columns // seq % 128:
             return []
-        return [whole((line, rows, columns // seq), LOW)] * 2
-
-    def sides(made, full):
+        return [
+            whole((*lead, line, n, columns // seq), LOW) for n in (rows, their_rows)
+        ]
+
+    def split_sides(made, full, their_rows):
         if made:
-            mine, theirs = made
-        else:
-            split = full.reshape(rows, line, 2, full.shape[1] // seq)
-            mine = jnp.swapaxes(lax.dynamic_index_in_dim(split, side, 2, keepdims=False), 0, 1)
-            theirs = jnp.swapaxes(
-                lax.dynamic_index_in_dim(split, 1 - side, 2, keepdims=False), 0, 1
-            )
-        return mine, other(theirs)
+            return made
+        split = full.reshape(*full.shape[:-1], line, 2, full.shape[-1] // seq)
+        mine, theirs = (
+            jnp.moveaxis(lax.dynamic_index_in_dim(split, i, split.ndim - 2, keepdims=False), -2, -3)
+            for i in (side, 1 - side)
+        )
+        return mine, theirs[..., :their_rows, :]
+
+    def from_other(theirs):
+        got = other(theirs)
+        return got, lax.ppermute(got, "mp", CORE)
 
     def without_sides(body, count):
         return body if count else lambda *refs: body(*refs, None, None)
 
-    def reduce_line(lefts, rights, final):
-        w, columns = lefts[0].shape[2], rights[0].shape[1]
-        flops = 2 * w * columns * rows * len(lefts)
-
-        def block(index, added, outs, kind):
+    def both_sides(mine, got):
+        lefts, spans = [], []
+        for array, first, count, partner in (
+            (mine, 0, rows, 0), (got[0], 0, half, 1), (got[1], half, half, 1)
+        ):
+            stacked_array = not isinstance(array, list)
+            for m in range(micro):
+                spans.append((len(lefts) if not stacked_array else len(lefts), m if stacked_array else None,
+                              m, partner, first, count))
+                if not stacked_array:
+                    lefts.append(array[m])
+            if stacked_array:
+                lefts.append(array)
+        return lefts, spans
+
+    class Chain:
+        def __init__(self, lefts, rights, terms, shape, turned=False, from_side=None):
+            self.args = [*lefts, *rights]
+            self.spec = (terms, len(lefts), len(rights))
+            self.shape, self.turned = shape, turned
+            self.from_side = [] if from_side is None else [from_side]
+            self.step, self.up, self.down = 0, None, None
+
+        def block(self, index, added, after, last=False):
+            turned = last and self.turned
+            body = functools.partial(
+                block_body, *self.spec, len(added), len(self.from_side), turned
+            )
+            shape = self.shape[::-1] if turned else self.shape
             return run(
-                lambda *refs: block_body(len(lefts), len(added), kind, *refs),
-                index.reshape(1),
-                [*lefts, *rights, *added],
-                outs,
-                flops,
-                name="block",
-            )
-
-        low = [whole((w, columns), LOW)]
-        up = down = None
-        for step in range(1, line):
+                body, index.reshape(1), [*self.args, *added, *self.from_side],
+                [whole(shape, F32 if last else LOW)], after, name="block",
+            )[0]
+
+        def advance(self, after):
+            self.step += 1
+            step = self.step
             goes_up = [(i, i + 2) for i in range(2 * step)]
             goes_down = [(seq - 1 - i, seq - 3 - i) for i in range(2 * step)]
             for_up, for_down = line - step + place, step - line + place
@@ -380,30 +426,24 @@
                 which = jnp.where(
                     place <= step - 1, for_up, jnp.where(place >= line - step, for_down, 0)
                 )
-                (term,) = block(which, [a for a in (up, down) if a is not None], low, None)
+                term = self.block(which, [a for a in (self.up, self.down) if a is not None], after)
                 if step == 1 and line > 3:
-                    up = lax.ppermute(term, "seq", goes_up + goes_down)
+                    self.up = lax.ppermute(term, "seq", goes_up + goes_down)
                 else:
-                    up = lax.ppermute(term, "seq", goes_up)
-                    down = lax.ppermute(term, "seq", goes_down)
-            else:
-                (term_up,) = block(jnp.clip(for_up, 0, line - 1), [up], low, None)
-                (term_down,) = block(jnp.clip(for_down, 0, line - 1), [down], low, None)
-                up = lax.ppermute(term_up, "seq", goes_up)
-                down = lax.ppermute(term_down, "seq", goes_down)
-        if final == "turned":
-            outs = [whole((columns, w), F32)]
-        elif final == "split":
-            outs = [whole((w, columns // 2), F32)] * 2
-        else:
-            outs = [whole((w, columns), F32)]
-        return block(place, [up, down], outs, final)
-
-    def with_other(arrays):
-        return list(arrays) + [other(a) for a in arrays]
-
-    def two_sides(pairs):
-        return [p[0] for p in pairs] + [p[1] for p in pairs]
+                    self.up = lax.ppermute(term, "seq", goes_up)
+                    self.down = lax.ppermute(term, "seq", goes_down)
+                return [term]
+            term_up = self.block(jnp.clip(for_up, 0, line - 1), [self.up], after)
+            term_down = self.block(jnp.clip(for_down, 0, line - 1), [self.down], [term_up])
+            self.up = lax.ppermute(term_up, "seq", goes_up)
+            self.down = lax.ppermute(term_down, "seq", goes_down)
+            return [term_down]
+
+        def finish(self, after):
+            while self.step < line - 1:
+                after = self.advance(after)
+            result = self.block(place, [self.up, self.down], after, last=True)
+            return result, [result]
 
     quarter_rows = jnp.arange(quarter, dtype=jnp.int32)
     row_ids = at * rows + jnp.concatenate([(me ^ k) * quarter + quarter_rows for k in ORDER])
@@ -418,23 +458,26 @@
     gain1_row, gain2_row, gain_c_row = norm1_gain[None, :], norm2_gain[None, :], latent_gain[None, :]
     kv_cols = lax.dynamic_slice_in_dim(kv_proj, me * kv_part, kv_part, 1)
     first_weights = jnp.concatenate([q_down, kv_cols], axis=1)
-    width_sides = sides_shape(width)
-    rank_sides = sides_shape(rank)
-
-    tables, starts, kv, c_part, h1_pairs = [], [], [], [], []
+    both_rows = sides_shape(width, rows)
+    half_rows = sides_shape(width, half)
+    rank_sides = sides_shape(rank, rows)
+
+    tables, starts, kv, c_part, h1_sides = [], [], [], [], []
+    order = []
     for m in range(micro):
         _, places = documents(lengths[m], row_ids)
         starts.append(row_ids - places)
         tables.append(rotation(places, head_dim))
         c, packed, h1, *made = run(
-            without_sides(lambda *refs: first_body(m, quarter, *refs), len(width_sides)),
+            without_sides(functools.partial(first_body, m, quarter), len(both_rows)),
             ids,
             [tokens, gain1_row, q_down, kv_proj, *tables[m]],
             [whole((rows, part), LOW), whole((half, 2 * head_dim), LOW), whole((rows, width), LOW),
-             *width_sides],
-            2 * width * (rows * part + half * 2 * head_dim),
+             *both_rows],
+            order,
             name="first",
         )
+        order = [c]
         blocks = [packed] + [
             lax.ppermute(packed, "seq", [(i, i + 2 * d) for i in range(seq - 2 * d)])
             for d in range(1, line)
@@ -445,89 +488,108 @@
             jnp.stack([near, lax.ppermute(near, "mp", CORE)], 0).reshape(key_count, 2 * head_dim)
         )
         c_part.append(c)
-        h1_pairs.append(sides(made, h1))
-
-    dhid, dz_pairs, dz_rows = [], [], []
-    for m in range(micro):
-        back, dz, *made = run(
-            without_sides(lambda *refs: cotangent_body(m, quarter, *refs), len(width_sides)),
-            ids,
-            [cotangent, w_down],
-            [whole((rows, hidden), F32), whole((rows, width), LOW), *width_sides],
-            2 * rows * width * hidden,
-            name="cotangent",
-        )
-        dhid.append(back)
-        dz_rows.append(dz)
-        dz_pairs.append(sides(made, dz))
-
-    qn_pairs, h2_pairs, hid, dgu, qs, os, lses, state = [], [], [], [], [], [], [], []
+        h1_sides.append(split_sides(made, h1, rows))
+
+    dhid, dz, *made = run(
+        functools.partial(cotangent_body, micro, quarter),
+        ids,
+        [cotangent, w_down],
+        [whole((micro, rows, hidden), F32), whole((micro, rows, width), LOW),
+         *sides_shape(width, half, (micro,))],
+        order,
+        name="cotangent",
+    )
+    order = [dz]
+    dz_mine, dz_theirs = split_sides(made, dz, half)
+    dz_got = from_other(dz_theirs)
+
+    qn_sides, qs, os, lses, sums, c_rows = [], [], [], [], [], []
     for m in range(micro):
         near = lax.ppermute(c_part[m], "mp", CROSS)
         swapped = jnp.concatenate(
-            [near[quarter : 2 * quarter], near[:quarter], near[3 * quarter :], near[2 * quarter : 3 * quarter]], 0
+            [near[quarter : 2 * quarter], near[:quarter], near[3 * quarter :],
+             near[2 * quarter : 3 * quarter]], 0
         )
         far = lax.ppermute(jnp.concatenate([c_part[m], swapped], 1), "mp", CORE)
         qn, q, o, lse, send, keep, *made = run(
-            without_sides(lambda *refs: attend_body(scale, *refs), len(rank_sides)),
+            without_sides(functools.partial(attend_body, scale), len(rank_sides)),
             ids,
             [c_part[m], near, far, gain_c_row, q_up, *tables[m], kv[m], key_ids[None, :],
              row_ids[:, None], starts[m][:, None], out_proj],
             [whole((rows, rank), LOW), whole((heads, rows, head_dim), LOW),
              whole((rows, heads * head_dim), LOW), whole((heads, rows), F32),
              whole((half, width), LOW), whole((half, width), F32), *rank_sides],
-            2 * rows * heads * head_dim * (rank + 2 * key_count + width),
+            order,
             name="attend",
         )
-        qn_pairs.append(sides(made, qn))
+        order = [o]
+        qn_sides.append(split_sides(made, qn, rows))
+        qs.append(q)
+        os.append(o)
+        lses.append(lse)
+        sums.append(sum_mp(send, keep))
+        c_rows.append(
+            jnp.concatenate([c_part[m][:quarter], swapped[:quarter], far[half : half + quarter]], 1)
+        )
+
+    h2_mine, h2_got, hid, dg, du, state = [], [], [], [], [], []
+    for m in range(micro):
         x = lax.dynamic_slice_in_dim(tokens[m], me * quarter, quarter, 0).astype(F32)
         inv1 = inverse_rms(x)
-        y = x + sum_mp(send, keep)
+        y = x + sums[m]
         inv2 = inverse_rms(y)
         n2 = y * inv2
         pieces = gather_mp((n2 * gain2_row).astype(LOW))
-        h2, hid_m, dgu_m, *made = run(
-            without_sides(forward_body, len(width_sides)),
+        h2, hid_m, dg_m, du_m, *made = run(
+            without_sides(functools.partial(forward_body, m), len(half_rows)),
             ids,
-            [*pieces, w_gate, w_up, dhid[m]],
-            [whole((rows, width), LOW), whole((rows, hidden), LOW), whole((rows, 2 * hidden), LOW),
-             *width_sides],
-            4 * rows * width * hidden,
+            [*pieces, w_gate, w_up, dhid],
+            [whole((rows, width), LOW), *[whole((rows, hidden), LOW)] * 3, *half_rows],
+            order,
             name="forward",
         )
-        h2_pairs.append(sides(made, h2))
+        order = [hid_m]
+        mine, theirs = split_sides(made, h2, half)
+        h2_mine.append(mine)
+        h2_got.append(from_other(theirs))
         hid.append(hid_m)
-        dgu.append(dgu_m)
-        qs.append(q)
-        os.append(o)
-        lses.append(lse)
-        c_rows = jnp.concatenate(
-            [c_part[m][:quarter], swapped[:quarter], far[half : half + quarter]], 1
-        )
-        state.append(dict(x=x, n1=x * inv1, inv1=inv1, y=y, n2=n2, inv2=inv2, c=c_rows))
-
-    (grad_down,) = reduce_line(two_sides(dz_pairs), with_other(hid), "turned")
-    grad_gate, grad_up = reduce_line(two_sides(h2_pairs), with_other(dgu), "split")
+        dg.append(dg_m)
+        du.append(du_m)
+        state.append(dict(x=x, n1=x * inv1, inv1=inv1, y=y, n2=n2, inv2=inv2, c=c_rows[m]))
 
     def stacked(name):
         return jnp.stack([st[name] for st in state], 0)
 
-    back = [
-        run(
-            hidden_back_body,
-            ids,
-            [dgu[m], w_gate, w_up],
-            [whole((half, width), LOW), whole((half, width), F32)],
-            4 * rows * width * hidden,
-            name="hidden_back",
-        )
-        for m in range(micro)
-    ]
-    dh2 = sum_mp(jnp.stack([b[0] for b in back], 0), jnp.stack([b[1] for b in back], 0))
+    def with_other(arrays):
+        return [*arrays, *[other(a) for a in arrays]]
+
+    def terms_of(spans):
+        return [(a, lead, m + micro * partner, None, first, count)
+                for a, lead, m, partner, first, count in spans]
+
+    lefts, spans = both_sides(dz_mine, dz_got)
+    chain_down = Chain(lefts, with_other(hid), terms_of(spans), (wide, hidden), turned=True)
+    lefts, spans = both_sides(h2_mine, [list(p) for p in zip(*h2_got)])
+    chain_gate = Chain(lefts, with_other(dg), terms_of(spans), (wide, hidden))
+    chain_up = Chain(lefts, with_other(du), terms_of(spans), (wide, hidden))
+
+    send, keep = run(
+        functools.partial(hidden_back_body, micro),
+        ids,
+        [*dg, *du, w_gate, w_up],
+        [whole((micro, half, width), LOW), whole((micro, half, width), F32)],
+        order,
+        name="hidden_back",
+    )
+    order = chain_down.advance([send])
+    dh2 = sum_mp(send, keep)
     y, n2, inv2, n1, inv1 = (stacked(k) for k in ("y", "n2", "inv2", "n1", "inv1"))
-    dz_own = jnp.stack([dz[:quarter] for dz in dz_rows], 0).astype(F32)
+    dz_own = dz[:, :quarter].astype(F32)
     gain2 = jnp.sum(dh2 * n2, axis=(0, 1))
     dy = dz_own + norm_backward(dh2 * gain2_row, n2, inv2)
+    for _ in range(2):
+        order = chain_down.advance(order)
+    order = chain_gate.advance(order)
 
     def attend_back(which, pieces):
         args = [*pieces, out_proj, q_up, key_ids[:, None]]
@@ -535,14 +597,14 @@
             args += [qs[m], kv[m], os[m], lses[m], jnp.stack([row_ids, starts[m]], 0), *tables[m]]
         n = len(which)
         return run(
-            lambda *refs: attend_back_body(scale, n, min(1024, key_count // 2), *refs),
+            functools.partial(attend_back_body, scale, n, min(1024, key_count // 2)),
             ids,
             args,
             [whole((n, rows, width), LOW), whole((n, rows, heads * head_dim), LOW),
              whole((n, half, rank), LOW), whole((n, half, rank), F32),
              whole((n, key_count // 2, 2 * head_dim), LOW),
-             whole((n, key_count // 2, 2 * head_dim), F32), *(width_sides * n)],
-            2 * n * rows * heads * head_dim * (5 * key_count + width + rank),
+             whole((n, key_count // 2, 2 * head_dim), F32), *sides_shape(width, half, (n,))],
+            order,
             scratch=[pltpu.VMEM((heads, rows, head_dim), F32),
                      pltpu.VMEM((heads, rows, head_dim), LOW),
                      pltpu.VMEM((heads, 8, rows), F32)],
@@ -552,16 +614,37 @@
 
     pieces = gather_mp(dy.astype(LOW))
     if key_count <= 2048:
-        dyl, dqp, send, keep, kv_send, kv_keep, *made = attend_back(range(micro), pieces)
+        made = attend_back(range(micro), pieces)
     else:
         each = [attend_back([m], [p[m : m + 1] for p in pieces]) for m in range(micro)]
-        dyl, dqp, send, keep, kv_send, kv_keep = (
-            jnp.concatenate([e[i] for e in each], 0) for i in range(6)
-        )
-        made = [a for e in each for a in e[6:]]
-    dyl_pairs = [sides(made[2 * m : 2 * m + 2], dyl[m]) for m in range(micro)]
-    (grad_out,) = reduce_line(two_sides(dyl_pairs), with_other(os), "turned")
-    (grad_qup,) = reduce_line(two_sides(qn_pairs), with_other([dqp[m] for m in range(micro)]), None)
+        made = [jnp.concatenate(parts, 0) for parts in zip(*each)]
+    dyl, dqp, send, keep, kv_send, kv_keep, *made = made
+    order = [send]
+    dyl_mine, dyl_theirs = split_sides(made, dyl, half)
+    lefts, spans = both_sides(dyl_mine, from_other(dyl_theirs))
+    chain_out = Chain(lefts, with_other(os), terms_of(spans), (wide, heads * head_dim), turned=True)
+
+    def side_sum(lefts, rights, shape, after):
+        terms = [(m, None, 0, m, 0, rows) for m in range(micro)]
+        (made,) = run(
+            functools.partial(side_sum_body, terms, len(lefts)),
+            ids,
+            [*lefts, *rights],
+            [whole((line, *shape), LOW)],
+            after,
+            name="side_sum",
+        )
+        return other(made), [made]
+
+    def own_chain(side_pairs, right, shape, after):
+        from_side, after = side_sum([p[1] for p in side_pairs], [right], shape, after)
+        terms = [(m, None, 0, m, 0, rows) for m in range(micro)]
+        return Chain([p[0] for p in side_pairs], [right], terms, shape, from_side=from_side), after
+
+    shape = (rank // seq, heads * head_dim)
+    chain_qup, order = own_chain(qn_sides, dqp, shape, order)
+    order = chain_gate.advance(order)
+    order = chain_up.advance(order)
 
     dqn = sum_mp(send, keep)
     c = stacked("c").astype(F32)
@@ -590,8 +673,27 @@
         [lax.dynamic_slice_in_dim(both, me * part, part, 2),
          lax.dynamic_slice_in_dim(both, rank + me * kv_part, kv_part, 2)], -1
     )
-    dfirst_list = [dfirst[m] for m in range(micro)]
-    (grad_first,) = reduce_line(two_sides(h1_pairs), with_other(dfirst_list), None)
+
+    grad_down, order = chain_down.finish(order)
+    order = chain_gate.advance(order)
+    order = chain_up.advance(order)
+    order = chain_out.advance(order)
+    grad_gate, order = chain_gate.finish(order)
+    order = chain_up.advance(order)
+    order = chain_out.advance(order)
+    grad_up, order = chain_up.finish(order)
+    order = chain_qup.advance(order)
+    order = chain_out.advance(order)
+    chain_first, order = own_chain(h1_sides, dfirst, (wide, part + kv_part), order)
+    order = chain_qup.advance(order)
+    grad_out, order = chain_out.finish(order)
+    order = chain_first.advance(order)
+    order = chain_qup.advance(order)
+    order = chain_first.advance(order)
+    grad_qup, order = chain_qup.finish(order)
+    order = chain_first.advance(order)
+    grad_first, order = chain_first.finish(order)
+
     grad_qdown = grad_first[:, :part]
     kv_cols_grad = grad_first[:, part:]
     pieces = []
@@ -603,11 +705,10 @@
 
     def put_natural(pieces):
         return run(
-            lambda *refs: natural_body(micro, quarter, *refs),
+            functools.partial(natural_body, micro, quarter),
             ids,
             pieces,
             [whole((micro, rows, width), LOW)],
-            0,
             name="natural",
         )[0]
 

time: 748 us -> 613 us (0.82)
  waiting for transfers between devices: 257 us -> 154 us
  starting transfers between devices: 191 us -> 161 us
  Pallas kernels: 149 us -> 161 us
  local copies, waits for them, and re-layouts: 78.9 us -> 66.9 us
    ppermute x23 -> x17, waiting for transfers between devices: 138 us -> 54.9 us  [other(): return lax.ppermute(array, 'seq', beside)]
    ppermute x25 -> x34, starting transfers between devices: 115 us -> 86.5 us  [the longest x6 26.8 us: advance(): self.up = lax.ppermute(term_up, 'seq', goes_up)]
    ppermute x6, waiting for transfers between devices: 21.9 us -> 6.91 us  [sum_mp(): got = lax.ppermute(kept[..., quarter:, :].astype(LOW), 'mp', CROSS)]
    pallas_call x38 -> x43, Pallas kernels: 149 us -> 161 us  [run(): pl.pallas_call(without, grid_spec=pltpu.PrefetchScalarGridSpec(num_scalar...]
    unnamed x476 -> x292, local copies, waits for them, and re-layouts: 53.2 us -> 44.4 us
    ppermute x23 -> x17, starting transfers between devices: 24.2 us -> 16.9 us  [other(): return lax.ppermute(array, 'seq', beside)]
    ppermute x25 -> x34, waiting for transfers between devices: 61.7 us -> 61.4 us  [the longest x6 23.9 us: advance(): self.up = lax.ppermute(term, 'seq', goes_up)]
  transfers between devices with their start and end apart: 101 -> 104, of which waited for: 36 -> 31; matrix products, arithmetic and copies ran while one was open for 11% -> 12% of each run, Pallas kernels for 19% -> 15%
where the time goes in v3:
time: 613 us; the launch traced here: 606 us
  Pallas kernels  161 us (26%)
  starting transfers between devices  161 us (26%)
  waiting for transfers between devices  154 us (25%)
  local copies, waits for them, and re-layouts  66.9 us (11%)
  other arithmetic  49.1 us (8%)
  matrix products  7.73 us (1%)
  between operations  6.31 us (1%)
    pallas_call x43, Pallas kernels, run(): pl.pallas_call(without, grid_spec=pltpu.PrefetchScalarGridSpec(num_scalar...  161 us
    ppermute x17, waiting for transfers between devices, other(): return lax.ppermute(array, 'seq', beside)  54.9 us
    unnamed x292, local copies, waits for them, and re-layouts  44.4 us
    ppermute x6, starting transfers between devices, advance(): self.up = lax.ppermute(term_up, 'seq', goes_up)  26.8 us
    ppermute x6, waiting for transfers between devices, advance(): self.up = lax.ppermute(term, 'seq', goes_up)  23.9 us
    ppermute x6, starting transfers between devices, advance(): self.up = lax.ppermute(term, 'seq', goes_up + goes_down)  23.4 us
    ppermute x6, starting transfers between devices, advance(): self.up = lax.ppermute(term, 'seq', goes_up)  22.9 us
    ppermute x17, starting transfers between devices, other(): return lax.ppermute(array, 'seq', beside)  16.9 us
  transfers between devices with their start and end apart: 104, of which 31 were waited for; matrix products, arithmetic and copies ran while one was open for 12% of the time, Pallas kernels for 15%

profile of v3, /device:TPU:0, one launch (start us, length us, event | category | flops | bytes accessed | tf_op | source)
XLA Modules:
  0.0 606.1 jit_solution(6322422053083366409)
XLA Ops:
  16.8 7.0 %collective-permute-start.4 = (bf16[128,512]{1,0:T(8,128)(2,1)S(1)}, bf16[128,512]{1,0:T(8,128)(2,1)S(1)}, u32[]{:S(2)}, u32[]{:S(2)}) collective-permute-start(bf16[128,512]{1,0:T(8,128)(2,1)S(1)} %get-tuple-element.58), channel_id=1, source_target_pairs={{0,24},{4,28},{1,25},{5,29},{2,26},{6,30},{3,27},{7,31}} | collective-permute-start | bytes 393224 | tf_op jit(solution)/shard_map/ppermute | solution.py:482
  49.4 4.2 cotangent.1
  59.0 6.7 %collective-permute-done.14 = bf16[4,128,512]{2,1,0:T(8,128)(2,1)} collective-permute-done((bf16[4,128,512]{2,1,0:T(8,128)(2,1)}, bf16[4,128,512]{2,1,0:T(8,128)(2,1)}, u32[]{:S(2)}, u32[]{:S(2)}) %collective-permute-start.14) | collective-permute-done | bytes 524320 | tf_op jit(solution)/shard_map/ppermute | solution.py:349
  71.6 9.5 %attend.2 = (bf16[256,1024]{1,0:T(8,128)(2,1)}, bf16[4,256,256]{2,1,0:T(8,128)(2,1)S(1)}, bf16[256,1024]{1,0:T(8,128)(2,1)S(1)}, f32[4,256]{1,0:T(4,128)S(1)}, b...) custom-call(s32[2]{0:T(128)S(1)} %pad_add_fusion.3.refs_0_, ...), custom_call_target="tpu_custom_call" | custom-call | flops 1000 | bytes 1000 | tf_op jit(solution)/shard_map/attend/pallas_call | solution.py:82
  86.4 7.8 %attend.3 = (bf16[256,1024]{1,0:T(8,128)(2,1)}, bf16[4,256,256]{2,1,0:T(8,128)(2,1)S(1)}, bf16[256,1024]{1,0:T(8,128)(2,1)S(1)}, f32[4,256]{1,0:T(4,128)S(1)}, b...) custom-call(s32[2]{0:T(128)S(1)} %pad_add_fusion.3.refs_0_, ...), custom_call_target="tpu_custom_call" | custom-call | flops 1000 | bytes 1000 | tf_op jit(solution)/shard_map/attend/pallas_call | solution.py:82
  104.5 5.6 collective-permute-done.8
  121.7 4.6 collective-permute-done.20.refs_2_
  126.5 8.1 %forward.2 = (bf16[256,2048]{1,0:T(8,128)(2,1)}, bf16[256,1408]{1,0:T(8,128)(2,1)S(1)}, bf16[256,1408]{1,0:T(8,128)(2,1)}, bf16[256,1408]{1,0:T(8,128)(2,1)S(1)}...) custom-call(s32[2]{0:T(128)S(1)} %pad_add_fusion.3.refs_0_, ...), custom_call_target="tpu_custom_call" | custom-call | flops 1000 | bytes 1000 | tf_op jit(solution)/shard_map/forward/pallas_call | solution.py:82
  134.6 8.3 %forward.3 = (bf16[256,2048]{1,0:T(8,128)(2,1)}, bf16[256,1408]{1,0:T(8,128)(2,1)}, bf16[256,1408]{1,0:T(8,128)(2,1)}, bf16[256,1408]{1,0:T(8,128)(2,1)S(1)}, bf...) custom-call(s32[2]{0:T(128)S(1)} %pad_add_fusion.3.refs_0_, ...), custom_call_target="tpu_custom_call" | custom-call | flops 1000 | bytes 1000 | tf_op jit(solution)/shard_map/forward/pallas_call | solution.py:82
  142.9 18.3 %hidden_back.1 = (bf16[2,128,2048]{2,1,0:T(8,128)(2,1)S(1)}, f32[2,128,2048]{2,1,0:T(8,128)S(1)}) custom-call(s32[2]{0:T(128)S(1)} %pad_add_fusion.3.refs_0_, bf16[256,1408]{1,0:T(8,128)(2,1)} %get-tuple-element.71.refs_1_.refs_7_, bf16[256,1408]{1,0:T(8,128)(2,1)} %get-tuple-element.72.refs_2_.refs_8_, ...), custom_call_target="tpu_custom_call" | custom-call | flops 1000 | bytes 1000 | tf_op jit(solution)/shard_map/hidden_back/pallas_call | solution.py:82
  163.3 12.5 %collective-permute-done.36.refs_2_ = bf16[2,4,128,256]{3,2,1,0:T(8,128)(2,1)} collective-permute-done((bf16[2,4,128,256]{3,2,1,0:T(8,128)(2,1)S(1)}, bf16[2,4,128,256]{3,2,1,0:T(8,128)(2,1)}, u32[]{:S(2)}, u32[]{:S(2)}) %collective-permute-start.36) | collective-permute-done | bytes 524320 | tf_op jit(solution)/shard_map/ppermute | solution.py:349
  181.2 13.9 %collective-permute-done.39.refs_7_ = bf16[256,1408]{1,0:T(8,128)(2,1)} collective-permute-done((bf16[256,1408]{1,0:T(8,128)(2,1)}, bf16[256,1408]{1,0:T(8,128)(2,1)}, u32[]{:S(2)}, u32[]{:S(2)}) %collective-permute-start.39) | collective-permute-done | bytes 720928 | tf_op jit(solution)/shard_map/ppermute | solution.py:349
  195.1 15.1 %collective-permute-done.38.refs_6_ = bf16[256,1408]{1,0:T(8,128)(2,1)} collective-permute-done((bf16[256,1408]{1,0:T(8,128)(2,1)S(1)}, bf16[256,1408]{1,0:T(8,128)(2,1)}, u32[]{:S(2)}, u32[]{:S(2)}) %collective-permute-start.38) | collective-permute-done | bytes 720928 | tf_op jit(solution)/shard_map/ppermute | solution.py:349
  211.4 4.2 block.30.refs_9_
  228.5 4.3 collective-permute-done.40.refs_8_
  233.9 3.4 block.31.refs_9_
  237.4 4.6 collective-permute-start.42
  249.6 6.7 %collective-permute-done.42.refs_8_ = bf16[256,1408]{1,0:T(8,128)(2,1)S(1)} collective-permute-done((bf16[256,1408]{1,0:T(8,128)(2,1)S(1)}, bf16[256,1408]{1,0:T(8,128)(2,1)S(1)}, u32[]{:S(2)}, u32[]{:S(2)}) %collective-permute-start.42) | collective-permute-done | bytes 720928 | tf_op jit(solution)/shard_map/ppermute | solution.py:433
  269.8 3.3 block.32.refs_9_
  273.1 3.2 block.33.refs_11_
  276.4 4.3 collective-permute-done.34.refs_9_
  284.6 35.1 %attend_back.1 = (bf16[2,256,2048]{2,1,0:T(8,128)(2,1)}, bf16[2,256,1024]{2,1,0:T(8,128)(2,1)}, bf16[2,128,1024]{2,1,0:T(8,128)(2,1)}, f32[2,128,1024]{2,1,0:T(8...) custom-call(s32[2]{0:T(128)} %copy-done.80, ...), custom_call_target="tpu_custom_call" | custom-call | flops 1000 | bytes 1000 | tf_op jit(solution)/shard_map/attend_back/pallas_call | solution.py:82
  323.1 4.7 fusion.62
  337.5 10.3 %collective-permute-done.72.refs_11_ = bf16[256,1408]{1,0:T(8,128)(2,1)S(1)} collective-permute-done((bf16[256,1408]{1,0:T(8,128)(2,1)S(1)}, bf16[256,1408]{1,0:T(8,128)(2,1)S(1)}, u32[]{:S(2)}, u32[]{:S(2)}) %collective-permute-start.72) | collective-permute-done | bytes 720928 | tf_op jit(solution)/shard_map/ppermute | solution.py:431
  349.0 3.1 block.35.refs_11_
  352.2 5.1 collective-permute-start.76
  358.2 4.5 collective-permute-start.75
  373.8 4.8 collective-permute-start.73
  378.6 4.6 block.37.refs_12_
  383.1 6.1 %collective-permute-done.75.refs_11_ = bf16[256,1408]{1,0:T(8,128)(2,1)S(1)} collective-permute-done((bf16[256,1408]{1,0:T(8,128)(2,1)S(1)}, bf16[256,1408]{1,0:T(8,128)(2,1)S(1)}, u32[]{:S(2)}, u32[]{:S(2)}) %collective-permute-start.75) | collective-permute-done | bytes 720928 | tf_op jit(solution)/shard_map/ppermute | solution.py:433
  404.5 3.3 collective-permute-done.48
  408.4 5.8 collective-permute-done.49
  417.9 8.2 %collective-permute-done.51 = bf16[2,64,1536]{2,1,0:T(8,128)(2,1)S(1)} collective-permute-done((bf16[2,64,1536]{2,1,0:T(8,128)(2,1)S(1)}, bf16[2,64,1536]{2,1,0:T(8,128)(2,1)S(1)}, u32[]{:S(2)}, u32[]{:S(2)}) %collective-permute-start.51) | collective-permute-done | bytes 393248 | tf_op jit(solution)/shard_map/ppermute | solution.py:357
  428.3 4.6 collective-permute-start.81
  440.2 5.0 collective-permute-done.82.refs_12_
  449.9 4.2 block.42.refs_12_
  454.1 8.6 %collective-permute-done.80.refs_11_ = bf16[256,1408]{1,0:T(8,128)(2,1)S(1)} collective-permute-done((bf16[256,1408]{1,0:T(8,128)(2,1)S(1)}, bf16[256,1408]{1,0:T(8,128)(2,1)S(1)}, u32[]{:S(2)}, u32[]{:S(2)}) %collective-permute-start.80) | collective-permute-done | bytes 720928 | tf_op jit(solution)/shard_map/ppermute | solution.py:433
  462.8 4.4 collective-permute-start.78
  478.6 4.7 collective-permute-start.86
  491.4 8.3 %collective-permute-done.86.refs_11_ = bf16[256,1408]{1,0:T(8,128)(2,1)S(1)} collective-permute-done((bf16[256,1408]{1,0:T(8,128)(2,1)S(1)}, bf16[256,1408]{1,0:T(8,128)(2,1)S(1)}, u32[]{:S(2)}, u32[]{:S(2)}) %collective-permute-start.86) | collective-permute-done | bytes 720928 | tf_op jit(solution)/shard_map/ppermute | solution.py:438
  505.4 4.4 collective-permute-start.91
  512.0 4.5 collective-permute-start.89
  525.5 4.6 collective-permute-start.94
  540.4 4.3 collective-permute-start.92
  552.1 4.6 collective-permute-start.95
  564.2 6.5 %collective-permute-start.98 = (bf16[256,384]{1,0:T(8,128)(2,1)}, bf16[256,384]{1,0:T(8,128)(2,1)}, u32[]{:S(2)}, u32[]{:S(2)}) collective-permute-start(bf16[256,384]{1,0:T(8,128)(2,1)} %block.57.refs_6_), channel_id=1, source_target_pairs={{0,8},{4,12},{8,16},{12,20},{16,24},{20,28},{1,9},{5,13},{9,17},{1... | collective-permute-start | bytes 589832 | tf_op jit(solution)/shard_map/ppermute | solution.py:438
  571.7 3.2 natural.2
  602.5 3.2 natural.3
  (631 shorter events, 273.8 us)
Async XLA Ops:
  16.8 19.7 %collective-permute-start.4 = (bf16[128,512]{1,0:T(8,128)(2,1)S(1)}, bf16[128,512]{1,0:T(8,128)(2,1)S(1)}, u32[]{:S(2)}, u32[]{:S(2)}) collective-permute-start(bf16[128,512]{1,0:T(8,128)(2,1)S(1)} %get-tuple-element.58), channel_id=1, source_target_pairs={{0,24},{4,28},{1,25},{5,29},{2,26},{6,30},{3,27},{7,31}} | collective-permute-start | bytes 393224 | tf_op jit(solution)/shard_map/ppermute | solution.py:482
  38.5 29.3 %collective-permute-start = (bf16[256,256]{1,0:T(8,128)(2,1)S(1)}, bf16[256,256]{1,0:T(8,128)(2,1)S(1)}, u32[]{:S(2)}, u32[]{:S(2)}) collective-permute-start(bf16[256,256]{1,0:T(8,128)(2,1)S(1)} %get-tuple-element.57.refs_7_.refs_1_), channel_id=1, source_target_pairs={{0,2},{1,3},{2,0},{3,1},{4,6},{5,7},{6,4},{7,5},{8,10},{9,11},{10,... | collective-permute-start | bytes 393224 | tf_op jit(solution)/shard_map/ppermute | solution.py:508
  40.0 28.4 %collective-permute-start.9 = (bf16[256,256]{1,0:T(8,128)(2,1)S(1)}, bf16[256,256]{1,0:T(8,128)(2,1)S(1)}, u32[]{:S(2)}, u32[]{:S(2)}) collective-permute-start(bf16[256,256]{1,0:T(8,128)(2,1)S(1)} %get-tuple-element.59.refs_3_.refs_1_), channel_id=1, source_target_pairs={{0,2},{1,3},{2,0},{3,1},{4,6},{5,7},{6,4},{7,5},{8,10},{9,11},{10,... | collective-permute-start | bytes 393224 | tf_op jit(solution)/shard_map/ppermute | solution.py:508
  44.2 21.5 %collective-permute-start.14 = (bf16[4,128,512]{2,1,0:T(8,128)(2,1)}, bf16[4,128,512]{2,1,0:T(8,128)(2,1)}, u32[]{:S(2)}, u32[]{:S(2)}) collective-permute-start(bf16[4,128,512]{2,1,0:T(8,128)(2,1)} %get-tuple-element.152), channel_id=1, source_target_pairs={{0,4},{4,0},{8,12},{12,8},{16,20},{20,16},{24,28},{28,24},{1,5},{5... | collective-permute-start | bytes 1572872 | tf_op jit(solution)/shard_map/ppermute | solution.py:349
  175.8 19.2 %collective-permute-start.39 = (bf16[256,1408]{1,0:T(8,128)(2,1)}, bf16[256,1408]{1,0:T(8,128)(2,1)}, u32[]{:S(2)}, u32[]{:S(2)}) collective-permute-start(bf16[256,1408]{1,0:T(8,128)(2,1)} %get-tuple-element.70.refs_7_.refs_5_), channel_id=1, source_target_pairs={{0,4},{4,0},{8,12},{12,8},{16,20},{20,16},{24,28},{28,24},{1,5},{5... | collective-permute-start | bytes 2162696 | tf_op jit(solution)/shard_map/ppermute | solution.py:349
  177.3 32.8 %collective-permute-start.38 = (bf16[256,1408]{1,0:T(8,128)(2,1)S(1)}, bf16[256,1408]{1,0:T(8,128)(2,1)}, u32[]{:S(2)}, u32[]{:S(2)}) collective-permute-start(bf16[256,1408]{1,0:T(8,128)(2,1)S(1)} %get-tuple-element.69.refs_7_.refs_4_), channel_id=1, source_target_pairs={{0,4},{4,0},{8,12},{12,8},{16,20},{20,16},{24,28},{28,24},{1,5},{5... | collective-permute-start | bytes 2162696 | tf_op jit(solution)/shard_map/ppermute | solution.py:349
  179.7 38.6 %collective-permute-start.27 = (bf16[2,64,2048]{2,1,0:T(8,128)(2,1)}, bf16[2,64,2048]{2,1,0:T(8,128)(2,1)}, u32[]{:S(2)}, u32[]{:S(2)}) collective-permute-start(bf16[2,64,2048]{2,1,0:T(8,128)(2,1)} %slice.377), channel_id=1, source_target_pairs={{0,2},{1,3},{2,0},{3,1},{4,6},{5,7},{6,4},{7,5},{8,10},{9,11},{10,... | collective-permute-start | bytes 1572872 | tf_op jit(solution)/shard_map/ppermute | solution.py:353
  223.0 19.6 %collective-permute-start.28 = (bf16[2,64,2048]{2,1,0:T(8,128)(2,1)}, bf16[2,64,2048]{2,1,0:T(8,128)(2,1)}, u32[]{:S(2)}, u32[]{:S(2)}) collective-permute-start(bf16[2,64,2048]{2,1,0:T(8,128)(2,1)} %get-tuple-element.120.refs_1_), channel_id=1, source_target_pairs={{0,2},{1,3},{2,0},{3,1},{4,6},{5,7},{6,4},{7,5},{8,10},{9,11},{10,... | collective-permute-start | bytes 1572872 | tf_op jit(solution)/shard_map/ppermute | solution.py:357
  226.5 19.8 %collective-permute-start.31 = (bf16[4,128,256]{2,1,0:T(8,128)(2,1)}, bf16[4,128,256]{2,1,0:T(8,128)(2,1)S(1)}, u32[]{:S(2)}, u32[]{:S(2)}) collective-permute-start(bf16[4,128,256]{2,1,0:T(8,128)(2,1)} %get-tuple-element.84), channel_id=1, source_target_pairs={{0,4},{4,0},{8,12},{12,8},{16,20},{20,16},{24,28},{28,24},{1,5},{5... | collective-permute-start | bytes 786440 | tf_op jit(solution)/shard_map/ppermute | solution.py:349
  228.0 19.8 %collective-permute-start.30 = (bf16[4,128,256]{2,1,0:T(8,128)(2,1)}, bf16[4,128,256]{2,1,0:T(8,128)(2,1)S(1)}, u32[]{:S(2)}, u32[]{:S(2)}) collective-permute-start(bf16[4,128,256]{2,1,0:T(8,128)(2,1)} %copy-done.87), channel_id=1, source_target_pairs={{0,4},{4,0},{8,12},{12,8},{16,20},{20,16},{24,28},{28,24},{1,5},{5... | collective-permute-start | bytes 786440 | tf_op jit(solution)/shard_map/ppermute | solution.py:349
  237.4 18.9 %collective-permute-start.42 = (bf16[256,1408]{1,0:T(8,128)(2,1)S(1)}, bf16[256,1408]{1,0:T(8,128)(2,1)S(1)}, u32[]{:S(2)}, u32[]{:S(2)}) collective-permute-start(bf16[256,1408]{1,0:T(8,128)(2,1)S(1)} %block.31.refs_9_), channel_id=1, source_target_pairs={{0,8},{4,12},{8,16},{12,20},{1,9},{5,13},{9,17},{13,21},{2,10},{6,... | collective-permute-start | bytes 2162696 | tf_op jit(solution)/shard_map/ppermute | solution.py:433
  245.0 39.6 %collective-permute-start.29 = (bf16[2,128,2048]{2,1,0:T(8,128)(2,1)}, bf16[2,128,2048]{2,1,0:T(8,128)(2,1)}, u32[]{:S(2)}, u32[]{:S(2)}) collective-permute-start(bf16[2,128,2048]{2,1,0:T(8,128)(2,1)} %pad_maximum_fusion.8), channel_id=1, source_target_pairs={{0,1},{1,0},{2,3},{3,2},{4,5},{5,4},{6,7},{7,6},{8,9},{9,8},{10,11... | collective-permute-start | bytes 3145736 | tf_op jit(solution)/shard_map/ppermute | solution.py:359
  246.3 30.0 %collective-permute-start.35 = (bf16[256,1408]{1,0:T(8,128)(2,1)}, bf16[256,1408]{1,0:T(8,128)(2,1)}, u32[]{:S(2)}, u32[]{:S(2)}) collective-permute-start(bf16[256,1408]{1,0:T(8,128)(2,1)} %get-tuple-element.72.refs_2_.refs_8_), channel_id=1, source_target_pairs={{0,4},{4,0},{8,12},{12,8},{16,20},{20,16},{24,28},{28,24},{1,5},{5... | collective-permute-start | bytes 2162696 | tf_op jit(solution)/shard_map/ppermute | solution.py:349
  247.9 32.8 %collective-permute-start.34 = (bf16[256,1408]{1,0:T(8,128)(2,1)}, bf16[256,1408]{1,0:T(8,128)(2,1)}, u32[]{:S(2)}, u32[]{:S(2)}) collective-permute-start(bf16[256,1408]{1,0:T(8,128)(2,1)} %get-tuple-element.71.refs_1_.refs_7_), channel_id=1, source_target_pairs={{0,4},{4,0},{8,12},{12,8},{16,20},{20,16},{24,28},{28,24},{1,5},{5... | collective-permute-start | bytes 2162696 | tf_op jit(solution)/shard_map/ppermute | solution.py:349
  257.2 19.2 %collective-permute-start.33 = (bf16[4,128,256]{2,1,0:T(8,128)(2,1)S(1)}, bf16[4,128,256]{2,1,0:T(8,128)(2,1)S(1)}, u32[]{:S(2)}, u32[]{:S(2)}) collective-permute-start(bf16[4,128,256]{2,1,0:T(8,128)(2,1)S(1)} %collective-permute-done.31.refs_4_), channel_id=1, source_target_pairs={{0,1},{1,0},{2,3},{3,2},{4,5},{5,4},{6,7},{7,6},{8,9},{9,8},{10,11... | collective-permute-start | bytes 786440 | tf_op jit(solution)/shard_map/ppermute | solution.py:380
  321.0 37.2 %collective-permute-start.71 = (bf16[256,1408]{1,0:T(8,128)(2,1)S(1)}, bf16[256,1408]{1,0:T(8,128)(2,1)S(1)}, u32[]{:S(2)}, u32[]{:S(2)}) collective-permute-start(bf16[256,1408]{1,0:T(8,128)(2,1)S(1)} %copy-done.10), channel_id=1, source_target_pairs={{0,4},{4,0},{8,12},{12,8},{16,20},{20,16},{24,28},{28,24},{1,5},{5... | collective-permute-start | bytes 2162696 | tf_op jit(solution)/shard_map/ppermute | solution.py:349
  322.6 43.1 %collective-permute-start.70 = (bf16[256,1408]{1,0:T(8,128)(2,1)S(1)}, bf16[256,1408]{1,0:T(8,128)(2,1)S(1)}, u32[]{:S(2)}, u32[]{:S(2)}) collective-permute-start(bf16[256,1408]{1,0:T(8,128)(2,1)S(1)} %copy-done.8), channel_id=1, source_target_pairs={{0,4},{4,0},{8,12},{12,8},{16,20},{20,16},{24,28},{28,24},{1,5},{5... | collective-permute-start | bytes 2162696 | tf_op jit(solution)/shard_map/ppermute | solution.py:349
  332.5 19.7 %collective-permute-start.43 = (bf16[2,128,1024]{2,1,0:T(8,128)(2,1)S(1)}, bf16[2,128,1024]{2,1,0:T(8,128)(2,1)S(1)}, u32[]{:S(2)}, u32[]{:S(2)}) collective-permute-start(bf16[2,128,1024]{2,1,0:T(8,128)(2,1)S(1)} %copy-done.69), channel_id=1, source_target_pairs={{0,1},{1,0},{2,3},{3,2},{4,5},{5,4},{6,7},{7,6},{8,9},{9,8},{10,11... | collective-permute-start | bytes 1572872 | tf_op jit(solution)/shard_map/ppermute | solution.py:352
  334.5 28.2 %collective-permute-start.46 = (bf16[2,2,4,64,512]{4,3,0,2,1:T(8,128)(2,1)}, bf16[2,2,4,64,512]{4,3,0,2,1:T(8,128)(2,1)}, u32[]{:S(2)}, u32[]{:S(2)}) collective-permute-start(bf16[2,2,4,64,512]{4,3,0,2,1:T(8,128)(2,1)} %fusion.4), channel_id=1, source_target_pairs={{0,2},{1,3},{2,0},{3,1},{4,6},{5,7},{6,4},{7,5},{8,10},{9,11},{10,... | collective-permute-start | bytes 3145736 | tf_op jit(solution)/shard_map/ppermute | solution.py:659
  347.8 19.7 %collective-permute-start.77 = (bf16[256,1408]{1,0:T(8,128)(2,1)S(1)}, bf16[256,1408]{1,0:T(8,128)(2,1)S(1)}, u32[]{:S(2)}, u32[]{:S(2)}) collective-permute-start(bf16[256,1408]{1,0:T(8,128)(2,1)S(1)} %block.33.refs_11_), channel_id=1, source_target_pairs={{28,20},{24,16},{20,12},{16,8},{12,4},{8,0},{29,21},{25,17},{21,13... | collective-permute-start | bytes 2162696 | tf_op jit(solution)/shard_map/ppermute | solution.py:439
  352.2 21.6 %collective-permute-start.76 = (bf16[256,1408]{1,0:T(8,128)(2,1)S(1)}, bf16[256,1408]{1,0:T(8,128)(2,1)S(1)}, u32[]{:S(2)}, u32[]{:S(2)}) collective-permute-start(bf16[256,1408]{1,0:T(8,128)(2,1)S(1)} %block.32.refs_9_), channel_id=1, source_target_pairs={{0,8},{4,12},{8,16},{12,20},{16,24},{20,28},{1,9},{5,13},{9,17},{1... | collective-permute-start | bytes 2162696 | tf_op jit(solution)/shard_map/ppermute | solution.py:438
  358.2 31.1 %collective-permute-start.75 = (bf16[256,1408]{1,0:T(8,128)(2,1)S(1)}, bf16[256,1408]{1,0:T(8,128)(2,1)S(1)}, u32[]{:S(2)}, u32[]{:S(2)}) collective-permute-start(bf16[256,1408]{1,0:T(8,128)(2,1)S(1)} %block.35.refs_11_), channel_id=1, source_target_pairs={{0,8},{4,12},{8,16},{12,20},{1,9},{5,13},{9,17},{13,21},{2,10},{6,... | collective-permute-start | bytes 2162696 | tf_op jit(solution)/shard_map/ppermute | solution.py:433
  362.7 32.5 %collective-permute-start.74 = (bf16[256,1408]{1,0:T(8,128)(2,1)S(1)}, bf16[256,1408]{1,0:T(8,128)(2,1)S(1)}, u32[]{:S(2)}, u32[]{:S(2)}) collective-permute-start(bf16[256,1408]{1,0:T(8,128)(2,1)S(1)} %block.35.refs_11_), channel_id=1, source_target_pairs={{28,20},{24,16},{20,12},{16,8},{29,21},{25,17},{21,13},{17,9},{30,... | collective-permute-start | bytes 2162696 | tf_op jit(solution)/shard_map/ppermute | solution.py:434
  365.7 32.6 %collective-permute-start.44 = (bf16[2,64,1024]{2,1,0:T(8,128)(2,1)}, bf16[2,64,1024]{2,1,0:T(8,128)(2,1)S(1)}, u32[]{:S(2)}, u32[]{:S(2)}) collective-permute-start(bf16[2,64,1024]{2,1,0:T(8,128)(2,1)} %slice.379), channel_id=1, source_target_pairs={{0,2},{1,3},{2,0},{3,1},{4,6},{5,7},{6,4},{7,5},{8,10},{9,11},{10,... | collective-permute-start | bytes 786440 | tf_op jit(solution)/shard_map/ppermute | solution.py:353
  367.5 31.7 %collective-permute-start.47 = (bf16[2,4,64,512]{3,2,0,1:T(8,128)(2,1)S(1)}, bf16[2,4,64,512]{3,2,0,1:T(8,128)(2,1)S(1)}, u32[]{:S(2)}, u32[]{:S(2)}) collective-permute-start(bf16[2,4,64,512]{3,2,0,1:T(8,128)(2,1)S(1)} %fusion.17), channel_id=1, source_target_pairs={{0,4},{4,0},{8,12},{12,8},{16,20},{20,16},{24,28},{28,24},{1,5},{5... | collective-permute-start | bytes 1572872 | tf_op jit(solution)/shard_map/ppermute | solution.py:349
  373.8 41.1 %collective-permute-start.73 = (bf16[256,1408]{1,0:T(8,128)(2,1)S(1)}, bf16[256,1408]{1,0:T(8,128)(2,1)S(1)}, u32[]{:S(2)}, u32[]{:S(2)}) collective-permute-start(bf16[256,1408]{1,0:T(8,128)(2,1)S(1)} %block.36.refs_10_), channel_id=1, source_target_pairs={{0,8},{4,12},{28,20},{24,16},{1,9},{5,13},{29,21},{25,17},{2,10},{... | collective-permute-start | bytes 2162696 | tf_op jit(solution)/shard_map/ppermute | solution.py:431
  403.9 24.4 %collective-permute-start.69 = (bf16[256,1024]{1,0:T(8,128)(2,1)S(1)}, bf16[256,1024]{1,0:T(8,128)(2,1)S(1)}, u32[]{:S(2)}, u32[]{:S(2)}) collective-permute-start(bf16[256,1024]{1,0:T(8,128)(2,1)S(1)} %copy-done.12), channel_id=1, source_target_pairs={{0,4},{4,0},{8,12},{12,8},{16,20},{20,16},{24,28},{28,24},{1,5},{5... | collective-permute-start | bytes 1572872 | tf_op jit(solution)/shard_map/ppermute | solution.py:349
  407.8 25.1 %collective-permute-start.68 = (bf16[256,1024]{1,0:T(8,128)(2,1)S(1)}, bf16[256,1024]{1,0:T(8,128)(2,1)S(1)}, u32[]{:S(2)}, u32[]{:S(2)}) collective-permute-start(bf16[256,1024]{1,0:T(8,128)(2,1)S(1)} %copy-done.14), channel_id=1, source_target_pairs={{0,4},{4,0},{8,12},{12,8},{16,20},{20,16},{24,28},{28,24},{1,5},{5... | collective-permute-start | bytes 1572872 | tf_op jit(solution)/shard_map/ppermute | solution.py:349
  414.2 20.7 %collective-permute-start.22 = (bf16[2,128,2048]{2,1,0:T(8,128)(2,1)S(1)}, bf16[2,128,2048]{2,1,0:T(8,128)(2,1)S(1)}, u32[]{:S(2)}, u32[]{:S(2)}) collective-permute-start(bf16[2,128,2048]{2,1,0:T(8,128)(2,1)S(1)} %copy-done.113), channel_id=1, source_target_pairs={{0,1},{1,0},{2,3},{3,2},{4,5},{5,4},{6,7},{7,6},{8,9},{9,8},{10,11... | collective-permute-start | bytes 3145736 | tf_op jit(solution)/shard_map/ppermute | solution.py:352
  414.2 21.4 %collective-permute-start.67 = (bf16[2,4,128,256]{3,2,1,0:T(8,128)(2,1)S(1)}, bf16[2,4,128,256]{3,2,1,0:T(8,128)(2,1)S(1)}, u32[]{:S(2)}, u32[]{:S(2)}) collective-permute-start(bf16[2,4,128,256]{3,2,1,0:T(8,128)(2,1)S(1)} %collective-permute-done.66.refs_2_), channel_id=1, source_target_pairs={{0,1},{1,0},{2,3},{3,2},{4,5},{5,4},{6,7},{7,6},{8,9},{9,8},{10,11... | collective-permute-start | bytes 1572872 | tf_op jit(solution)/shard_map/ppermute | solution.py:380
  426.0 19.2 %collective-permute-start.82 = (bf16[256,1408]{1,0:T(8,128)(2,1)S(1)}, bf16[256,1408]{1,0:T(8,128)(2,1)S(1)}, u32[]{:S(2)}, u32[]{:S(2)}) collective-permute-start(bf16[256,1408]{1,0:T(8,128)(2,1)S(1)} %block.39.refs_12_), channel_id=1, source_target_pairs={{28,20},{24,16},{20,12},{16,8},{12,4},{8,0},{29,21},{25,17},{21,13... | collective-permute-start | bytes 2162696 | tf_op jit(solution)/shard_map/ppermute | solution.py:439
  428.3 21.1 %collective-permute-start.81 = (bf16[256,1408]{1,0:T(8,128)(2,1)S(1)}, bf16[256,1408]{1,0:T(8,128)(2,1)S(1)}, u32[]{:S(2)}, u32[]{:S(2)}) collective-permute-start(bf16[256,1408]{1,0:T(8,128)(2,1)S(1)} %block.38.refs_12_), channel_id=1, source_target_pairs={{0,8},{4,12},{8,16},{12,20},{16,24},{20,28},{1,9},{5,13},{9,17},{1... | collective-permute-start | bytes 2162696 | tf_op jit(solution)/shard_map/ppermute | solution.py:438
  432.9 29.9 %collective-permute-start.80 = (bf16[256,1408]{1,0:T(8,128)(2,1)S(1)}, bf16[256,1408]{1,0:T(8,128)(2,1)S(1)}, u32[]{:S(2)}, u32[]{:S(2)}) collective-permute-start(bf16[256,1408]{1,0:T(8,128)(2,1)S(1)} %block.40.refs_8_), channel_id=1, source_target_pairs={{0,8},{4,12},{8,16},{12,20},{1,9},{5,13},{9,17},{13,21},{2,10},{6,... | collective-permute-start | bytes 2162696 | tf_op jit(solution)/shard_map/ppermute | solution.py:433
  434.8 35.1 %collective-permute-start.79 = (bf16[256,1408]{1,0:T(8,128)(2,1)S(1)}, bf16[256,1408]{1,0:T(8,128)(2,1)S(1)}, u32[]{:S(2)}, u32[]{:S(2)}) collective-permute-start(bf16[256,1408]{1,0:T(8,128)(2,1)S(1)} %block.40.refs_8_), channel_id=1, source_target_pairs={{28,20},{24,16},{20,12},{16,8},{29,21},{25,17},{21,13},{17,9},{30,... | collective-permute-start | bytes 2162696 | tf_op jit(solution)/shard_map/ppermute | solution.py:434
  435.8 37.2 %collective-permute-start.52 = (bf16[2,128,1536]{2,1,0:T(8,128)(2,1)}, bf16[2,128,1536]{2,1,0:T(8,128)(2,1)}, u32[]{:S(2)}, u32[]{:S(2)}) collective-permute-start(bf16[2,128,1536]{2,1,0:T(8,128)(2,1)} %pad_maximum_fusion.11), channel_id=1, source_target_pairs={{0,1},{1,0},{2,3},{3,2},{4,5},{5,4},{6,7},{7,6},{8,9},{9,8},{10,11... | collective-permute-start | bytes 2359304 | tf_op jit(solution)/shard_map/ppermute | solution.py:359
  445.2 39.2 %collective-permute-start.23 = (bf16[2,64,2048]{2,1,0:T(8,128)(2,1)}, bf16[2,64,2048]{2,1,0:T(8,128)(2,1)}, u32[]{:S(2)}, u32[]{:S(2)}) collective-permute-start(bf16[2,64,2048]{2,1,0:T(8,128)(2,1)} %slice.378), channel_id=1, source_target_pairs={{0,2},{1,3},{2,0},{3,1},{4,6},{5,7},{6,4},{7,5},{8,10},{9,11},{10,... | collective-permute-start | bytes 1572872 | tf_op jit(solution)/shard_map/ppermute | solution.py:353
  449.4 54.3 %collective-permute-start.85 = (bf16[4,128,1024]{2,1,0:T(8,128)(2,1)S(1)}, bf16[4,128,1024]{2,1,0:T(8,128)(2,1)S(1)}, u32[]{:S(2)}, u32[]{:S(2)}) collective-permute-start(bf16[4,128,1024]{2,1,0:T(8,128)(2,1)S(1)} %side_sum.2.refs_12_), channel_id=1, source_target_pairs={{0,4},{4,0},{8,12},{12,8},{16,20},{20,16},{24,28},{28,24},{1,5},{5... | collective-permute-start | bytes 3145736 | tf_op jit(solution)/shard_map/ppermute | solution.py:349
  476.7 43.5 %collective-permute-start.53 = (bf16[2,128,2048]{2,1,0:T(8,128)(2,1)}, bf16[2,128,2048]{2,1,0:T(8,128)(2,1)}, u32[]{:S(2)}, u32[]{:S(2)}) collective-permute-start(bf16[2,128,2048]{2,1,0:T(8,128)(2,1)} %slice.375), channel_id=1, source_target_pairs={{0,1},{1,0},{2,3},{3,2},{4,5},{5,4},{6,7},{7,6},{8,9},{9,8},{10,11... | collective-permute-start | bytes 3145736 | tf_op jit(solution)/shard_map/ppermute | solution.py:352
  478.6 21.1 %collective-permute-start.86 = (bf16[256,1408]{1,0:T(8,128)(2,1)S(1)}, bf16[256,1408]{1,0:T(8,128)(2,1)S(1)}, u32[]{:S(2)}, u32[]{:S(2)}) collective-permute-start(bf16[256,1408]{1,0:T(8,128)(2,1)S(1)} %block.43.refs_12_), channel_id=1, source_target_pairs={{0,8},{4,12},{8,16},{12,20},{16,24},{20,28},{1,9},{5,13},{9,17},{1... | collective-permute-start | bytes 2162696 | tf_op jit(solution)/shard_map/ppermute | solution.py:438
  484.4 26.6 %collective-permute-start.84 = (bf16[256,1024]{1,0:T(8,128)(2,1)S(1)}, bf16[256,1024]{1,0:T(8,128)(2,1)S(1)}, u32[]{:S(2)}, u32[]{:S(2)}) collective-permute-start(bf16[256,1024]{1,0:T(8,128)(2,1)S(1)} %block.45.refs_13_), channel_id=1, source_target_pairs={{0,8},{4,12},{8,16},{12,20},{1,9},{5,13},{9,17},{13,21},{2,10},{6,... | collective-permute-start | bytes 1572872 | tf_op jit(solution)/shard_map/ppermute | solution.py:433
  489.1 27.5 %collective-permute-start.83 = (bf16[256,1024]{1,0:T(8,128)(2,1)S(1)}, bf16[256,1024]{1,0:T(8,128)(2,1)S(1)}, u32[]{:S(2)}, u32[]{:S(2)}) collective-permute-start(bf16[256,1024]{1,0:T(8,128)(2,1)S(1)} %block.45.refs_13_), channel_id=1, source_target_pairs={{28,20},{24,16},{20,12},{16,8},{29,21},{25,17},{21,13},{17,9},{30,... | collective-permute-start | bytes 1572872 | tf_op jit(solution)/shard_map/ppermute | solution.py:434
  499.7 25.7 %collective-permute-start.24 = (bf16[2,64,2048]{2,1,0:T(8,128)(2,1)S(1)}, bf16[2,64,2048]{2,1,0:T(8,128)(2,1)S(1)}, u32[]{:S(2)}, u32[]{:S(2)}) collective-permute-start(bf16[2,64,2048]{2,1,0:T(8,128)(2,1)S(1)} %fusion.7.refs_1_), channel_id=1, source_target_pairs={{0,2},{1,3},{2,0},{3,1},{4,6},{5,7},{6,4},{7,5},{8,10},{9,11},{10,... | collective-permute-start | bytes 1572872 | tf_op jit(solution)/shard_map/ppermute | solution.py:357
  512.0 22.2 %collective-permute-start.89 = (bf16[256,1024]{1,0:T(8,128)(2,1)S(1)}, bf16[256,1024]{1,0:T(8,128)(2,1)S(1)}, u32[]{:S(2)}, u32[]{:S(2)}) collective-permute-start(bf16[256,1024]{1,0:T(8,128)(2,1)S(1)} %block.48.refs_9_), channel_id=1, source_target_pairs={{0,8},{4,12},{8,16},{12,20},{16,24},{20,28},{1,9},{5,13},{9,17},{1... | collective-permute-start | bytes 1572872 | tf_op jit(solution)/shard_map/ppermute | solution.py:438
  522.5 25.8 %collective-permute-start.54 = (bf16[2,64,2048]{2,1,0:T(8,128)(2,1)S(1)}, bf16[2,64,2048]{2,1,0:T(8,128)(2,1)S(1)}, u32[]{:S(2)}, u32[]{:S(2)}) collective-permute-start(bf16[2,64,2048]{2,1,0:T(8,128)(2,1)S(1)} %slice.376), channel_id=1, source_target_pairs={{0,2},{1,3},{2,0},{3,1},{4,6},{5,7},{6,4},{7,5},{8,10},{9,11},{10,... | collective-permute-start | bytes 1572872 | tf_op jit(solution)/shard_map/ppermute | solution.py:353
  525.5 19.2 %collective-permute-start.94 = (bf16[128,1024]{1,0:T(8,128)(2,1)S(1)}, bf16[128,1024]{1,0:T(8,128)(2,1)S(1)}, u32[]{:S(2)}, u32[]{:S(2)}) collective-permute-start(bf16[128,1024]{1,0:T(8,128)(2,1)S(1)} %block.50.refs_10_), channel_id=1, source_target_pairs={{0,8},{4,12},{8,16},{12,20},{1,9},{5,13},{9,17},{13,21},{2,10},{6,... | collective-permute-start | bytes 786440 | tf_op jit(solution)/shard_map/ppermute | solution.py:433
  534.1 36.5 %collective-permute-start.25 = (bf16[2,128,2048]{2,1,0:T(8,128)(2,1)}, bf16[2,128,2048]{2,1,0:T(8,128)(2,1)}, u32[]{:S(2)}, u32[]{:S(2)}) collective-permute-start(bf16[2,128,2048]{2,1,0:T(8,128)(2,1)} %pad_maximum_fusion.6), channel_id=1, source_target_pairs={{0,1},{1,0},{2,3},{3,2},{4,5},{5,4},{6,7},{7,6},{8,9},{9,8},{10,11... | collective-permute-start | bytes 3145736 | tf_op jit(solution)/shard_map/ppermute | solution.py:359
  550.3 27.7 %collective-permute-start.55 = (bf16[2,64,2048]{2,1,0:T(8,128)(2,1)}, bf16[2,64,2048]{2,1,0:T(8,128)(2,1)}, u32[]{:S(2)}, u32[]{:S(2)}) collective-permute-start(bf16[2,64,2048]{2,1,0:T(8,128)(2,1)} %add_convert_fusion.refs_1_), channel_id=1, source_target_pairs={{0,2},{1,3},{2,0},{3,1},{4,6},{5,7},{6,4},{7,5},{8,10},{9,11},{10,... | collective-permute-start | bytes 1572872 | tf_op jit(solution)/shard_map/ppermute | solution.py:357
  579.3 23.2 %collective-permute-start.56 = (bf16[2,128,2048]{2,1,0:T(8,128)(2,1)S(1)}, bf16[2,128,2048]{2,1,0:T(8,128)(2,1)S(1)}, u32[]{:S(2)}, u32[]{:S(2)}) collective-permute-start(bf16[2,128,2048]{2,1,0:T(8,128)(2,1)S(1)} %pad_maximum_fusion.10), channel_id=1, source_target_pairs={{0,1},{1,0},{2,3},{3,2},{4,5},{5,4},{6,7},{7,6},{8,9},{9,8},{10,11... | collective-permute-start | bytes 3145736 | tf_op jit(solution)/shard_map/ppermute | solution.py:359
  (204 other events, 2947.3 us)

commit v4 on v3

--- a/solution.py
+++ b/solution.py
@@ -299,6 +299,285 @@
         pieces = (a0[m], a1[m], a2[m, :quarter, :], a2[m, quarter:, :])
         for k, piece in zip(ORDER, pieces):
             out[m, pl.ds(pl.multiple_of((ids[0] ^ k) * quarter, quarter), quarter), :] = piece
+
+
+class Wire:
+    def __init__(self, sends, recvs):
+        self.sends, self.recvs, self.used = sends, recvs, 0
+        self.seq, self.mp = lax.axis_index("seq"), lax.axis_index("mp")
+        self.place, self.side = self.seq // 2, self.seq % 2
+        core, cross = self.mp % 2, self.mp // 2
+        self.blocks = (
+            self.mp, 2 * (1 - cross) + core, 2 * cross + 1 - core, 2 * (1 - cross) + 1 - core
+        )
+        self.core, self.cross = {"mp": self.blocks[2]}, {"mp": self.blocks[1]}
+        self.beside = {"seq": self.seq + 1 - 2 * self.side}
+        self.up, self.down = {"seq": self.seq + 2}, {"seq": self.seq - 2}
+
+    def copy(self, source, target, device):
+        at = self.used
+        self.used += 1
+        return pltpu.make_async_remote_copy(
+            src_ref=source, dst_ref=target, send_sem=self.sends.at[at], recv_sem=self.recvs.at[at],
+            device_id=device, device_id_type=pl.DeviceIdType.MESH,
+        )
+
+    def send(self, source, target, device):
+        made = self.copy(source, target, device)
+        made.start()
+        return made
+
+    def greet(self, line, far=1):
+        barrier = pltpu.get_barrier_semaphore()
+        for device in (self.core, self.cross, self.beside):
+            pl.semaphore_signal(barrier, 1, device_id=device, device_id_type=pl.DeviceIdType.MESH)
+        for d in range(1, far + 1):
+            for way, there in ((1, self.place < line - d), (-1, self.place >= d)):
+
+                @pl.when(there)
+                def _():
+                    pl.semaphore_signal(
+                        barrier, 1, device_id={"seq": self.seq + 2 * way * d},
+                        device_id_type=pl.DeviceIdType.MESH,
+                    )
+        below, above = jnp.minimum(self.place, far), jnp.minimum(line - 1 - self.place, far)
+        pl.semaphore_wait(barrier, 3 + below + above)
+
+
+class LineSum:
+    def __init__(self, wire, term, room, rows, columns, keep):
+        got, out = room
+        view = lambda ref, i: ref.at[i, :rows, :columns]
+        self.place, self.term, self.keep = wire.place, term, keep
+        self.got = [view(got, i) for i in range(5)]
+        self.out = [view(out, i) for i in range(3)]
+        one, two_up, two_down, three_up, three_down = self.got
+        a, b, c = self.out
+        self.one = wire.copy(a, one, wire.up), wire.copy(a, one, wire.down)
+        self.two = wire.copy(b, two_up, wire.up), wire.copy(b, two_down, wire.down)
+        self.three = wire.copy(a, three_up, wire.up), wire.copy(c, three_down, wire.down)
+
+    def clear(self):
+        place = self.place
+        for ref, empty in zip(
+            self.got, ((place == 0) | (place == 3),) * 3 + (place == 0, place == 3)
+        ):
+
+            @pl.when(empty)
+            def _(ref=ref):
+                ref[...] = jnp.zeros(ref.shape, ref.dtype)
+
+    def step1(self):
+        place = self.place
+
+        @pl.when((place == 0) | (place == 3))
+        def _():
+            self.out[0][...] = self.term(3 - place).astype(LOW)
+
+        pl.when(place == 0)(self.one[0].start)
+        pl.when(place == 3)(self.one[1].start)
+
+    def step2(self):
+        place = self.place
+        pl.when(place == 1)(self.one[0].wait_recv)
+        pl.when(place == 2)(self.one[1].wait_recv)
+        self.out[1][...] = (
+            self.term((place + 2) % 4) + self.got[0][...].astype(F32)
+        ).astype(LOW)
+        pl.when(place <= 1)(self.two[0].start)
+        pl.when(place >= 2)(self.two[1].start)
+
+    def step3(self):
+        place = self.place
+
+        @pl.when((place == 1) | (place == 2))
+        def _():
+            self.two[0].wait_recv()
+            self.two[1].wait_recv()
+
+        pl.when(place == 0)(self.one[0].wait_send)
+        pl.when(place == 3)(self.one[1].wait_send)
+
+        @pl.when(place <= 2)
+        def _():
+            self.out[0][...] = (self.term(place + 1) + self.got[1][...].astype(F32)).astype(LOW)
+            self.three[0].start()
+
+        @pl.when(place >= 1)
+        def _():
+            self.out[2][...] = (self.term(place - 1) + self.got[2][...].astype(F32)).astype(LOW)
+            self.three[1].start()
+
+    def finish(self):
+        place = self.place
+        pl.when(place >= 1)(self.three[0].wait_recv)
+        pl.when(place <= 2)(self.three[1].wait_recv)
+        self.keep(
+            self.term(place) + self.got[3][...].astype(F32) + self.got[4][...].astype(F32)
+        )
+
+    def settle(self):
+        place = self.place
+        pl.when(place <= 1)(self.two[0].wait_send)
+        pl.when(place >= 2)(self.two[1].wait_send)
+        pl.when(place <= 2)(self.three[0].wait_send)
+        pl.when(place >= 1)(self.three[1].wait_send)
+
+
+def mesh_run(body, args, outs, scratch, number, name, limit, sends):
+    return pl.pallas_call(
+        body,
+        in_specs=[in_vmem() if kind else pl.BlockSpec(memory_space=pl.ANY) for kind, _ in args],
+        out_specs=[in_vmem() if kind else pl.BlockSpec(memory_space=pl.ANY) for kind, _ in outs],
+        out_shape=[shape for _, shape in outs],
+        scratch_shapes=[
+            *scratch, pltpu.SemaphoreType.DMA((sends,)), pltpu.SemaphoreType.DMA((sends,))
+        ],
+        cost_estimate=pl.CostEstimate(flops=1000, bytes_accessed=1000, transcendentals=0),
+        compiler_params=pltpu.CompilerParams(
+            collective_id=number, has_side_effects=True, vmem_limit_bytes=limit << 20
+        ),
+        name=name,
+    )(*[array for _, array in args])
+
+
+def attend_back_one(
+    scale, chunk, dyl, out_proj, q_up, key_ids, q, kv, o, lse, row_ids, cos, sin,
+    dqp, send, keep, kv_send, kv_keep, dq_acc, do_acc, delta_acc,
+):
+    heads, rows, wide = q.shape
+    half_rows = rows // 2
+    low = dyl[...]
+    for h in range(heads):
+        do = inner_cols(low, out_proj[h * wide : (h + 1) * wide, :]).astype(LOW)
+        do_acc[h] = do
+        delta = jnp.sum(
+            do.astype(F32) * o[:, h * wide : (h + 1) * wide].astype(F32), axis=-1, keepdims=True
+        )
+        delta_acc[h] = jnp.transpose(jnp.broadcast_to(delta, (rows, 128)))[:8]
+        dq_acc[h] = jnp.zeros((rows, wide), F32)
+    count = kv.shape[0] // 2 // chunk
+    for part, out in ((0, kv_keep), (1, kv_send)):
+        for i in range(count):
+            base = (part * count + i) * chunk
+            keys = kv[base : base + chunk, :wide]
+            values = kv[base : base + chunk, wide:]
+            at = key_ids[base : base + chunk, :]
+            bias = jnp.where((at >= row_ids[1:2, :]) & (at <= row_ids[0:1, :]), 0.0, NEG_LARGE)
+
+            def head(h, sums):
+                dk, dv = sums
+                q_h, do_h = q[h], do_acc[h]
+                probs = jnp.exp(inner_cols(keys, q_h) + bias - lse[pl.ds(h, 1), :])
+                back = inner_cols(values, do_h) - delta_acc[h][:1]
+                ds = (probs * back).astype(LOW)
+                dv = dv + dot(probs.astype(LOW), do_h)
+                dk = dk + dot(ds, q_h)
+                dq_acc[h] = dq_acc[h] + inner_rows(ds, keys)
+                return dk, dv
+
+            zero = jnp.zeros((chunk, wide), F32)
+            dk, dv = lax.fori_loop(0, heads, head, (zero, zero))
+            out[i * chunk : (i + 1) * chunk, :wide] = dk.astype(out.dtype)
+            out[i * chunk : (i + 1) * chunk, wide:] = dv.astype(out.dtype)
+    for h in range(heads):
+        dq = unrotate(dq_acc[h] * scale, cos[...], sin[...])
+        dqp[:, h * wide : (h + 1) * wide] = dq.astype(LOW)
+    low = dqp[...]
+    send[...] = inner_cols(low[half_rows:], q_up[...]).astype(LOW)
+    keep[...] = inner_cols(low[:half_rows], q_up[...])
+
+
+def mean_of(values):
+    return jnp.mean(values, axis=-1, keepdims=True)
+
+
+def terms_sum(pairs):
+    total = None
+    for left, right in pairs:
+        term = inner_rows(left, right)
+        total = term if total is None else total + term
+    return total
+
+
+def back1_body(quarter, scale, chunk, *refs):
+    refs = list(refs)
+    take = lambda n: [refs.pop(0) for _ in range(n)]
+    hid, (hid_other0, dz_mine, dz_got, dz_far) = take(2), take(4)
+    h2_theirs, dg = take(2), take(2)
+    dh2_send, dh2_keep, n2, inv2, dz, gain2, out_proj, q_up, key_ids = take(9)
+    groups = [take(7) for _ in range(2)]
+    grad, dy, gain_sum, dyl_mine, dyl_theirs, dqp, dqn_send, dqn_keep, kv_send, kv_keep = take(10)
+    h2_got, h2_far, dg_other = take(2), take(2), take(2)
+    hid_other1, got, out, core_got, cross_out, cross_got, dyl, dq_acc, do_acc, delta_acc = take(10)
+    wire = Wire(*take(2))
+    half, rows = 2 * quarter, 4 * quarter
+    wire.greet(4)
+    y_hid = wire.send(hid[1], hid_other1, wire.beside)
+    core_dh2 = wire.send(dh2_send, core_got, wire.core)
+    hid_all = (hid[0], hid[1], hid_other0, hid_other1)
+
+    def term(z):
+        pairs = [(dz_mine[m, z], hid_all[m][...]) for m in range(2)]
+        for m in range(2):
+            pairs.append((dz_got[m, z], hid_all[2 + m][:half, :]))
+            pairs.append((dz_far[m, z], hid_all[2 + m][half:, :]))
+        return terms_sum(pairs)
+
+    def keep(total):
+        grad[...] = jnp.transpose(total)
+
+    chain = LineSum(wire, term, (got, out), grad.shape[1], grad.shape[0], keep)
+    chain.clear()
+
+    core_dh2.wait_recv()
+    cross_out[...] = (
+        dh2_keep[:, quarter:, :] + core_got[:, quarter:, :].astype(F32)
+    ).astype(LOW)
+    cross_dh2 = wire.send(cross_out, cross_got, wire.cross)
+
+    y_hid.wait_recv()
+    y_next = [wire.send(h2_theirs[m], h2_got[m], wire.beside) for m in range(2)]
+    y_next += [wire.send(dg[m], dg_other[m], wire.beside) for m in range(2)]
+    chain.step1()
+
+    cross_dh2.wait_recv()
+    dh2 = (
+        dh2_keep[:, :quarter, :] + core_got[:, :quarter, :].astype(F32) + cross_got[...].astype(F32)
+    )
+    gain_sum[...] = jnp.sum(jnp.sum(dh2 * n2[...], axis=0), axis=0, keepdims=True)
+    back = dh2 * gain2[...]
+    grad_y = dz[:, :quarter, :].astype(F32) + inv2[...] * (
+        back - n2[...] * mean_of(back * n2[...])
+    )
+    dy[...] = grad_y
+    dyl[:, :quarter, :] = grad_y.astype(LOW)
+    cross_dyl = wire.send(dyl.at[:, :quarter, :], dyl.at[:, quarter:half, :], wire.cross)
+    chain.step2()
+    cross_dyl.wait_recv()
+    core_dyl = wire.send(dyl.at[:, :half, :], dyl.at[:, half:, :], wire.core)
+    core_dyl.wait_recv()
+
+    for m in range(2):
+        side_columns(dyl.at[m], dyl_mine.at[m], dyl_theirs.at[m], wire.side)
+        q, kv, o, lse, row_ids, cos, sin = groups[m]
+        attend_back_one(
+            scale, chunk, dyl.at[m], out_proj, q_up, key_ids, q, kv, o, lse, row_ids, cos, sin,
+            dqp.at[m], dqn_send.at[m], dqn_keep.at[m], kv_send.at[m], kv_keep.at[m],
+            dq_acc, do_acc, delta_acc,
+        )
+        if m == 0:
+            chain.step3()
+            core_h2 = []
+            for i in range(2):
+                y_next[i].wait_recv()
+                core_h2.append(wire.send(h2_got[i], h2_far[i], wire.core))
+    chain.finish()
+    for made in y_next[2:] + core_h2:
+        made.wait_recv()
+    for made in [y_hid, core_dh2, cross_dh2, cross_dyl, core_dyl, *y_next, *core_h2]:
+        made.wait_send()
+    chain.settle()
 
 
 def local(
@@ -334,6 +613,7 @@
     scale = head_dim ** (-0.5)
     key_count = seq * rows
     beside = [(i, i ^ 1) for i in range(seq)]
+    narrow = line == 4 and micro == 2 and key_count <= 2048 and not wide % 128
 
     def swap(index):
         return ((index & 1) << 1) | (index >> 1)
@@ -532,7 +812,7 @@
             jnp.concatenate([c_part[m][:quarter], swapped[:quarter], far[half : half + quarter]], 1)
         )
 
-    h2_mine, h2_got, hid, dg, du, state = [], [], [], [], [], []
+    h2_mine, h2_theirs, hid, dg, du, state = [], [], [], [], [], []
     for m in range(micro):
         x = lax.dynamic_slice_in_dim(tokens[m], me * quarter, quarter, 0).astype(F32)
         inv1 = inverse_rms(x)
@@ -551,7 +831,7 @@
         order = [hid_m]
         mine, theirs = split_sides(made, h2, half)
         h2_mine.append(mine)
-        h2_got.append(from_other(theirs))
+        h2_theirs.append(theirs)
         hid.append(hid_m)
         dg.append(dg_m)
         du.append(du_m)
@@ -566,12 +846,6 @@
     def terms_of(spans):
         return [(a, lead, m + micro * partner, None, first, count)
                 for a, lead, m, partner, first, count in spans]
-
-    lefts, spans = both_sides(dz_mine, dz_got)
-    chain_down = Chain(lefts, with_other(hid), terms_of(spans), (wide, hidden), turned=True)
-    lefts, spans = both_sides(h2_mine, [list(p) for p in zip(*h2_got)])
-    chain_gate = Chain(lefts, with_other(dg), terms_of(spans), (wide, hidden))
-    chain_up = Chain(lefts, with_other(du), terms_of(spans), (wide, hidden))
 
     send, keep = run(
         functools.partial(hidden_back_body, micro),
@@ -581,48 +855,95 @@
         order,
         name="hidden_back",
     )
-    order = chain_down.advance([send])
-    dh2 = sum_mp(send, keep)
-    y, n2, inv2, n1, inv1 = (stacked(k) for k in ("y", "n2", "inv2", "n1", "inv1"))
-    dz_own = dz[:, :quarter].astype(F32)
-    gain2 = jnp.sum(dh2 * n2, axis=(0, 1))
-    dy = dz_own + norm_backward(dh2 * gain2_row, n2, inv2)
-    for _ in range(2):
-        order = chain_down.advance(order)
-    order = chain_gate.advance(order)
-
-    def attend_back(which, pieces):
-        args = [*pieces, out_proj, q_up, key_ids[:, None]]
-        for m in which:
-            args += [qs[m], kv[m], os[m], lses[m], jnp.stack([row_ids, starts[m]], 0), *tables[m]]
-        n = len(which)
-        return run(
-            functools.partial(attend_back_body, scale, n, min(1024, key_count // 2)),
-            ids,
+    if narrow:
+        y, n2, inv2, n1, inv1 = (stacked(k) for k in ("y", "n2", "inv2", "n1", "inv1"))
+        args = [(1, a) for a in (*hid, other(hid[0]), dz_mine, *dz_got)]
+        args += [(0, a) for a in (*h2_theirs, *dg)]
+        args += [(1, a) for a in (send, keep, n2, inv2, dz, gain2_row, out_proj, q_up,
+                                  key_ids[:, None])]
+        for m in range(micro):
+            args += [(1, a) for a in (qs[m], kv[m], os[m], lses[m],
+                                      jnp.stack([row_ids, starts[m]], 0), *tables[m])]
+        outs = [(1, whole(shape, dtype)) for shape, dtype in (
+            ((hidden, wide), F32), ((micro, quarter, width), F32), ((1, width), F32),
+            ((micro, line, rows, wide), LOW), ((micro, line, half, wide), LOW),
+            ((micro, rows, heads * head_dim), LOW), ((micro, half, rank), LOW),
+            ((micro, half, rank), F32), ((micro, key_count // 2, 2 * head_dim), LOW),
+            ((micro, key_count // 2, 2 * head_dim), F32))]
+        outs += [(0, whole((line, half, wide), LOW))] * 4 + [(0, whole((rows, hidden), LOW))] * 2
+        low = lambda *shape: pltpu.VMEM(shape, LOW)
+        (grad_down, dy, gain2, dyl_mine, dyl_theirs, dqp, send, keep, kv_send, kv_keep,
+         *exchanged) = mesh_run(
+            functools.partial(back1_body, quarter, scale, 1024),
             args,
-            [whole((n, rows, width), LOW), whole((n, rows, heads * head_dim), LOW),
-             whole((n, half, rank), LOW), whole((n, half, rank), F32),
-             whole((n, key_count // 2, 2 * head_dim), LOW),
-             whole((n, key_count // 2, 2 * head_dim), F32), *sides_shape(width, half, (n,))],
-            order,
-            scratch=[pltpu.VMEM((heads, rows, head_dim), F32),
-                     pltpu.VMEM((heads, rows, head_dim), LOW),
-                     pltpu.VMEM((heads, 8, rows), F32)],
-            name="attend_back",
-            limit=56,
-        )
-
-    pieces = gather_mp(dy.astype(LOW))
-    if key_count <= 2048:
-        made = attend_back(range(micro), pieces)
+            outs,
+            [low(rows, hidden), low(5, wide, hidden), low(3, wide, hidden),
+             low(micro, half, width), low(micro, quarter, width), low(micro, quarter, width),
+             low(micro, rows, width), pltpu.VMEM((heads, rows, head_dim), F32),
+             low(heads, rows, head_dim), pltpu.VMEM((heads, 8, rows), F32)],
+            1,
+            "back1",
+            60,
+            24,
+        )
+        gain2 = gain2[0]
+        order = [send]
+        h2_parts = [exchanged[0:2], exchanged[2:4]]
+        lefts, spans = both_sides(h2_mine, h2_parts)
+        chain_gate = Chain(lefts, [*dg, *exchanged[4:6]], terms_of(spans), (wide, hidden))
+        chain_up = Chain(lefts, with_other(du), terms_of(spans), (wide, hidden))
+        lefts, spans = both_sides(dyl_mine, from_other(dyl_theirs))
+        chain_out = Chain(
+            lefts, with_other(os), terms_of(spans), (wide, heads * head_dim), turned=True
+        )
     else:
-        each = [attend_back([m], [p[m : m + 1] for p in pieces]) for m in range(micro)]
-        made = [jnp.concatenate(parts, 0) for parts in zip(*each)]
-    dyl, dqp, send, keep, kv_send, kv_keep, *made = made
-    order = [send]
-    dyl_mine, dyl_theirs = split_sides(made, dyl, half)
-    lefts, spans = both_sides(dyl_mine, from_other(dyl_theirs))
-    chain_out = Chain(lefts, with_other(os), terms_of(spans), (wide, heads * head_dim), turned=True)
+        lefts, spans = both_sides(dz_mine, dz_got)
+        chain_down = Chain(lefts, with_other(hid), terms_of(spans), (wide, hidden), turned=True)
+        lefts, spans = both_sides(h2_mine, [list(p) for p in zip(*[from_other(t) for t in h2_theirs])])
+        chain_gate = Chain(lefts, with_other(dg), terms_of(spans), (wide, hidden))
+        chain_up = Chain(lefts, with_other(du), terms_of(spans), (wide, hidden))
+        order = chain_down.advance([send])
+        dh2 = sum_mp(send, keep)
+        y, n2, inv2, n1, inv1 = (stacked(k) for k in ("y", "n2", "inv2", "n1", "inv1"))
+        dz_own = dz[:, :quarter].astype(F32)
+        gain2 = jnp.sum(dh2 * n2, axis=(0, 1))
+        dy = dz_own + norm_backward(dh2 * gain2_row, n2, inv2)
+        for _ in range(2):
+            order = chain_down.advance(order)
+        order = chain_gate.advance(order)
+
+        def attend_back(which, pieces):
+            args = [*pieces, out_proj, q_up, key_ids[:, None]]
+            for m in which:
+                args += [qs[m], kv[m], os[m], lses[m], jnp.stack([row_ids, starts[m]], 0), *tables[m]]
+            n = len(which)
+            return run(
+                functools.partial(attend_back_body, scale, n, min(1024, key_count // 2)),
+                ids,
+                args,
+                [whole((n, rows, width), LOW), whole((n, rows, heads * head_dim), LOW),
+                 whole((n, half, rank), LOW), whole((n, half, rank), F32),
+                 whole((n, key_count // 2, 2 * head_dim), LOW),
+                 whole((n, key_count // 2, 2 * head_dim), F32), *sides_shape(width, half, (n,))],
+                order,
+                scratch=[pltpu.VMEM((heads, rows, head_dim), F32),
+                         pltpu.VMEM((heads, rows, head_dim), LOW),
+                         pltpu.VMEM((heads, 8, rows), F32)],
+                name="attend_back",
+                limit=56,
+            )
+
+        pieces = gather_mp(dy.astype(LOW))
+        if key_count <= 2048:
+            made = attend_back(range(micro), pieces)
+        else:
+            each = [attend_back([m], [p[m : m + 1] for p in pieces]) for m in range(micro)]
+            made = [jnp.concatenate(parts, 0) for parts in zip(*each)]
+        dyl, dqp, send, keep, kv_send, kv_keep, *made = made
+        order = [send]
+        dyl_mine, dyl_theirs = split_sides(made, dyl, half)
+        lefts, spans = both_sides(dyl_mine, from_other(dyl_theirs))
+        chain_out = Chain(lefts, with_other(os), terms_of(spans), (wide, heads * head_dim), turned=True)
 
     def side_sum(lefts, rights, shape, after):
         terms = [(m, None, 0, m, 0, rows) for m in range(micro)]
@@ -674,7 +995,8 @@
          lax.dynamic_slice_in_dim(both, rank + me * kv_part, kv_part, 2)], -1
     )
 
-    grad_down, order = chain_down.finish(order)
+    if not narrow:
+        grad_down, order = chain_down.finish(order)
     order = chain_gate.advance(order)
     order = chain_up.advance(order)
     order = chain_out.advance(order)

time: 613 us -> 599 us (0.977)
  waiting for transfers between devices: 154 us -> 126 us
  Pallas kernels: 161 us -> 184 us
  starting transfers between devices: 161 us -> 139 us
  other arithmetic: 49.1 us -> 55.6 us
    pallas_call x0 -> x1, Pallas kernels: none -> 87.4 us  [mesh_run(): pl.pallas_call(body, in_specs=[in_vmem() if kind else pl.BlockSpec(memory...]
    pallas_call x43 -> x37, Pallas kernels: 161 us -> 96.3 us  [run(): pl.pallas_call(without, grid_spec=pltpu.PrefetchScalarGridSpec(num_scalar...]
    ppermute x6 -> x5, waiting for transfers between devices: 14.6 us -> 0.01 us  [advance(): self.up = lax.ppermute(term, 'seq', goes_up + goes_down)]
    ppermute x1, waiting for transfers between devices: 0.01 us -> 13.4 us  [local(): lax.ppermute(dkv[:, :, :, 1].astype(LOW), 'mp', CROSS).astype(F32)]
    ppermute x6 -> x5, waiting for transfers between devices: 23.9 us -> 10.8 us  [advance(): self.up = lax.ppermute(term, 'seq', goes_up)]
    ppermute x6 -> x5, waiting for transfers between devices: 14.4 us -> 3.34 us  [gather_mp(): near = lax.ppermute(piece, 'mp', CROSS)]
    ppermute x6 -> x5, waiting for transfers between devices: 9.41 us -> 16.7 us  [advance(): self.down = lax.ppermute(term_down, 'seq', goes_down)]
    ppermute x6 -> x5, starting transfers between devices: 22.9 us -> 15.7 us  [advance(): self.up = lax.ppermute(term, 'seq', goes_up)]
  transfers between devices with their start and end apart: 104 -> 88, of which waited for: 31 -> 22; matrix products, arithmetic and copies ran while one was open for 12% -> 15% of each run, Pallas kernels for 15% -> 15%
where the time goes in v4:
time: 599 us; the launch traced here: 593 us
  Pallas kernels  184 us (31%)
  starting transfers between devices  139 us (23%)
  waiting for transfers between devices  126 us (21%)
  local copies, waits for them, and re-layouts  72.9 us (12%)
  other arithmetic  55.6 us (9%)
  matrix products  10.3 us (2%)
    pallas_call x37, Pallas kernels, run(): pl.pallas_call(without, grid_spec=pltpu.PrefetchScalarGridSpec(num_scalar...  96.3 us
    pallas_call x1, Pallas kernels, mesh_run(): pl.pallas_call(body, in_specs=[in_vmem() if kind else pl.BlockSpec(memory...  87.4 us
    ppermute x12, waiting for transfers between devices, other(): return lax.ppermute(array, 'seq', beside)  48.2 us
    unnamed x255, local copies, waits for them, and re-layouts  46.5 us
    ppermute x5, starting transfers between devices, advance(): self.up = lax.ppermute(term_up, 'seq', goes_up)  22.5 us
    ppermute x5, starting transfers between devices, advance(): self.up = lax.ppermute(term, 'seq', goes_up + goes_down)  22.4 us
    ppermute x5, waiting for transfers between devices, advance(): self.down = lax.ppermute(term_down, 'seq', goes_down)  16.7 us
    ppermute x6, starting transfers between devices, local(): lax.ppermute(packed, 'seq', [(i, i + 2 * d) for i in range(seq - 2 * d)])  16.5 us
  transfers between devices with their start and end apart: 88, of which 22 were waited for; matrix products, arithmetic and copies ran while one was open for 15% of the time, Pallas kernels for 15%

profile of v4, /device:TPU:0, one launch (start us, length us, event | category | flops | bytes accessed | tf_op | source)
XLA Modules:
  0.0 592.9 jit_solution(12068812255371250773)
XLA Ops:
  12.5 2.4 first.2
  16.5 7.6 %collective-permute-start.4 = (bf16[128,512]{1,0:T(8,128)(2,1)}, bf16[128,512]{1,0:T(8,128)(2,1)}, u32[]{:S(2)}, u32[]{:S(2)}) collective-permute-start(bf16[128,512]{1,0:T(8,128)(2,1)} %get-tuple-element.67), channel_id=1, source_target_pairs={{0,24},{4,28},{1,25},{5,29},{2,26},{6,30},{3,27},{7,31}} | collective-permute-start | bytes 393224 | tf_op jit(solution)/shard_map/ppermute | solution.py:762
  29.5 2.4 first.3
  46.0 2.6 copy-done.38
  50.3 4.8 cotangent.1
  67.8 15.0 %collective-permute-done.14 = bf16[4,128,512]{2,1,0:T(8,128)(2,1)} collective-permute-done((bf16[4,128,512]{2,1,0:T(8,128)(2,1)}, bf16[4,128,512]{2,1,0:T(8,128)(2,1)}, u32[]{:S(2)}, u32[]{:S(2)}) %collective-permute-start.14) | collective-permute-done | bytes 524320 | tf_op jit(solution)/shard_map/ppermute | solution.py:629
  87.8 9.5 %attend.2 = (bf16[256,1024]{1,0:T(8,128)(2,1)}, bf16[4,256,256]{2,1,0:T(8,128)(2,1)S(1)}, bf16[256,1024]{1,0:T(8,128)(2,1)S(1)}, f32[4,256]{1,0:T(4,128)S(1)}, b...) custom-call(s32[2]{0:T(128)S(1)} %pad_add_fusion.3.refs_0_, ...), custom_call_target="tpu_custom_call" | custom-call | flops 1000 | bytes 1000 | tf_op jit(solution)/shard_map/attend/pallas_call | solution.py:82
  101.3 2.8 copy-done.3
  104.0 7.6 %attend.3 = (bf16[256,1024]{1,0:T(8,128)(2,1)}, bf16[4,256,256]{2,1,0:T(8,128)(2,1)S(1)}, bf16[256,1024]{1,0:T(8,128)(2,1)S(1)}, f32[4,256]{1,0:T(4,128)S(1)}, b...) custom-call(s32[2]{0:T(128)S(1)} %pad_add_fusion.3.refs_0_, ...), custom_call_target="tpu_custom_call" | custom-call | flops 1000 | bytes 1000 | tf_op jit(solution)/shard_map/attend/pallas_call | solution.py:82
  119.5 5.8 collective-permute-done.8
  132.7 3.3 collective-permute-done.18.refs_2_
  140.7 2.6 copy-done
  143.3 7.8 %forward.2 = (bf16[256,2048]{1,0:T(8,128)(2,1)}, bf16[256,1408]{1,0:T(8,128)(2,1)}, bf16[256,1408]{1,0:T(8,128)(2,1)S(1)}, bf16[256,1408]{1,0:T(8,128)(2,1)S(1)}...) custom-call(s32[2]{0:T(128)S(1)} %pad_add_fusion.3.refs_0_, ...), custom_call_target="tpu_custom_call" | custom-call | flops 1000 | bytes 1000 | tf_op jit(solution)/shard_map/forward/pallas_call | solution.py:82
  154.6 2.7 add.601.refs_18_
  162.7 2.3 pad_maximum_fusion.7.refs_12_
  165.8 2.6 copy-done.1
  171.3 7.2 %forward.3 = (bf16[256,2048]{1,0:T(8,128)(2,1)}, bf16[256,1408]{1,0:T(8,128)(2,1)S(1)}, bf16[256,1408]{1,0:T(8,128)(2,1)S(1)}, bf16[256,1408]{1,0:T(8,128)(2,1)S...) custom-call(s32[2]{0:T(128)S(1)} %pad_add_fusion.3.refs_0_, ...), custom_call_target="tpu_custom_call" | custom-call | flops 1000 | bytes 1000 | tf_op jit(solution)/shard_map/forward/pallas_call | solution.py:82
  178.6 3.5 copy-done.2
  182.0 17.8 %hidden_back.1 = (bf16[2,128,2048]{2,1,0:T(8,128)(2,1)S(1)}, f32[2,128,2048]{2,1,0:T(8,128)S(1)}) custom-call(s32[2]{0:T(128)S(1)} %pad_add_fusion.3.refs_0_, bf16[256,1408]{1,0:T(8,128)(2,1)S(1)} %get-tuple-element.84.refs_1_.refs_8_.refs_7_, bf16[256,1408]{1,0:T(8,128)(2,1)S(1)} %get-tuple-element.85.refs_2_.refs_9_.refs_8_, ...), custom_call_target="tpu_custom_call" | custom-call | flops 1000 | bytes 1000 | tf_op jit(solution)/shard_map/hidden_back/pallas_call | solution.py:82
  202.2 87.4 %back1.1 = (f32[1408,256]{1,0:T(8,128)}, f32[2,64,2048]{2,1,0:T(8,128)}, f32[1,2048]{1,0:T(1,128)}, bf16[2,4,256,256]{3,2,1,0:T(8,128)(2,1)}, bf16[2,4,128,256]{...) custom-call(bf16[256,1408]{1,0:T(8,128)(2,1)} %get-tuple-element.78., ...), custom_call_target="tpu_custom_call" | custom-call | flops 1000 | bytes 1000 | tf_op jit(solution)/shard_map/back1/pallas_call | solution.py:428
  300.1 4.6 fusion.61
  304.7 3.1 convert_add_fusion
  310.7 4.5 fusion.60
  318.1 2.4 collective-permute-start.59
  321.9 13.4 %collective-permute-done.32 = bf16[2,2,4,64,512]{4,3,0,2,1:T(8,128)(2,1)S(1)} collective-permute-done((bf16[2,2,4,64,512]{4,3,0,2,1:T(8,128)(2,1)}, bf16[2,2,4,64,512]{4,3,0,2,1:T(8,128)(2,1)S(1)}, u32[]{:S(2)}, u32[]{:S(2)}) %collective-permute-start.32) | collective-permute-done | bytes 1048608 | tf_op jit(solution)/shard_map/ppermute | solution.py:980
  347.9 2.8 collective-permute-done.33
  352.4 27.9 %collective-permute-done.52.refs_2_ = bf16[2,4,128,256]{3,2,1,0:T(8,128)(2,1)S(1)} collective-permute-done((bf16[2,4,128,256]{3,2,1,0:T(8,128)(2,1)S(1)}, bf16[2,4,128,256]{3,2,1,0:T(8,128)(2,1)S(1)}, u32[]{:S(2)}, u32[]{:S(2)}) %collective-permute-start.52) | collective-permute-done | bytes 524320 | tf_op jit(solution)/shard_map/ppermute | solution.py:629
  383.1 7.8 %collective-permute-done.35 = bf16[2,64,512]{2,1,0:T(8,128)(2,1)S(1)} collective-permute-done((bf16[2,64,512]{2,1,0:T(8,128)(2,1)S(1)}, bf16[2,64,512]{2,1,0:T(8,128)(2,1)S(1)}, u32[]{:S(2)}, u32[]{:S(2)}) %collective-permute-start.35) | collective-permute-done | bytes 131104 | tf_op jit(solution)/shard_map/ppermute | solution.py:984
  396.7 3.2 collective-permute-start.62
  401.0 8.3 %collective-permute-done.63.refs_11_ = bf16[256,1408]{1,0:T(8,128)(2,1)S(1)} collective-permute-done((bf16[256,1408]{1,0:T(8,128)(2,1)S(1)}, bf16[256,1408]{1,0:T(8,128)(2,1)S(1)}, u32[]{:S(2)}, u32[]{:S(2)}) %collective-permute-start.63) | collective-permute-done | bytes 720928 | tf_op jit(solution)/shard_map/ppermute | solution.py:713
  411.4 5.0 collective-permute-start.64
  423.8 13.0 %collective-permute-done.66.refs_12_ = bf16[256,1408]{1,0:T(8,128)(2,1)S(1)} collective-permute-done((bf16[256,1408]{1,0:T(8,128)(2,1)S(1)}, bf16[256,1408]{1,0:T(8,128)(2,1)S(1)}, u32[]{:S(2)}, u32[]{:S(2)}) %collective-permute-start.66) | collective-permute-done | bytes 720928 | tf_op jit(solution)/shard_map/ppermute | solution.py:719
  441.1 2.5 block.32.refs_12_
  443.5 9.3 %collective-permute-start.60 = (bf16[256,1024]{1,0:T(8,128)(2,1)S(1)}, bf16[256,1024]{1,0:T(8,128)(2,1)S(1)}, u32[]{:S(2)}, u32[]{:S(2)}) collective-permute-start(bf16[256,1024]{1,0:T(8,128)(2,1)S(1)} %block.29.refs_12_), channel_id=1, source_target_pairs={{0,8},{4,12},{28,20},{24,16},{1,9},{5,13},{29,21},{25,17},{2,10},{... | collective-permute-start | bytes 1572872 | tf_op jit(solution)/shard_map/ppermute | solution.py:711
  464.3 4.9 collective-permute-start.70
  476.0 9.6 %collective-permute-done.70.refs_11_ = bf16[256,1408]{1,0:T(8,128)(2,1)S(1)} collective-permute-done((bf16[256,1408]{1,0:T(8,128)(2,1)S(1)}, bf16[256,1408]{1,0:T(8,128)(2,1)S(1)}, u32[]{:S(2)}, u32[]{:S(2)}) %collective-permute-start.70) | collective-permute-done | bytes 720928 | tf_op jit(solution)/shard_map/ppermute | solution.py:718
  487.1 2.5 block.36.refs_5_
  491.3 4.4 collective-permute-start.75
  497.9 4.6 collective-permute-start.73
  511.5 4.6 collective-permute-start.78
  521.9 2.5 collective-permute-done.72.refs_4_.refs_5_.refs_6_
  525.9 4.3 collective-permute-start.76
  537.9 4.6 collective-permute-start.79
  549.3 6.6 %collective-permute-start.82 = (bf16[256,384]{1,0:T(8,128)(2,1)}, bf16[256,384]{1,0:T(8,128)(2,1)}, u32[]{:S(2)}, u32[]{:S(2)}) collective-permute-start(bf16[256,384]{1,0:T(8,128)(2,1)} %block.47.refs_6_), channel_id=1, source_target_pairs={{0,8},{4,12},{8,16},{12,20},{16,24},{20,28},{1,9},{5,13},{9,17},{1... | collective-permute-start | bytes 589832 | tf_op jit(solution)/shard_map/ppermute | solution.py:718
  558.2 3.2 natural.2
  578.4 2.6 collective-permute-start.50
  583.8 3.5 collective-permute-done.51
  588.4 3.2 natural.3
  (555 shorter events, 220.8 us)
Async XLA Ops:
  16.5 22.2 %collective-permute-start.4 = (bf16[128,512]{1,0:T(8,128)(2,1)}, bf16[128,512]{1,0:T(8,128)(2,1)}, u32[]{:S(2)}, u32[]{:S(2)}) collective-permute-start(bf16[128,512]{1,0:T(8,128)(2,1)} %get-tuple-element.67), channel_id=1, source_target_pairs={{0,24},{4,28},{1,25},{5,29},{2,26},{6,30},{3,27},{7,31}} | collective-permute-start | bytes 393224 | tf_op jit(solution)/shard_map/ppermute | solution.py:762
  28.0 56.1 %collective-permute-start = (bf16[256,256]{1,0:T(8,128)(2,1)S(1)}, bf16[256,256]{1,0:T(8,128)(2,1)S(1)}, u32[]{:S(2)}, u32[]{:S(2)}) collective-permute-start(bf16[256,256]{1,0:T(8,128)(2,1)S(1)} %get-tuple-element.66.refs_7_.refs_1_), channel_id=1, source_target_pairs={{0,2},{1,3},{2,0},{3,1},{4,6},{5,7},{6,4},{7,5},{8,10},{9,11},{10,... | collective-permute-start | bytes 393224 | tf_op jit(solution)/shard_map/ppermute | solution.py:788
  32.7 25.5 %collective-permute-start.11 = (bf16[128,512]{1,0:T(8,128)(2,1)}, bf16[128,512]{1,0:T(8,128)(2,1)}, u32[]{:S(2)}, u32[]{:S(2)}) collective-permute-start(bf16[128,512]{1,0:T(8,128)(2,1)} %get-tuple-element.72), channel_id=1, source_target_pairs={{0,8},{4,12},{8,16},{12,20},{16,24},{20,28},{1,9},{5,13},{9,17},{1... | collective-permute-start | bytes 393224 | tf_op jit(solution)/shard_map/ppermute | solution.py:762
  38.7 20.0 %collective-permute-start.12 = (bf16[128,512]{1,0:T(8,128)(2,1)}, bf16[128,512]{1,0:T(8,128)(2,1)S(1)}, u32[]{:S(2)}, u32[]{:S(2)}) collective-permute-start(bf16[128,512]{1,0:T(8,128)(2,1)} %get-tuple-element.72), channel_id=1, source_target_pairs={{0,16},{4,20},{8,24},{12,28},{1,17},{5,21},{9,25},{13,29},{2,18},{... | collective-permute-start | bytes 393224 | tf_op jit(solution)/shard_map/ppermute | solution.py:762
  40.0 19.2 %collective-permute-start.13 = (bf16[128,512]{1,0:T(8,128)(2,1)}, bf16[128,512]{1,0:T(8,128)(2,1)S(1)}, u32[]{:S(2)}, u32[]{:S(2)}) collective-permute-start(bf16[128,512]{1,0:T(8,128)(2,1)} %get-tuple-element.72), channel_id=1, source_target_pairs={{0,24},{4,28},{1,25},{5,29},{2,26},{6,30},{3,27},{7,31}} | collective-permute-start | bytes 393224 | tf_op jit(solution)/shard_map/ppermute | solution.py:762
  44.0 21.6 %collective-permute-start.5 = (bf16[4,128,512]{2,1,0:T(8,128)(2,1)}, bf16[4,128,512]{2,1,0:T(8,128)(2,1)}, u32[]{:S(2)}, u32[]{:S(2)}) collective-permute-start(bf16[4,128,512]{2,1,0:T(8,128)(2,1)} %get-tuple-element.164), channel_id=1, source_target_pairs={{0,4},{4,0},{8,12},{12,8},{16,20},{20,16},{24,28},{28,24},{1,5},{5... | collective-permute-start | bytes 1572872 | tf_op jit(solution)/shard_map/ppermute | solution.py:629
  58.2 26.5 %collective-permute-start.9 = (bf16[256,256]{1,0:T(8,128)(2,1)S(1)}, bf16[256,256]{1,0:T(8,128)(2,1)S(1)}, u32[]{:S(2)}, u32[]{:S(2)}) collective-permute-start(bf16[256,256]{1,0:T(8,128)(2,1)S(1)} %get-tuple-element.68.refs_3_.refs_1_), channel_id=1, source_target_pairs={{0,2},{1,3},{2,0},{3,1},{4,6},{5,7},{6,4},{7,5},{8,10},{9,11},{10,... | collective-permute-start | bytes 393224 | tf_op jit(solution)/shard_map/ppermute | solution.py:788
  58.7 81.7 %collective-permute-start.27 = (bf16[2,4,128,256]{3,2,1,0:T(8,128)(2,1)}, bf16[2,4,128,256]{3,2,1,0:T(8,128)(2,1)}, u32[]{:S(2)}, u32[]{:S(2)}) collective-permute-start(bf16[2,4,128,256]{3,2,1,0:T(8,128)(2,1)} %get-tuple-element.81), channel_id=1, source_target_pairs={{0,4},{4,0},{8,12},{12,8},{16,20},{20,16},{24,28},{28,24},{1,5},{5... | collective-permute-start | bytes 1572872 | tf_op jit(solution)/shard_map/ppermute | solution.py:629
  61.3 21.6 %collective-permute-start.14 = (bf16[4,128,512]{2,1,0:T(8,128)(2,1)}, bf16[4,128,512]{2,1,0:T(8,128)(2,1)}, u32[]{:S(2)}, u32[]{:S(2)}) collective-permute-start(bf16[4,128,512]{2,1,0:T(8,128)(2,1)} %get-tuple-element.166), channel_id=1, source_target_pairs={{0,4},{4,0},{8,12},{12,8},{16,20},{20,16},{24,28},{28,24},{1,5},{5... | collective-permute-start | bytes 1572872 | tf_op jit(solution)/shard_map/ppermute | solution.py:629
  67.0 18.5 %collective-permute-start.6 = (bf16[2,4,128,512]{3,2,1,0:T(8,128)(2,1)S(1)}, bf16[2,4,128,512]{3,2,1,0:T(8,128)(2,1)S(1)}, u32[]{:S(2)}, u32[]{:S(2)}) collective-permute-start(bf16[2,4,128,512]{3,2,1,0:T(8,128)(2,1)S(1)} %get-tuple-element.149), channel_id=1, source_target_pairs={{0,1},{1,0},{2,3},{3,2},{4,5},{5,4},{6,7},{7,6},{8,9},{9,8},{10,11... | collective-permute-start | bytes 3145736 | tf_op jit(solution)/shard_map/ppermute | solution.py:768
  140.4 61.7 %collective-permute-start.28 = (bf16[2,4,128,256]{3,2,1,0:T(8,128)(2,1)}, bf16[2,4,128,256]{3,2,1,0:T(8,128)(2,1)}, u32[]{:S(2)}, u32[]{:S(2)}) collective-permute-start(bf16[2,4,128,256]{3,2,1,0:T(8,128)(2,1)} %collective-permute-done.27.refs_4_), channel_id=1, source_target_pairs={{0,1},{1,0},{2,3},{3,2},{4,5},{5,4},{6,7},{7,6},{8,9},{9,8},{10,11... | collective-permute-start | bytes 1572872 | tf_op jit(solution)/shard_map/ppermute | solution.py:660
  151.2 51.0 %collective-permute-start.26 = (bf16[256,1408]{1,0:T(8,128)(2,1)}, bf16[256,1408]{1,0:T(8,128)(2,1)}, u32[]{:S(2)}, u32[]{:S(2)}) collective-permute-start(bf16[256,1408]{1,0:T(8,128)(2,1)} %get-tuple-element.78.refs_7_.refs_0_), channel_id=1, source_target_pairs={{0,4},{4,0},{8,12},{12,8},{16,20},{20,16},{24,28},{28,24},{1,5},{5... | collective-permute-start | bytes 2162696 | tf_op jit(solution)/shard_map/ppermute | solution.py:629
  298.0 41.6 %collective-permute-start.57 = (bf16[256,1408]{1,0:T(8,128)(2,1)S(1)}, bf16[256,1408]{1,0:T(8,128)(2,1)S(1)}, u32[]{:S(2)}, u32[]{:S(2)}) collective-permute-start(bf16[256,1408]{1,0:T(8,128)(2,1)S(1)} %copy-done.15), channel_id=1, source_target_pairs={{0,4},{4,0},{8,12},{12,8},{16,20},{20,16},{24,28},{28,24},{1,5},{5... | collective-permute-start | bytes 2162696 | tf_op jit(solution)/shard_map/ppermute | solution.py:629
  299.5 40.7 %collective-permute-start.56 = (bf16[256,1408]{1,0:T(8,128)(2,1)S(1)}, bf16[256,1408]{1,0:T(8,128)(2,1)S(1)}, u32[]{:S(2)}, u32[]{:S(2)}) collective-permute-start(bf16[256,1408]{1,0:T(8,128)(2,1)S(1)} %get-tuple-element.86.refs_3_.refs_7_), channel_id=1, source_target_pairs={{0,4},{4,0},{8,12},{12,8},{16,20},{20,16},{24,28},{28,24},{1,5},{5... | collective-permute-start | bytes 2162696 | tf_op jit(solution)/shard_map/ppermute | solution.py:629
  308.9 26.3 %collective-permute-start.32 = (bf16[2,2,4,64,512]{4,3,0,2,1:T(8,128)(2,1)}, bf16[2,2,4,64,512]{4,3,0,2,1:T(8,128)(2,1)S(1)}, u32[]{:S(2)}, u32[]{:S(2)}) collective-permute-start(bf16[2,2,4,64,512]{4,3,0,2,1:T(8,128)(2,1)} %fusion.4), channel_id=1, source_target_pairs={{0,2},{1,3},{2,0},{3,1},{4,6},{5,7},{6,4},{7,5},{8,10},{9,11},{10,... | collective-permute-start | bytes 3145736 | tf_op jit(solution)/shard_map/ppermute | solution.py:980
  318.1 24.9 %collective-permute-start.59 = (bf16[256,1408]{1,0:T(8,128)(2,1)S(1)}, bf16[256,1408]{1,0:T(8,128)(2,1)S(1)}, u32[]{:S(2)}, u32[]{:S(2)}) collective-permute-start(bf16[256,1408]{1,0:T(8,128)(2,1)S(1)} %block.25.refs_11_), channel_id=1, source_target_pairs={{0,8},{4,12},{28,20},{24,16},{1,9},{5,13},{29,21},{25,17},{2,10},{... | collective-permute-start | bytes 2162696 | tf_op jit(solution)/shard_map/ppermute | solution.py:711
  321.4 25.1 %collective-permute-start.30 = (bf16[2,64,1024]{2,1,0:T(8,128)(2,1)}, bf16[2,64,1024]{2,1,0:T(8,128)(2,1)S(1)}, u32[]{:S(2)}, u32[]{:S(2)}) collective-permute-start(bf16[2,64,1024]{2,1,0:T(8,128)(2,1)} %slice.354), channel_id=1, source_target_pairs={{0,2},{1,3},{2,0},{3,1},{4,6},{5,7},{6,4},{7,5},{8,10},{9,11},{10,... | collective-permute-start | bytes 786440 | tf_op jit(solution)/shard_map/ppermute | solution.py:633
  339.7 51.9 %collective-permute-start.55 = (bf16[256,1024]{1,0:T(8,128)(2,1)S(1)}, bf16[256,1024]{1,0:T(8,128)(2,1)S(1)}, u32[]{:S(2)}, u32[]{:S(2)}) collective-permute-start(bf16[256,1024]{1,0:T(8,128)(2,1)S(1)} %copy-done.17), channel_id=1, source_target_pairs={{0,4},{4,0},{8,12},{12,8},{16,20},{20,16},{24,28},{28,24},{1,5},{5... | collective-permute-start | bytes 1572872 | tf_op jit(solution)/shard_map/ppermute | solution.py:629
  340.2 52.7 %collective-permute-start.54 = (bf16[256,1024]{1,0:T(8,128)(2,1)S(1)}, bf16[256,1024]{1,0:T(8,128)(2,1)S(1)}, u32[]{:S(2)}, u32[]{:S(2)}) collective-permute-start(bf16[256,1024]{1,0:T(8,128)(2,1)S(1)} %copy-done.19), channel_id=1, source_target_pairs={{0,4},{4,0},{8,12},{12,8},{16,20},{20,16},{24,28},{28,24},{1,5},{5... | collective-permute-start | bytes 1572872 | tf_op jit(solution)/shard_map/ppermute | solution.py:629
  343.1 50.6 %collective-permute-start.58 = (bf16[256,1408]{1,0:T(8,128)(2,1)S(1)}, bf16[256,1408]{1,0:T(8,128)(2,1)S(1)}, u32[]{:S(2)}, u32[]{:S(2)}) collective-permute-start(bf16[256,1408]{1,0:T(8,128)(2,1)S(1)} %block.26.refs_12_), channel_id=1, source_target_pairs={{0,8},{4,12},{28,20},{24,16},{1,9},{5,13},{29,21},{25,17},{2,10},{... | collective-permute-start | bytes 2162696 | tf_op jit(solution)/shard_map/ppermute | solution.py:711
  346.6 33.7 %collective-permute-start.52 = (bf16[2,4,128,256]{3,2,1,0:T(8,128)(2,1)S(1)}, bf16[2,4,128,256]{3,2,1,0:T(8,128)(2,1)S(1)}, u32[]{:S(2)}, u32[]{:S(2)}) collective-permute-start(bf16[2,4,128,256]{3,2,1,0:T(8,128)(2,1)S(1)} %copy-done.124), channel_id=1, source_target_pairs={{0,4},{4,0},{8,12},{12,8},{16,20},{20,16},{24,28},{28,24},{1,5},{5... | collective-permute-start | bytes 1572872 | tf_op jit(solution)/shard_map/ppermute | solution.py:629
  351.0 30.6 %collective-permute-start.34 = (bf16[2,64,512]{2,1,0:T(8,128)(2,1)S(1)}, bf16[2,64,512]{2,1,0:T(8,128)(2,1)S(1)}, u32[]{:S(2)}, u32[]{:S(2)}) collective-permute-start(bf16[2,64,512]{2,1,0:T(8,128)(2,1)S(1)} %get-tuple-element.160), channel_id=1, source_target_pairs={{8,0},{12,4},{16,8},{20,12},{24,16},{28,20},{9,1},{13,5},{17,9},{2... | collective-permute-start | bytes 393224 | tf_op jit(solution)/shard_map/ppermute | solution.py:984
  390.9 29.2 %collective-permute-start.22 = (bf16[2,128,2048]{2,1,0:T(8,128)(2,1)}, bf16[2,128,2048]{2,1,0:T(8,128)(2,1)}, u32[]{:S(2)}, u32[]{:S(2)}) collective-permute-start(bf16[2,128,2048]{2,1,0:T(8,128)(2,1)} %pad_maximum_fusion.5), channel_id=1, source_target_pairs={{0,1},{1,0},{2,3},{3,2},{4,5},{5,4},{6,7},{7,6},{8,9},{9,8},{10,11... | collective-permute-start | bytes 3145736 | tf_op jit(solution)/shard_map/ppermute | solution.py:632
  391.5 17.8 %collective-permute-start.63 = (bf16[256,1408]{1,0:T(8,128)(2,1)S(1)}, bf16[256,1408]{1,0:T(8,128)(2,1)S(1)}, u32[]{:S(2)}, u32[]{:S(2)}) collective-permute-start(bf16[256,1408]{1,0:T(8,128)(2,1)S(1)} %block.27.refs_12_), channel_id=1, source_target_pairs={{0,8},{4,12},{8,16},{12,20},{1,9},{5,13},{9,17},{13,21},{2,10},{6,... | collective-permute-start | bytes 2162696 | tf_op jit(solution)/shard_map/ppermute | solution.py:713
  392.9 18.5 %collective-permute-start.65 = (bf16[256,1408]{1,0:T(8,128)(2,1)S(1)}, bf16[256,1408]{1,0:T(8,128)(2,1)S(1)}, u32[]{:S(2)}, u32[]{:S(2)}) collective-permute-start(bf16[256,1408]{1,0:T(8,128)(2,1)S(1)} %block.27.refs_12_), channel_id=1, source_target_pairs={{28,20},{24,16},{20,12},{16,8},{29,21},{25,17},{21,13},{17,9},{30,... | collective-permute-start | bytes 2162696 | tf_op jit(solution)/shard_map/ppermute | solution.py:714
  393.7 24.1 %collective-permute-start.37 = (bf16[2,64,1536]{2,1,0:T(8,128)(2,1)S(1)}, bf16[2,64,1536]{2,1,0:T(8,128)(2,1)S(1)}, u32[]{:S(2)}, u32[]{:S(2)}) collective-permute-start(bf16[2,64,1536]{2,1,0:T(8,128)(2,1)S(1)} %pad_maximum_fusion.16), channel_id=1, source_target_pairs={{0,2},{1,3},{2,0},{3,1},{4,6},{5,7},{6,4},{7,5},{8,10},{9,11},{10,... | collective-permute-start | bytes 1179656 | tf_op jit(solution)/shard_map/ppermute | solution.py:637
  396.7 46.8 %collective-permute-start.62 = (bf16[256,1408]{1,0:T(8,128)(2,1)S(1)}, bf16[256,1408]{1,0:T(8,128)(2,1)S(1)}, u32[]{:S(2)}, u32[]{:S(2)}) collective-permute-start(bf16[256,1408]{1,0:T(8,128)(2,1)S(1)} %block.28.refs_8_), channel_id=1, source_target_pairs={{0,8},{4,12},{8,16},{12,20},{1,9},{5,13},{9,17},{13,21},{2,10},{6,... | collective-permute-start | bytes 2162696 | tf_op jit(solution)/shard_map/ppermute | solution.py:713
  409.3 46.2 %collective-permute-start.61 = (bf16[256,1408]{1,0:T(8,128)(2,1)S(1)}, bf16[256,1408]{1,0:T(8,128)(2,1)S(1)}, u32[]{:S(2)}, u32[]{:S(2)}) collective-permute-start(bf16[256,1408]{1,0:T(8,128)(2,1)S(1)} %block.28.refs_8_), channel_id=1, source_target_pairs={{28,20},{24,16},{20,12},{16,8},{29,21},{25,17},{21,13},{17,9},{30,... | collective-permute-start | bytes 2162696 | tf_op jit(solution)/shard_map/ppermute | solution.py:714
  411.4 28.2 %collective-permute-start.64 = (bf16[256,1408]{1,0:T(8,128)(2,1)S(1)}, bf16[256,1408]{1,0:T(8,128)(2,1)S(1)}, u32[]{:S(2)}, u32[]{:S(2)}) collective-permute-start(bf16[256,1408]{1,0:T(8,128)(2,1)S(1)} %block.30.refs_12_), channel_id=1, source_target_pairs={{0,8},{4,12},{8,16},{12,20},{16,24},{20,28},{1,9},{5,13},{9,17},{1... | collective-permute-start | bytes 2162696 | tf_op jit(solution)/shard_map/ppermute | solution.py:718
  417.8 19.1 %collective-permute-start.66 = (bf16[256,1408]{1,0:T(8,128)(2,1)S(1)}, bf16[256,1408]{1,0:T(8,128)(2,1)S(1)}, u32[]{:S(2)}, u32[]{:S(2)}) collective-permute-start(bf16[256,1408]{1,0:T(8,128)(2,1)S(1)} %block.31.refs_13_), channel_id=1, source_target_pairs={{28,20},{24,16},{20,12},{16,8},{12,4},{8,0},{29,21},{25,17},{21,13... | collective-permute-start | bytes 2162696 | tf_op jit(solution)/shard_map/ppermute | solution.py:719
  420.0 38.4 %collective-permute-start.38 = (bf16[2,128,1536]{2,1,0:T(8,128)(2,1)}, bf16[2,128,1536]{2,1,0:T(8,128)(2,1)}, u32[]{:S(2)}, u32[]{:S(2)}) collective-permute-start(bf16[2,128,1536]{2,1,0:T(8,128)(2,1)} %pad_maximum_fusion.10), channel_id=1, source_target_pairs={{0,1},{1,0},{2,3},{3,2},{4,5},{5,4},{6,7},{7,6},{8,9},{9,8},{10,11... | collective-permute-start | bytes 2359304 | tf_op jit(solution)/shard_map/ppermute | solution.py:639
  436.8 52.8 %collective-permute-start.69 = (bf16[4,128,1024]{2,1,0:T(8,128)(2,1)S(1)}, bf16[4,128,1024]{2,1,0:T(8,128)(2,1)S(1)}, u32[]{:S(2)}, u32[]{:S(2)}) collective-permute-start(bf16[4,128,1024]{2,1,0:T(8,128)(2,1)S(1)} %side_sum.2.refs_11_), channel_id=1, source_target_pairs={{0,4},{4,0},{8,12},{12,8},{16,20},{20,16},{24,28},{28,24},{1,5},{5... | collective-permute-start | bytes 3145736 | tf_op jit(solution)/shard_map/ppermute | solution.py:629
  439.6 30.7 %collective-permute-start.23 = (bf16[2,64,2048]{2,1,0:T(8,128)(2,1)}, bf16[2,64,2048]{2,1,0:T(8,128)(2,1)}, u32[]{:S(2)}, u32[]{:S(2)}) collective-permute-start(bf16[2,64,2048]{2,1,0:T(8,128)(2,1)} %slice.353), channel_id=1, source_target_pairs={{0,2},{1,3},{2,0},{3,1},{4,6},{5,7},{6,4},{7,5},{8,10},{9,11},{10,... | collective-permute-start | bytes 1572872 | tf_op jit(solution)/shard_map/ppermute | solution.py:633
  443.5 20.8 %collective-permute-start.60 = (bf16[256,1024]{1,0:T(8,128)(2,1)S(1)}, bf16[256,1024]{1,0:T(8,128)(2,1)S(1)}, u32[]{:S(2)}, u32[]{:S(2)}) collective-permute-start(bf16[256,1024]{1,0:T(8,128)(2,1)S(1)} %block.29.refs_12_), channel_id=1, source_target_pairs={{0,8},{4,12},{28,20},{24,16},{1,9},{5,13},{29,21},{25,17},{2,10},{... | collective-permute-start | bytes 1572872 | tf_op jit(solution)/shard_map/ppermute | solution.py:711
  456.9 17.1 %collective-permute-start.71 = (bf16[256,1408]{1,0:T(8,128)(2,1)S(1)}, bf16[256,1408]{1,0:T(8,128)(2,1)S(1)}, u32[]{:S(2)}, u32[]{:S(2)}) collective-permute-start(bf16[256,1408]{1,0:T(8,128)(2,1)S(1)} %block.34.refs_9_), channel_id=1, source_target_pairs={{28,20},{24,16},{20,12},{16,8},{12,4},{8,0},{29,21},{25,17},{21,13... | collective-permute-start | bytes 2162696 | tf_op jit(solution)/shard_map/ppermute | solution.py:719
  462.3 44.0 %collective-permute-start.39 = (bf16[2,128,2048]{2,1,0:T(8,128)(2,1)}, bf16[2,128,2048]{2,1,0:T(8,128)(2,1)}, u32[]{:S(2)}, u32[]{:S(2)}) collective-permute-start(bf16[2,128,2048]{2,1,0:T(8,128)(2,1)} %slice.351), channel_id=1, source_target_pairs={{0,1},{1,0},{2,3},{3,2},{4,5},{5,4},{6,7},{7,6},{8,9},{9,8},{10,11... | collective-permute-start | bytes 3145736 | tf_op jit(solution)/shard_map/ppermute | solution.py:632
  464.3 21.3 %collective-permute-start.70 = (bf16[256,1408]{1,0:T(8,128)(2,1)S(1)}, bf16[256,1408]{1,0:T(8,128)(2,1)S(1)}, u32[]{:S(2)}, u32[]{:S(2)}) collective-permute-start(bf16[256,1408]{1,0:T(8,128)(2,1)S(1)} %block.33.refs_12_), channel_id=1, source_target_pairs={{0,8},{4,12},{8,16},{12,20},{16,24},{20,28},{1,9},{5,13},{9,17},{1... | collective-permute-start | bytes 2162696 | tf_op jit(solution)/shard_map/ppermute | solution.py:718
  470.2 26.6 %collective-permute-start.68 = (bf16[256,1024]{1,0:T(8,128)(2,1)S(1)}, bf16[256,1024]{1,0:T(8,128)(2,1)S(1)}, u32[]{:S(2)}, u32[]{:S(2)}) collective-permute-start(bf16[256,1024]{1,0:T(8,128)(2,1)S(1)} %block.35.refs_13_), channel_id=1, source_target_pairs={{0,8},{4,12},{8,16},{12,20},{1,9},{5,13},{9,17},{13,21},{2,10},{6,... | collective-permute-start | bytes 1572872 | tf_op jit(solution)/shard_map/ppermute | solution.py:713
  474.1 28.4 %collective-permute-start.67 = (bf16[256,1024]{1,0:T(8,128)(2,1)S(1)}, bf16[256,1024]{1,0:T(8,128)(2,1)S(1)}, u32[]{:S(2)}, u32[]{:S(2)}) collective-permute-start(bf16[256,1024]{1,0:T(8,128)(2,1)S(1)} %block.35.refs_13_), channel_id=1, source_target_pairs={{28,20},{24,16},{20,12},{16,8},{29,21},{25,17},{21,13},{17,9},{30,... | collective-permute-start | bytes 1572872 | tf_op jit(solution)/shard_map/ppermute | solution.py:714
  485.6 25.9 %collective-permute-start.24 = (bf16[2,64,2048]{2,1,0:T(8,128)(2,1)S(1)}, bf16[2,64,2048]{2,1,0:T(8,128)(2,1)S(1)}, u32[]{:S(2)}, u32[]{:S(2)}) collective-permute-start(bf16[2,64,2048]{2,1,0:T(8,128)(2,1)S(1)} %fusion.7.refs_1_), channel_id=1, source_target_pairs={{0,2},{1,3},{2,0},{3,1},{4,6},{5,7},{6,4},{7,5},{8,10},{9,11},{10,... | collective-permute-start | bytes 1572872 | tf_op jit(solution)/shard_map/ppermute | solution.py:637
  491.3 18.2 %collective-permute-start.75 = (bf16[128,1024]{1,0:T(8,128)(2,1)S(1)}, bf16[128,1024]{1,0:T(8,128)(2,1)S(1)}, u32[]{:S(2)}, u32[]{:S(2)}) collective-permute-start(bf16[128,1024]{1,0:T(8,128)(2,1)S(1)} %block.37.refs_9_), channel_id=1, source_target_pairs={{0,8},{4,12},{28,20},{24,16},{1,9},{5,13},{29,21},{25,17},{2,10},{... | collective-permute-start | bytes 786440 | tf_op jit(solution)/shard_map/ppermute | solution.py:711
  497.9 21.8 %collective-permute-start.73 = (bf16[256,1024]{1,0:T(8,128)(2,1)S(1)}, bf16[256,1024]{1,0:T(8,128)(2,1)S(1)}, u32[]{:S(2)}, u32[]{:S(2)}) collective-permute-start(bf16[256,1024]{1,0:T(8,128)(2,1)S(1)} %block.38.refs_9_), channel_id=1, source_target_pairs={{0,8},{4,12},{8,16},{12,20},{16,24},{20,28},{1,9},{5,13},{9,17},{1... | collective-permute-start | bytes 1572872 | tf_op jit(solution)/shard_map/ppermute | solution.py:718
  506.3 18.1 %collective-permute-start.72 = (bf16[4,256,384]{2,1,0:T(8,128)(2,1)S(1)}, bf16[4,256,384]{2,1,0:T(8,128)(2,1)S(1)}, u32[]{:S(2)}, u32[]{:S(2)}) collective-permute-start(bf16[4,256,384]{2,1,0:T(8,128)(2,1)S(1)} %side_sum.3.refs_6_), channel_id=1, source_target_pairs={{0,4},{4,0},{8,12},{12,8},{16,20},{20,16},{24,28},{28,24},{1,5},{5... | collective-permute-start | bytes 2359304 | tf_op jit(solution)/shard_map/ppermute | solution.py:629
  509.5 24.5 %collective-permute-start.40 = (bf16[2,64,2048]{2,1,0:T(8,128)(2,1)S(1)}, bf16[2,64,2048]{2,1,0:T(8,128)(2,1)S(1)}, u32[]{:S(2)}, u32[]{:S(2)}) collective-permute-start(bf16[2,64,2048]{2,1,0:T(8,128)(2,1)S(1)} %slice.352), channel_id=1, source_target_pairs={{0,2},{1,3},{2,0},{3,1},{4,6},{5,7},{6,4},{7,5},{8,10},{9,11},{10,... | collective-permute-start | bytes 1572872 | tf_op jit(solution)/shard_map/ppermute | solution.py:633
  511.5 18.7 %collective-permute-start.78 = (bf16[128,1024]{1,0:T(8,128)(2,1)S(1)}, bf16[128,1024]{1,0:T(8,128)(2,1)S(1)}, u32[]{:S(2)}, u32[]{:S(2)}) collective-permute-start(bf16[128,1024]{1,0:T(8,128)(2,1)S(1)} %block.40.refs_10_), channel_id=1, source_target_pairs={{0,8},{4,12},{8,16},{12,20},{1,9},{5,13},{9,17},{13,21},{2,10},{6,... | collective-permute-start | bytes 786440 | tf_op jit(solution)/shard_map/ppermute | solution.py:713
  519.7 37.5 %collective-permute-start.25 = (bf16[2,128,2048]{2,1,0:T(8,128)(2,1)}, bf16[2,128,2048]{2,1,0:T(8,128)(2,1)}, u32[]{:S(2)}, u32[]{:S(2)}) collective-permute-start(bf16[2,128,2048]{2,1,0:T(8,128)(2,1)} %pad_maximum_fusion.6), channel_id=1, source_target_pairs={{0,1},{1,0},{2,3},{3,2},{4,5},{5,4},{6,7},{7,6},{8,9},{9,8},{10,11... | collective-permute-start | bytes 3145736 | tf_op jit(solution)/shard_map/ppermute | solution.py:639
  536.1 26.9 %collective-permute-start.41 = (bf16[2,64,2048]{2,1,0:T(8,128)(2,1)}, bf16[2,64,2048]{2,1,0:T(8,128)(2,1)}, u32[]{:S(2)}, u32[]{:S(2)}) collective-permute-start(bf16[2,64,2048]{2,1,0:T(8,128)(2,1)} %add_convert_fusion.refs_1_), channel_id=1, source_target_pairs={{0,2},{1,3},{2,0},{3,1},{4,6},{5,7},{6,4},{7,5},{8,10},{9,11},{10,... | collective-permute-start | bytes 1572872 | tf_op jit(solution)/shard_map/ppermute | solution.py:637
  564.3 24.1 %collective-permute-start.42 = (bf16[2,128,2048]{2,1,0:T(8,128)(2,1)S(1)}, bf16[2,128,2048]{2,1,0:T(8,128)(2,1)S(1)}, u32[]{:S(2)}, u32[]{:S(2)}) collective-permute-start(bf16[2,128,2048]{2,1,0:T(8,128)(2,1)S(1)} %pad_maximum_fusion.9), channel_id=1, source_target_pairs={{0,1},{1,0},{2,3},{3,2},{4,5},{5,4},{6,7},{7,6},{8,9},{9,8},{10,11... | collective-permute-start | bytes 3145736 | tf_op jit(solution)/shard_map/ppermute | solution.py:639
  (169 other events, 2181.7 us)

commit v5 on v4

--- a/solution.py
+++ b/solution.py
@@ -192,13 +192,17 @@
 
 def hidden_back_body(micro, ids, *refs):
     dgs, dus = refs[:micro], refs[micro : 2 * micro]
-    w_gate, w_up, send, keep = refs[2 * micro :]
+    hids = refs[2 * micro : 3 * micro]
+    w_gate, w_up, w_down, send, keep, out_send, out_keep = refs[3 * micro :]
     half = send.shape[1]
     for m in range(micro):
         for rows, out in ((slice(half, None), send), (slice(0, half), keep)):
             out[m] = (
                 inner_cols(dgs[m][rows, :], w_gate[...]) + inner_cols(dus[m][rows, :], w_up[...])
             ).astype(out.dtype)
+    for m in range(micro):
+        for rows, out in ((slice(half, None), out_send), (slice(0, half), out_keep)):
+            out[m] = dot(hids[m][rows, :], w_down[...]).astype(out.dtype)
 
 
 def pick(ref, lead):
@@ -327,9 +331,12 @@
         made.start()
         return made
 
-    def greet(self, line, far=1):
+    def greet(self, line, far=1, diagonal=False):
         barrier = pltpu.get_barrier_semaphore()
-        for device in (self.core, self.cross, self.beside):
+        devices = [self.core, self.cross, self.beside]
+        if diagonal:
+            devices.append({"mp": self.blocks[3]})
+        for device in devices:
             pl.semaphore_signal(barrier, 1, device_id=device, device_id_type=pl.DeviceIdType.MESH)
         for d in range(1, far + 1):
             for way, there in ((1, self.place < line - d), (-1, self.place >= d)):
@@ -341,7 +348,7 @@
                         device_id_type=pl.DeviceIdType.MESH,
                     )
         below, above = jnp.minimum(self.place, far), jnp.minimum(line - 1 - self.place, far)
-        pl.semaphore_wait(barrier, 3 + below + above)
+        pl.semaphore_wait(barrier, len(devices) + below + above)
 
 
 class LineSum:
@@ -578,6 +585,349 @@
     for made in [y_hid, core_dh2, cross_dh2, cross_dyl, core_dyl, *y_next, *core_h2]:
         made.wait_send()
     chain.settle()
+
+
+class Share:
+    def __init__(self, wire, out, quarter):
+        spot = lambda block: out.at[:, pl.ds(pl.multiple_of(block * quarter, quarter), quarter), :]
+        own, near = spot(wire.blocks[0]), spot(wire.blocks[1])
+        self.own = own
+        self.first = wire.copy(own, own, wire.cross)
+        self.rest = wire.copy(own, own, wire.core), wire.copy(near, near, wire.core)
+
+    def begin(self, value):
+        self.own[...] = value
+        self.first.start()
+        self.rest[0].start()
+
+    def forward(self):
+        self.first.wait_recv()
+        self.rest[1].start()
+
+    def end(self):
+        for made in self.rest:
+            made.wait_recv()
+        for made in (self.first, *self.rest):
+            made.wait_send()
+
+
+class RowSum:
+    def __init__(self, wire, send, kept, got, cross_out, cross_got, quarter):
+        self.kept, self.got, self.quarter = kept, got, quarter
+        self.out, self.back = cross_out, cross_got
+        self.core = wire.copy(send, got, wire.core)
+        self.cross = wire.copy(cross_out, cross_got, wire.cross)
+
+    def pass_on(self):
+        self.core.wait_recv()
+        rest = slice(self.quarter, None)
+        self.out[...] = (self.kept[:, rest, :] + self.got[:, rest, :].astype(F32)).astype(LOW)
+        self.cross.start()
+
+    def result(self):
+        self.cross.wait_recv()
+        own = slice(0, self.quarter)
+        return (
+            self.kept[:, own, :] + self.got[:, own, :].astype(F32) + self.back[...].astype(F32)
+        )
+
+    def end(self):
+        self.core.wait_send()
+        self.cross.wait_send()
+
+
+def halves_terms(mine, got, far, rights, half):
+    pairs = [(mine[m], rights[m][...]) for m in range(2)]
+    for m in range(2):
+        pairs.append((got[m], rights[2 + m][:half, :]))
+        pairs.append((far[m], rights[2 + m][half:, :]))
+    return pairs
+
+
+def back2_body(quarter, *refs):
+    refs = list(refs)
+    take = lambda n: [refs.pop(0) for _ in range(n)]
+    dg, dg_other, du, h2_mine, h2_got, h2_far = (take(2) for _ in range(6))
+    kv_send, kv_keep, dqn_send, dqn_keep, chat, inv_c, gain_c, cos, sin = take(9)
+    qn_theirs = take(2)
+    dqp, dyl_theirs, o0, o1, ffn_send, ffn_keep, y = take(7)
+    grad_gate, grad_up, dfirst, gain_sum, qup_side, dyl_got, dyl_far, oo0, oo1, layer_out = take(10)
+    du_other = take(2)
+    got_a, out_a, got_b, out_b = take(4)
+    dqn_got, dqn_out, dqn_back = take(3)
+    kv_got, kv_out, kv_back, side_out, side_got, line_out, line_got, kv_own = take(8)
+    both, side_sums = take(2)
+    ffn_got, ffn_out, ffn_back = take(3)
+    wire = Wire(*take(2))
+    half, rows = 2 * quarter, 4 * quarter
+    wide = kv_own.shape[2] // 2
+    place = wire.place
+    wire.greet(4, 3)
+
+    y_du = [wire.send(du[m], du_other[m], wire.beside) for m in range(2)]
+    dqn_sum = RowSum(wire, dqn_send, dqn_keep, dqn_got, dqn_out, dqn_back, quarter)
+    dqn_sum.core.start()
+    core_kv = wire.send(kv_send, kv_got, wire.core)
+    ffn_sum = RowSum(wire, ffn_send, ffn_keep, ffn_got, ffn_out, ffn_back, quarter)
+    ffn_sum.core.start()
+
+    def gate_term(z):
+        return terms_sum(halves_terms(
+            [a.at[z][...] for a in h2_mine], [a.at[z][...] for a in h2_got],
+            [a.at[z][...] for a in h2_far], (*dg, *dg_other), half))
+
+    def up_term(z):
+        return terms_sum(halves_terms(
+            [a.at[z][...] for a in h2_mine], [a.at[z][...] for a in h2_got],
+            [a.at[z][...] for a in h2_far], (*du, *du_other), half))
+
+    def keep_gate(total):
+        grad_gate[...] = total
+
+    def keep_up(total):
+        grad_up[...] = total
+
+    gate = LineSum(wire, gate_term, (got_a, out_a), *grad_gate.shape, keep_gate)
+    up = LineSum(wire, up_term, (got_b, out_b), *grad_up.shape, keep_up)
+    gate.clear()
+    up.clear()
+    line_kv = []
+    for d in range(1, 4):
+        line_kv.append(wire.copy(line_out.at[d - 1], line_got.at[d - 1],
+                                 {"seq": wire.seq - 2 * d}))
+
+        @pl.when(place > 3 - d)
+        def _(d=d):
+            line_got[d - 1] = jnp.zeros(line_got.shape[1:], LOW)
+
+    gate.step1()
+    dqn_sum.pass_on()
+    core_kv.wait_recv()
+    kv_out[...] = (kv_keep[:, :, 1] + kv_got[:, :, 1].astype(F32)).astype(LOW)
+    cross_kv = wire.send(kv_out, kv_back, wire.cross)
+    for z in range(4):
+        side_sums[z] = terms_sum([(qn_theirs[m][z], dqp[m]) for m in range(2)]).astype(LOW)
+    dqn = dqn_sum.result()
+    gain_sum[...] = jnp.sum(jnp.sum(dqn * chat[...], axis=0), axis=0, keepdims=True)
+    back = dqn * gain_c[...]
+    rank = chat.shape[2]
+    both[:, :quarter, :rank] = (
+        inv_c[...] * (back - chat[...] * mean_of(back * chat[...]))
+    ).astype(LOW)
+    gate.step2()
+
+    cross_kv.wait_recv()
+    for part in range(2):
+        span = slice(4 * part, 4 * part + 4)
+        total = kv_keep[:, span, 0] + kv_got[:, span, 0].astype(F32) + kv_back[:, span].astype(F32)
+        if part:
+            side_out[...] = total.astype(LOW)
+    for made in y_du:
+        made.wait_recv()
+    side_kv = wire.send(side_out, side_got, wire.beside)
+    y_rest = [wire.send(side_sums, qup_side, wire.beside)]
+    up.step1()
+    gate.step3()
+    ffn_sum.pass_on()
+    side_kv.wait_recv()
+    y_rest.append(wire.send(dyl_theirs, dyl_got, wire.beside))
+    y_rest += [wire.send(a, b, wire.beside) for a, b in ((o0, oo0), (o1, oo1))]
+    own = kv_keep[:, :4, 0] + kv_got[:, :4, 0].astype(F32) + kv_back[:, :4].astype(F32)
+    own = own + side_got[...].astype(F32)
+    kv_own[...] = own[:, 0]
+    for d in range(1, 4):
+        line_out[d - 1] = own[:, d].astype(LOW)
+        pl.when(place >= d)(line_kv[d - 1].start)
+    up.step2()
+    gate.finish()
+    share = Share(wire, layer_out, quarter)
+    share.begin((y[...] + ffn_sum.result()).astype(LOW))
+    for d in range(1, 4):
+        pl.when(place <= 3 - d)(line_kv[d - 1].wait_recv)
+    total = kv_own[...]
+    for d in range(1, 4):
+        total = total + line_got[d - 1].astype(F32)
+    both[:, :quarter, rank : rank + wide] = unrotate(
+        total[:, :, :wide], cos[...], sin[...]
+    ).astype(LOW)
+    both[:, :quarter, rank + wide :] = total[:, :, wide:].astype(LOW)
+    cross_both = wire.send(both.at[:, :quarter, :], both.at[:, quarter:half, :], wire.cross)
+    share.forward()
+    cross_both.wait_recv()
+    core_both = wire.send(both.at[:, :half, :], both.at[:, half:, :], wire.core)
+    up.step3()
+    core_both.wait_recv()
+    part = rank // 4
+    kv_part = wide // 2
+    dfirst[:, :, :part] = both[:, :, pl.ds(pl.multiple_of(wire.mp * part, part), part)]
+    dfirst[:, :, part:] = both[
+        :, :, pl.ds(pl.multiple_of(rank + wire.mp * kv_part, kv_part), kv_part)
+    ]
+    y_rest[1].wait_recv()
+    core_dyl = wire.send(dyl_got, dyl_far, wire.core)
+    up.finish()
+    share.end()
+    core_dyl.wait_recv()
+    for made in (y_rest[0], y_rest[2], y_rest[3]):
+        made.wait_recv()
+    for made in [*y_du, core_kv, cross_kv, side_kv, cross_both, core_both, *y_rest, core_dyl]:
+        made.wait_send()
+    for d in range(1, 4):
+        pl.when(place >= d)(line_kv[d - 1].wait_send)
+    dqn_sum.end()
+    ffn_sum.end()
+    gate.settle()
+    up.settle()
+
+
+def back3_body(quarter, *refs):
+    refs = list(refs)
+    take = lambda n: [refs.pop(0) for _ in range(n)]
+    dfirst, weights = take(2)
+    h1_mine, h1_theirs, o, oo = (take(2) for _ in range(4))
+    dyl_mine, dyl_got, dyl_far = take(3)
+    qn_mine = take(2)
+    dqp, qup_side, n1, inv1, dy, gain1, gain2_sum, gain_c_sum = take(8)
+    grad_out, grad_qup, grad_qdown, grad_kv, grad_tokens, gains = take(6)
+    got_a, out_a, got_b, out_b, got_c, out_c = take(6)
+    side_sums, side_got = take(2)
+    send, kept, row_got, row_out, row_back = take(5)
+    kv_out, kv_got = take(2)
+    sums, sums_core, sums_cross, sums_side, sums_line = take(5)
+    wire = Wire(*take(2))
+    half, rows = 2 * quarter, 4 * quarter
+    place = wire.place
+    wire.greet(4, 3, diagonal=True)
+
+    for z in range(4):
+        side_sums[z] = terms_sum([(h1_theirs[m][z], dfirst[m]) for m in range(2)]).astype(LOW)
+    side_first = wire.send(side_sums, side_got, wire.beside)
+
+    def out_term(z):
+        return terms_sum(halves_terms(
+            [dyl_mine[m, z] for m in range(2)], [dyl_got[m, z] for m in range(2)],
+            [dyl_far[m, z] for m in range(2)], (*o, *oo), half))
+
+    def qup_term(z):
+        return terms_sum([(qn_mine[m][z], dqp[m]) for m in range(2)]) + qup_side[z].astype(F32)
+
+    def first_term(z):
+        return terms_sum([(h1_mine[m][z], dfirst[m]) for m in range(2)]) + side_got[z].astype(F32)
+
+    def keep_out(total):
+        grad_out[...] = jnp.transpose(total)
+
+    def keep_qup(total):
+        grad_qup[...] = total
+
+    part = grad_qdown.shape[1]
+
+    def keep_first(total):
+        grad_qdown[...] = total[:, :part]
+        kv_out[...] = total[:, part:]
+
+    out = LineSum(wire, out_term, (got_a, out_a), *grad_out.shape[::-1], keep_out)
+    qup = LineSum(wire, qup_term, (got_b, out_b), *grad_qup.shape, keep_qup)
+    first = LineSum(wire, first_term, (got_c, out_c), kv_out.shape[0], dfirst.shape[2], keep_first)
+    for chain in (out, qup, first):
+        chain.clear()
+    row_sum = RowSum(wire, send, kept, row_got, row_out, row_back, quarter)
+    out.step1()
+    for m in range(2):
+        send[m] = inner_cols(dfirst[m, half:, :], weights[...]).astype(LOW)
+    row_sum.core.start()
+    for m in range(2):
+        kept[m] = inner_cols(dfirst[m, :half, :], weights[...])
+    row_sum.pass_on()
+    qup.step1()
+    out.step2()
+    qup.step2()
+    dh1 = row_sum.result()
+    gain1_sum = jnp.sum(jnp.sum(dh1 * n1[...], axis=0), axis=0, keepdims=True)
+    back = dh1 * gain1[...]
+    share = Share(wire, grad_tokens, quarter)
+    share.begin(
+        (dy[...] + inv1[...] * (back - n1[...] * mean_of(back * n1[...]))).astype(LOW)
+    )
+    w, r = gain1_sum.shape[1] // 8, gain_c_sum.shape[1] // 8
+    for s in range(8):
+        sums[s] = jnp.concatenate(
+            [gain1_sum[:, s * w : (s + 1) * w], gain2_sum[:, s * w : (s + 1) * w],
+             gain_c_sum[:, s * r : (s + 1) * r]], axis=1
+        )
+    core_sums = wire.send(sums, sums_core, wire.core)
+    side_first.wait_recv()
+    first.step1()
+    out.step3()
+    core_sums.wait_recv()
+    core_sums.wait_send()
+    sums[...] = sums[...] + sums_core[...]
+    cross_sums = wire.send(sums, sums_cross, wire.cross)
+    qup.step3()
+    share.forward()
+    first.step2()
+    cross_sums.wait_recv()
+    cross_sums.wait_send()
+    sums[...] = sums[...] + sums_cross[...]
+    side_of = lambda p, s: sums.at[2 * p + s]
+    side_sends = [
+        wire.send(side_of(p, 1 - wire.side), sums_side.at[p], wire.beside) for p in range(4)
+    ]
+    out.finish()
+    first.step3()
+    for made in side_sends:
+        made.wait_recv()
+        made.wait_send()
+    line_sends = []
+    for d in range(1, 4):
+        for way, there in ((1, place + d <= 3), (-1, place - d >= 0)):
+            index = 2 * (d - 1) + (way < 0)
+            line_sends.append(
+                (wire.copy(sums_line.at[6 + index], sums_line.at[index],
+                           {"seq": wire.seq + 2 * way * d}), d, way, there)
+            )
+
+            @pl.when(there)
+            def _(index=index, d=d, way=way):
+                to = place + way * d
+                sums_line[6 + index] = sums[2 * to + wire.side] + sums_side[to]
+                line_sends[-1][0].start()
+
+            @pl.when((place - way * d < 0) | (place - way * d > 3))
+            def _(index=index):
+                sums_line[index] = jnp.zeros(sums_line.shape[1:], F32)
+
+    qup.finish()
+    first.finish()
+    cores = []
+    size = kv_out.shape[0] // 4
+    for k in range(4):
+        rows_of = pl.ds(pl.multiple_of(wire.blocks[k] * size, size), size)
+        if k:
+            device = {"mp": wire.blocks[k]}
+            cores.append(wire.send(kv_out.at[rows_of], kv_got.at[k], device))
+        else:
+            kv_got[0] = kv_out[rows_of]
+    total = sums[2 * place + wire.side] + sums_side[place]
+    for made, d, way, there in line_sends:
+        pl.when((place - way * d >= 0) & (place - way * d <= 3))(made.wait_recv)
+    for index in range(6):
+        total = total + sums_line[index]
+    gains[...] = total
+    for made in cores:
+        made.wait_recv()
+    columns = kv_out.shape[1]
+    for k in range(4):
+        at = pl.ds(pl.multiple_of(wire.blocks[k] * columns, columns), columns)
+        grad_kv[:, at] = kv_got[k]
+    share.end()
+    for made in (side_first, *cores):
+        made.wait_send()
+    for made, d, way, there in line_sends:
+        pl.when(there)(made.wait_send)
+    row_sum.end()
+    for chain in (out, qup, first):
+        chain.settle()
 
 
 def local(
@@ -847,103 +1197,154 @@
         return [(a, lead, m + micro * partner, None, first, count)
                 for a, lead, m, partner, first, count in spans]
 
-    send, keep = run(
+    send, keep, ffn_send, ffn_keep = run(
         functools.partial(hidden_back_body, micro),
         ids,
-        [*dg, *du, w_gate, w_up],
-        [whole((micro, half, width), LOW), whole((micro, half, width), F32)],
+        [*dg, *du, *hid, w_gate, w_up, w_down],
+        [whole((micro, half, width), LOW), whole((micro, half, width), F32)] * 2,
         order,
         name="hidden_back",
     )
     if narrow:
         y, n2, inv2, n1, inv1 = (stacked(k) for k in ("y", "n2", "inv2", "n1", "inv1"))
-        args = [(1, a) for a in (*hid, other(hid[0]), dz_mine, *dz_got)]
-        args += [(0, a) for a in (*h2_theirs, *dg)]
-        args += [(1, a) for a in (send, keep, n2, inv2, dz, gain2_row, out_proj, q_up,
-                                  key_ids[:, None])]
+        low = lambda *shape: pltpu.VMEM(shape, LOW)
+        full = lambda *shape: pltpu.VMEM(shape, F32)
+        near = lambda *arrays: [(1, a) for a in arrays]
+        far = lambda *arrays: [(0, a) for a in arrays]
+        columns = heads * head_dim
+        both_columns = rank + 2 * head_dim
+        first_columns = part + kv_part
+
+        args = near(*hid, other(hid[0]), dz_mine, *dz_got) + far(*h2_theirs, *dg)
+        args += near(send, keep, n2, inv2, dz, gain2_row, out_proj, q_up, key_ids[:, None])
         for m in range(micro):
-            args += [(1, a) for a in (qs[m], kv[m], os[m], lses[m],
-                                      jnp.stack([row_ids, starts[m]], 0), *tables[m])]
-        outs = [(1, whole(shape, dtype)) for shape, dtype in (
-            ((hidden, wide), F32), ((micro, quarter, width), F32), ((1, width), F32),
-            ((micro, line, rows, wide), LOW), ((micro, line, half, wide), LOW),
-            ((micro, rows, heads * head_dim), LOW), ((micro, half, rank), LOW),
-            ((micro, half, rank), F32), ((micro, key_count // 2, 2 * head_dim), LOW),
-            ((micro, key_count // 2, 2 * head_dim), F32))]
-        outs += [(0, whole((line, half, wide), LOW))] * 4 + [(0, whole((rows, hidden), LOW))] * 2
-        low = lambda *shape: pltpu.VMEM(shape, LOW)
+            args += near(qs[m], kv[m], os[m], lses[m], jnp.stack([row_ids, starts[m]], 0),
+                         *tables[m])
+        outs = near(
+            whole((hidden, wide), F32), whole((micro, quarter, width), F32),
+            whole((1, width), F32), whole((micro, line, rows, wide), LOW),
+            whole((micro, line, half, wide), LOW), whole((micro, rows, columns), LOW),
+            whole((micro, half, rank), LOW), whole((micro, half, rank), F32),
+            whole((micro, key_count // 2, 2 * head_dim), LOW),
+            whole((micro, key_count // 2, 2 * head_dim), F32),
+        ) + far(*[whole((line, half, wide), LOW)] * 4, *[whole((rows, hidden), LOW)] * 2)
         (grad_down, dy, gain2, dyl_mine, dyl_theirs, dqp, send, keep, kv_send, kv_keep,
          *exchanged) = mesh_run(
-            functools.partial(back1_body, quarter, scale, 1024),
-            args,
-            outs,
+            functools.partial(back1_body, quarter, scale, 1024), args, outs,
             [low(rows, hidden), low(5, wide, hidden), low(3, wide, hidden),
              low(micro, half, width), low(micro, quarter, width), low(micro, quarter, width),
-             low(micro, rows, width), pltpu.VMEM((heads, rows, head_dim), F32),
-             low(heads, rows, head_dim), pltpu.VMEM((heads, 8, rows), F32)],
-            1,
-            "back1",
-            60,
-            24,
-        )
-        gain2 = gain2[0]
-        order = [send]
-        h2_parts = [exchanged[0:2], exchanged[2:4]]
-        lefts, spans = both_sides(h2_mine, h2_parts)
-        chain_gate = Chain(lefts, [*dg, *exchanged[4:6]], terms_of(spans), (wide, hidden))
-        chain_up = Chain(lefts, with_other(du), terms_of(spans), (wide, hidden))
-        lefts, spans = both_sides(dyl_mine, from_other(dyl_theirs))
-        chain_out = Chain(
-            lefts, with_other(os), terms_of(spans), (wide, heads * head_dim), turned=True
-        )
+             low(micro, rows, width), full(heads, rows, head_dim), low(heads, rows, head_dim),
+             full(heads, 8, rows)],
+            1, "back1", 60, 24,
+        )
+
+        c = stacked("c").astype(F32)
+        inv_c = inverse_rms(c)
+        chat = to_natural(c * inv_c, 2)
+        kv_shape = (micro, 2 * line, 2, quarter, 2 * head_dim)
+        args = near(*dg, *exchanged[4:6], *du, *h2_mine, *exchanged[0:4])
+        args += far(kv_send.reshape(kv_shape)) + near(kv_keep.reshape(kv_shape)) + far(send)
+        args += near(keep, chat, inv_c, gain_c_row,
+                     jnp.stack([t[0][:quarter] for t in tables], 0),
+                     jnp.stack([t[1][:quarter] for t in tables], 0),
+                     *[pair[1] for pair in qn_sides], dqp)
+        args += far(dyl_theirs, *os, ffn_send) + near(ffn_keep, y)
+        side_rows = rank // seq
+        outs = near(whole((wide, hidden), F32), whole((wide, hidden), F32),
+                    whole((micro, rows, first_columns), LOW), whole((1, rank), F32))
+        outs += far(whole((line, side_rows, columns), LOW),
+                    *[whole((micro, line, half, wide), LOW)] * 2,
+                    *[whole((rows, columns), LOW)] * 2)
+        outs += near(whole((micro, rows, width), LOW))
+        kv_low = lambda *lead: low(*lead, quarter, 2 * head_dim)
+        (grad_gate, grad_up, dfirst, gain_c, qup_side, dyl_got, dyl_far, *o_other,
+         layer_out) = mesh_run(
+            functools.partial(back2_body, quarter), args, outs,
+            [low(rows, hidden), low(rows, hidden), low(5, wide, hidden), low(3, wide, hidden),
+             low(5, wide, hidden), low(3, wide, hidden), low(micro, half, rank),
+             low(micro, quarter, rank), low(micro, quarter, rank), kv_low(micro, 2 * line, 2),
+             kv_low(micro, 2 * line), kv_low(micro, 2 * line), kv_low(micro, line),
+             kv_low(micro, line), kv_low(3, micro), kv_low(3, micro),
+             full(micro, quarter, 2 * head_dim), low(micro, rows, both_columns),
+             low(line, side_rows, columns), low(micro, half, width), low(micro, quarter, width),
+             low(micro, quarter, width)],
+            2, "back2", 60, 40,
+        )
+
+        args = near(dfirst, first_weights, *[pair[0] for pair in h1_sides],
+                    *[pair[1] for pair in h1_sides], *os, *o_other, dyl_mine, dyl_got, dyl_far,
+                    *[pair[0] for pair in qn_sides], dqp, qup_side, n1, inv1, dy, gain1_row,
+                    gain2, gain_c)
+        block = width // 4 // seq
+        gain_columns = 2 * wide + side_rows
+        outs = near(whole((columns, wide), F32), whole((side_rows, columns), F32),
+                    whole((wide, part), F32), whole((block, 2 * head_dim), F32),
+                    whole((micro, rows, width), LOW), whole((1, gain_columns), F32))
+        grad_out, grad_qup, grad_qdown, grad_kv, input_grads, gains = mesh_run(
+            functools.partial(back3_body, quarter), args, outs,
+            [low(5, wide, columns), low(3, wide, columns), low(5, side_rows, columns),
+             low(3, side_rows, columns), low(5, wide, first_columns),
+             low(3, wide, first_columns), low(line, wide, first_columns),
+             low(line, wide, first_columns), low(micro, half, width), full(micro, half, width),
+             low(micro, half, width), low(micro, quarter, width), low(micro, quarter, width),
+             full(wide, kv_part), full(4, block, kv_part), full(seq, 1, gain_columns),
+             full(seq, 1, gain_columns), full(seq, 1, gain_columns), full(line, 1, gain_columns),
+             full(12, 1, gain_columns)],
+            3, "back3", 60, 44,
+        )
+        return (
+            layer_out, input_grads, gains[0, :wide], grad_qdown, gains[0, 2 * wide :], grad_qup,
+            grad_kv, grad_out, gains[0, wide : 2 * wide], grad_gate, grad_up, grad_down,
+        )
+
+    lefts, spans = both_sides(dz_mine, dz_got)
+    chain_down = Chain(lefts, with_other(hid), terms_of(spans), (wide, hidden), turned=True)
+    lefts, spans = both_sides(h2_mine, [list(p) for p in zip(*[from_other(t) for t in h2_theirs])])
+    chain_gate = Chain(lefts, with_other(dg), terms_of(spans), (wide, hidden))
+    chain_up = Chain(lefts, with_other(du), terms_of(spans), (wide, hidden))
+
+    order = chain_down.advance([send])
+    dh2 = sum_mp(send, keep)
+    y, n2, inv2, n1, inv1 = (stacked(k) for k in ("y", "n2", "inv2", "n1", "inv1"))
+    dz_own = dz[:, :quarter].astype(F32)
+    gain2 = jnp.sum(dh2 * n2, axis=(0, 1))
+    dy = dz_own + norm_backward(dh2 * gain2_row, n2, inv2)
+    for _ in range(2):
+        order = chain_down.advance(order)
+    order = chain_gate.advance(order)
+
+    def attend_back(which, pieces):
+        args = [*pieces, out_proj, q_up, key_ids[:, None]]
+        for m in which:
+            args += [qs[m], kv[m], os[m], lses[m], jnp.stack([row_ids, starts[m]], 0), *tables[m]]
+        n = len(which)
+        return run(
+            functools.partial(attend_back_body, scale, n, min(1024, key_count // 2)),
+            ids,
+            args,
+            [whole((n, rows, width), LOW), whole((n, rows, heads * head_dim), LOW),
+             whole((n, half, rank), LOW), whole((n, half, rank), F32),
+             whole((n, key_count // 2, 2 * head_dim), LOW),
+             whole((n, key_count // 2, 2 * head_dim), F32), *sides_shape(width, half, (n,))],
+            order,
+            scratch=[pltpu.VMEM((heads, rows, head_dim), F32),
+                     pltpu.VMEM((heads, rows, head_dim), LOW),
+                     pltpu.VMEM((heads, 8, rows), F32)],
+            name="attend_back",
+            limit=56,
+        )
+
+    pieces = gather_mp(dy.astype(LOW))
+    if key_count <= 2048:
+        made = attend_back(range(micro), pieces)
     else:
-        lefts, spans = both_sides(dz_mine, dz_got)
-        chain_down = Chain(lefts, with_other(hid), terms_of(spans), (wide, hidden), turned=True)
-        lefts, spans = both_sides(h2_mine, [list(p) for p in zip(*[from_other(t) for t in h2_theirs])])
-        chain_gate = Chain(lefts, with_other(dg), terms_of(spans), (wide, hidden))
-        chain_up = Chain(lefts, with_other(du), terms_of(spans), (wide, hidden))
-        order = chain_down.advance([send])
-        dh2 = sum_mp(send, keep)
-        y, n2, inv2, n1, inv1 = (stacked(k) for k in ("y", "n2", "inv2", "n1", "inv1"))
-        dz_own = dz[:, :quarter].astype(F32)
-        gain2 = jnp.sum(dh2 * n2, axis=(0, 1))
-        dy = dz_own + norm_backward(dh2 * gain2_row, n2, inv2)
-        for _ in range(2):
-            order = chain_down.advance(order)
-        order = chain_gate.advance(order)
-
-        def attend_back(which, pieces):
-            args = [*pieces, out_proj, q_up, key_ids[:, None]]
-            for m in which:
-                args += [qs[m], kv[m], os[m], lses[m], jnp.stack([row_ids, starts[m]], 0), *tables[m]]
-            n = len(which)
-            return run(
-                functools.partial(attend_back_body, scale, n, min(1024, key_count // 2)),
-                ids,
-                args,
-                [whole((n, rows, width), LOW), whole((n, rows, heads * head_dim), LOW),
-                 whole((n, half, rank), LOW), whole((n, half, rank), F32),
-                 whole((n, key_count // 2, 2 * head_dim), LOW),
-                 whole((n, key_count // 2, 2 * head_dim), F32), *sides_shape(width, half, (n,))],
-                order,
-                scratch=[pltpu.VMEM((heads, rows, head_dim), F32),
-                         pltpu.VMEM((heads, rows, head_dim), LOW),
-                         pltpu.VMEM((heads, 8, rows), F32)],
-                name="attend_back",
-                limit=56,
-            )
-
-        pieces = gather_mp(dy.astype(LOW))
-        if key_count <= 2048:
-            made = attend_back(range(micro), pieces)
-        else:
-            each = [attend_back([m], [p[m : m + 1] for p in pieces]) for m in range(micro)]
-            made = [jnp.concatenate(parts, 0) for parts in zip(*each)]
-        dyl, dqp, send, keep, kv_send, kv_keep, *made = made
-        order = [send]
-        dyl_mine, dyl_theirs = split_sides(made, dyl, half)
-        lefts, spans = both_sides(dyl_mine, from_other(dyl_theirs))
-        chain_out = Chain(lefts, with_other(os), terms_of(spans), (wide, heads * head_dim), turned=True)
+        each = [attend_back([m], [p[m : m + 1] for p in pieces]) for m in range(micro)]
+        made = [jnp.concatenate(parts, 0) for parts in zip(*each)]
+    dyl, dqp, send, keep, kv_send, kv_keep, *made = made
+    order = [send]
+    dyl_mine, dyl_theirs = split_sides(made, dyl, half)
+    lefts, spans = both_sides(dyl_mine, from_other(dyl_theirs))
+    chain_out = Chain(lefts, with_other(os), terms_of(spans), (wide, heads * head_dim), turned=True)
 
     def side_sum(lefts, rights, shape, after):
         terms = [(m, None, 0, m, 0, rows) for m in range(micro)]
@@ -995,8 +1396,7 @@
          lax.dynamic_slice_in_dim(both, rank + me * kv_part, kv_part, 2)], -1
     )
 
-    if not narrow:
-        grad_down, order = chain_down.finish(order)
+    grad_down, order = chain_down.finish(order)
     order = chain_gate.advance(order)
     order = chain_up.advance(order)
     order = chain_out.advance(order)
@@ -1040,10 +1440,7 @@
     dx = (dy + norm_backward(dh1 * gain1_row, n1, inv1)).astype(LOW)
     input_grads = put_natural(gather_mp(dx))
 
-    ffn = [dot(hid[m], w_down) for m in range(micro)]
-    ffn = sum_mp(
-        jnp.stack([f[half:] for f in ffn], 0).astype(LOW), jnp.stack([f[:half] for f in ffn], 0)
-    )
+    ffn = sum_mp(ffn_send, ffn_keep)
     layer_out = put_natural(gather_mp((y + ffn).astype(LOW)))
 
     gains = jnp.concatenate(

time: 599 us -> 533 us (0.89)
  Pallas kernels: 184 us -> 357 us
  starting transfers between devices: 139 us -> 30.6 us
  waiting for transfers between devices: 126 us -> 47 us
  other arithmetic: 55.6 us -> 34.2 us
  local copies, waits for them, and re-layouts: 72.9 us -> 54.5 us
  matrix products: 10.3 us -> 0 us
    pallas_call x1 -> x3, Pallas kernels: 87.4 us -> 291 us  [mesh_run(): pl.pallas_call(body, in_specs=[in_vmem() if kind else pl.BlockSpec(memory...]
    ppermute x42 -> x0, starting transfers between devices: 92.2 us -> none  [the longest x5 22.5 us: advance(): self.up = lax.ppermute(term_up, 'seq', goes_up)]
    ppermute x42 -> x0, waiting for transfers between devices: 66.3 us -> none  [the longest x5 16.7 us: advance(): self.down = lax.ppermute(term_down, 'seq', goes_down)]
    pallas_call x37 -> x8, Pallas kernels: 96.3 us -> 66.4 us  [run(): pl.pallas_call(without, grid_spec=pltpu.PrefetchScalarGridSpec(num_scalar...]
    ppermute x12 -> x4, waiting for transfers between devices: 48.2 us -> 24.3 us  [other(): return lax.ppermute(array, 'seq', beside)]
    dot_general x3 -> x0, matrix products: 10.3 us -> none  [the longest x2 9.03 us: dot(): return jnp.dot(left, right, preferred_element_type=F32)]
    ppermute x12 -> x4, starting transfers between devices: 13.3 us -> 5.1 us  [other(): return lax.ppermute(array, 'seq', beside)]
    ppermute x5 -> x2, waiting for transfers between devices: 3.34 us -> 9.68 us  [gather_mp(): near = lax.ppermute(piece, 'mp', CROSS)]
  transfers between devices with their start and end apart: 88 -> 25, of which waited for: 22 -> 7; matrix products, arithmetic and copies ran while one was open for 15% -> 8% of each run, Pallas kernels for 15% -> 12%
where the time goes in v5:
time: 533 us; the launch traced here: 528 us
  Pallas kernels  357 us (67%)
  local copies, waits for them, and re-layouts  54.5 us (10%)
  waiting for transfers between devices  47 us (9%)
  other arithmetic  34.2 us (6%)
  starting transfers between devices  30.6 us (6%)
    pallas_call x3, Pallas kernels, mesh_run(): pl.pallas_call(body, in_specs=[in_vmem() if kind else pl.BlockSpec(memory...  291 us
    pallas_call x8, Pallas kernels, run(): pl.pallas_call(without, grid_spec=pltpu.PrefetchScalarGridSpec(num_scalar...  66.4 us
    unnamed x201, local copies, waits for them, and re-layouts  42.1 us
    ppermute x4, waiting for transfers between devices, other(): return lax.ppermute(array, 'seq', beside)  24.3 us
    ppermute x6, starting transfers between devices, local(): lax.ppermute(packed, 'seq', [(i, i + 2 * d) for i in range(seq - 2 * d)])  17.4 us
    ppermute x2, waiting for transfers between devices, sum_mp(): got = lax.ppermute(kept[..., quarter:, :].astype(LOW), 'mp', CROSS)  11.7 us
  transfers between devices with their start and end apart: 25, of which 7 were waited for; matrix products, arithmetic and copies ran while one was open for 8% of the time, Pallas kernels for 12%

profile of v5, /device:TPU:0, one launch (start us, length us, event | category | flops | bytes accessed | tf_op | source)
XLA Modules:
  0.0 527.7 jit_solution(4479394673369490351)
XLA Ops:
  0.7 1.4 fusion.34
  7.2 1.8 copy-done.3
  9.0 1.6 copy-done.10
  12.5 2.4 first.2
  16.5 2.4 first.3
  19.7 5.6 %collective-permute-start.13 = (bf16[128,512]{1,0:T(8,128)(2,1)}, bf16[128,512]{1,0:T(8,128)(2,1)}, u32[]{:S(2)}, u32[]{:S(2)}) collective-permute-start(bf16[128,512]{1,0:T(8,128)(2,1)} %get-tuple-element.91), channel_id=1, source_target_pairs={{0,8},{4,12},{8,16},{12,20},{16,24},{20,28},{1,9},{5,13},{9,17},{1... | collective-permute-start | bytes 393224 | tf_op jit(solution)/shard_map/ppermute | solution.py:1112
  25.3 4.5 collective-permute-start.14
  29.8 1.9 collective-permute-start.15
  31.7 1.9 collective-permute-start.4
  33.6 1.9 collective-permute-start.2
  37.6 1.5 fusion.30
  39.7 1.3 select_select_fusion
  42.3 1.9 constant_dynamic-slice_fusion
  45.6 1.5 collective-permute-start.3
  47.7 2.6 copy-done.2
  50.3 1.6 copy-done.30
  51.9 4.8 cotangent.1
  56.7 1.5 copy-done.8
  59.2 1.5 collective-permute-start.11
  61.3 2.1 fusion.26
  63.4 1.5 collective-permute-start.23
  65.5 2.1 fusion.27
  67.5 1.5 collective-permute-start.5
  70.3 2.0 add.386.refs_18_
  73.0 16.9 %collective-permute-done.16 = bf16[4,128,512]{2,1,0:T(8,128)(2,1)} collective-permute-done((bf16[4,128,512]{2,1,0:T(8,128)(2,1)}, bf16[4,128,512]{2,1,0:T(8,128)(2,1)}, u32[]{:S(2)}, u32[]{:S(2)}) %collective-permute-start.16) | collective-permute-done | bytes 524320 | tf_op jit(solution)/shard_map/ppermute | solution.py:979
  89.8 1.3 fusion.24
  91.3 7.5 %collective-permute-done.5 = bf16[4,128,512]{2,1,0:T(8,128)(2,1)} collective-permute-done((bf16[4,128,512]{2,1,0:T(8,128)(2,1)}, bf16[4,128,512]{2,1,0:T(8,128)(2,1)}, u32[]{:S(2)}, u32[]{:S(2)}) %collective-permute-start.5) | collective-permute-done | bytes 524320 | tf_op jit(solution)/shard_map/ppermute | solution.py:979
  100.9 1.4 pad_maximum_fusion.2.refs_1_
  104.2 2.8 copy-done.7
  107.1 9.8 %attend.2 = (bf16[256,1024]{1,0:T(8,128)(2,1)}, bf16[4,256,256]{2,1,0:T(8,128)(2,1)S(1)}, bf16[256,1024]{1,0:T(8,128)(2,1)S(1)}, f32[4,256]{1,0:T(4,128)S(1)}, b...) custom-call(s32[2]{0:T(128)S(1)} %pad_add_fusion.3.refs_0_, ...), custom_call_target="tpu_custom_call" | custom-call | flops 1000 | bytes 1000 | tf_op jit(solution)/shard_map/attend/pallas_call | solution.py:82
  118.0 7.1 %attend.3 = (bf16[256,1024]{1,0:T(8,128)(2,1)}, bf16[4,256,256]{2,1,0:T(8,128)(2,1)S(1)}, bf16[256,1024]{1,0:T(8,128)(2,1)S(1)}, f32[4,256]{1,0:T(4,128)S(1)}, b...) custom-call(s32[2]{0:T(128)S(1)} %pad_add_fusion.3.refs_0_, ...), custom_call_target="tpu_custom_call" | custom-call | flops 1000 | bytes 1000 | tf_op jit(solution)/shard_map/attend/pallas_call | solution.py:82
  128.8 1.5 convert_add_fusion
  130.3 1.6 collective-permute-start.19
  132.7 6.9 %collective-permute-done.19 = bf16[64,2048]{1,0:T(8,128)(2,1)S(1)} collective-permute-done((bf16[64,2048]{1,0:T(8,128)(2,1)S(1)}, bf16[64,2048]{1,0:T(8,128)(2,1)S(1)}, u32[]{:S(2)}, u32[]{:S(2)}) %collective-permute-start.19) | collective-permute-done | bytes 262176 | tf_op jit(solution)/shard_map/ppermute | solution.py:983
  139.8 4.8 collective-permute-done.8
  145.9 1.5 collective-permute-start.20
  149.8 9.7 %collective-permute-done.9.refs_2_ = bf16[64,2048]{1,0:T(8,128)(2,1)S(1)} collective-permute-done((bf16[64,2048]{1,0:T(8,128)(2,1)S(1)}, bf16[64,2048]{1,0:T(8,128)(2,1)S(1)}, u32[]{:S(2)}, u32[]{:S(2)}) %collective-permute-start.9) | collective-permute-done | bytes 262176 | tf_op jit(solution)/shard_map/ppermute | solution.py:987
  163.6 2.3 pad_maximum_fusion.5.refs_12_
  166.7 2.6 copy-done
  169.3 1.8 copy-done.9
  172.2 7.5 %forward.2 = (bf16[256,2048]{1,0:T(8,128)(2,1)}, bf16[256,1408]{1,0:T(8,128)(2,1)S(1)}, bf16[256,1408]{1,0:T(8,128)(2,1)S(1)}, bf16[256,1408]{1,0:T(8,128)(2,1)S...) custom-call(s32[2]{0:T(128)S(1)} %pad_add_fusion.3.refs_0_, bf16[64,2048]{1,0:T(8,128)(2,1)S(1)} %copy-done.27, ...), custom_call_target="tpu_custom_call" | custom-call | flops 1000 | bytes 1000 | tf_op jit(solution)/shard_map/forward/pallas_call | solution.py:82
  179.8 1.6 collective-permute-start.22
  185.7 7.2 %forward.3 = (bf16[256,2048]{1,0:T(8,128)(2,1)}, bf16[256,1408]{1,0:T(8,128)(2,1)S(1)}, bf16[256,1408]{1,0:T(8,128)(2,1)S(1)}, bf16[256,1408]{1,0:T(8,128)(2,1)S...) custom-call(s32[2]{0:T(128)S(1)} %pad_add_fusion.3.refs_0_, ...), custom_call_target="tpu_custom_call" | custom-call | flops 1000 | bytes 1000 | tf_op jit(solution)/shard_map/forward/pallas_call | solution.py:82
  192.9 25.1 %hidden_back.1 = (bf16[2,128,2048]{2,1,0:T(8,128)(2,1)S(1)}, f32[2,128,2048]{2,1,0:T(8,128)S(1)}, bf16[2,128,2048]{2,1,0:T(8,128)(2,1)S(1)}, f32[2,128,2048]{2,1,0:T(8,128)S(1)}) custom-call(s32[2]{0:T(128)S(1)} %pad_add_fusion.3.refs_0_, bf16[256,1408]{1,0:T(8,128)(2,1)S(1)} %get-tuple-element.94.refs_1_.refs_8_.refs_0_, ...), custom_call_target="tpu_custom_call" | custom-call | flops 1000 | bytes 1000 | tf_op jit(solution)/shard_map/hidden_back/pallas_call | solution.py:82
  223.6 86.6 %back1.1 = (f32[1408,256]{1,0:T(8,128)}, f32[2,64,2048]{2,1,0:T(8,128)}, f32[1,2048]{1,0:T(1,128)}, bf16[2,4,256,256]{3,2,1,0:T(8,128)(2,1)}, bf16[2,4,128,256]{...) custom-call(bf16[256,1408]{1,0:T(8,128)(2,1)} %copy-done.17, ...), custom_call_target="tpu_custom_call" | custom-call | flops 1000 | bytes 1000 | tf_op jit(solution)/shard_map/back1/pallas_call | solution.py:435
  310.2 120.7 %back2.1 = (f32[256,1408]{1,0:T(8,128)}, f32[256,1408]{1,0:T(8,128)}, bf16[2,256,384]{2,1,0:T(8,128)(2,1)}, f32[1,1024]{1,0:T(1,128)}, bf16[4,128,1024]{2,1,0:T(...) custom-call(bf16[256,1408]{1,0:T(8,128)(2,1)} %copy-done.16, ...), custom_call_target="tpu_custom_call" | custom-call | flops 1000 | bytes 1000 | tf_op jit(solution)/shard_map/back2/pallas_call | solution.py:435
  430.9 83.3 %back3.1 = (f32[1024,256]{1,0:T(8,128)}, f32[128,1024]{1,0:T(8,128)}, f32[256,256]{1,0:T(8,128)}, f32[64,512]{1,0:T(8,128)}, bf16[2,256,2048]{2,1,0:T(8,128)(2,1)}, /*index=5*/f32[1,640]{1,0:T(1,128)}) custom-call(bf16[2,256,384]{2,1,0:T(8,128)(2,1)} %get-tuple-element.131.refs_0_, bf16[2048,384]{1,0:T(8,128)(2,1)} %pad_maximum_fusion.2.refs_1_, ...), custom_call_target="tpu_custom_call" | custom-call | flops 1000 | bytes 1000 | tf_op jit(solution)/shard_map/back3/pallas_call | solution.py:435
  518.9 1.3 copy.70
  (301 shorter events, 57.6 us)
Async XLA Ops:
  7.2 97.1 %copy-start.24 = (f32[256,128]{1,0:T(8,128)}, f32[256,128]{1,0:T(8,128)S(1)}, u32[]{:S(2)}) copy-start(f32[256,128]{1,0:T(8,128)S(1)} %get-tuple-element.216.refs_5_.refs_6_.refs_24_) | copy-start | bytes 393220
  7.2 97.1 %copy-start.25 = (f32[256,128]{1,0:T(8,128)}, f32[256,128]{1,0:T(8,128)S(1)}, u32[]{:S(2)}) copy-start(f32[256,128]{1,0:T(8,128)S(1)} %get-tuple-element.217.refs_6_.refs_7_.refs_25_) | copy-start | bytes 393220
  7.2 110.8 %copy-start.22 = (f32[256,128]{1,0:T(8,128)}, f32[256,128]{1,0:T(8,128)S(1)}, u32[]{:S(2)}) copy-start(f32[256,128]{1,0:T(8,128)S(1)} %get-tuple-element.196.refs_6_.refs_7_.refs_32_) | copy-start | bytes 393220
  7.2 110.8 %copy-start.23 = (f32[256,128]{1,0:T(8,128)}, f32[256,128]{1,0:T(8,128)S(1)}, u32[]{:S(2)}) copy-start(f32[256,128]{1,0:T(8,128)S(1)} %get-tuple-element.197.refs_5_.refs_6_.refs_31_) | copy-start | bytes 393220
  16.5 21.2 %copy-start.4 = (bf16[2,256,2048]{2,1,0:T(8,128)(2,1)S(1)}, bf16[2,256,2048]{2,1,0:T(8,128)(2,1)}, u32[]{:S(2)}) copy-start(bf16[2,256,2048]{2,1,0:T(8,128)(2,1)} %refs_1_.4) | copy-start | bytes 6291460
  19.7 19.4 %copy-start.48 = (bf16[4,256,256]{2,1,0:T(8,128)(2,1)}, bf16[4,256,256]{2,1,0:T(8,128)(2,1)S(1)}, u32[]{:S(2)}) copy-start(bf16[4,256,256]{2,1,0:T(8,128)(2,1)S(1)} %get-tuple-element.135.refs_5_) | copy-start | bytes 1572868
  19.7 25.9 %collective-permute-start.13 = (bf16[128,512]{1,0:T(8,128)(2,1)}, bf16[128,512]{1,0:T(8,128)(2,1)}, u32[]{:S(2)}, u32[]{:S(2)}) collective-permute-start(bf16[128,512]{1,0:T(8,128)(2,1)} %get-tuple-element.91), channel_id=1, source_target_pairs={{0,8},{4,12},{8,16},{12,20},{16,24},{20,28},{1,9},{5,13},{9,17},{1... | collective-permute-start | bytes 393224 | tf_op jit(solution)/shard_map/ppermute | solution.py:1112
  25.3 34.0 %collective-permute-start.14 = (bf16[128,512]{1,0:T(8,128)(2,1)}, bf16[128,512]{1,0:T(8,128)(2,1)}, u32[]{:S(2)}, u32[]{:S(2)}) collective-permute-start(bf16[128,512]{1,0:T(8,128)(2,1)} %get-tuple-element.91), channel_id=1, source_target_pairs={{0,16},{4,20},{8,24},{12,28},{1,17},{5,21},{9,25},{13,29},{2,18},{... | collective-permute-start | bytes 393224 | tf_op jit(solution)/shard_map/ppermute | solution.py:1112
  29.8 31.0 %collective-permute-start.15 = (bf16[128,512]{1,0:T(8,128)(2,1)}, bf16[128,512]{1,0:T(8,128)(2,1)}, u32[]{:S(2)}, u32[]{:S(2)}) collective-permute-start(bf16[128,512]{1,0:T(8,128)(2,1)} %get-tuple-element.91), channel_id=1, source_target_pairs={{0,24},{4,28},{1,25},{5,29},{2,26},{6,30},{3,27},{7,31}} | collective-permute-start | bytes 393224 | tf_op jit(solution)/shard_map/ppermute | solution.py:1112
  31.7 31.7 %collective-permute-start.4 = (bf16[128,512]{1,0:T(8,128)(2,1)}, bf16[128,512]{1,0:T(8,128)(2,1)}, u32[]{:S(2)}, u32[]{:S(2)}) collective-permute-start(bf16[128,512]{1,0:T(8,128)(2,1)} %get-tuple-element.85), channel_id=1, source_target_pairs={{0,24},{4,28},{1,25},{5,29},{2,26},{6,30},{3,27},{7,31}} | collective-permute-start | bytes 393224 | tf_op jit(solution)/shard_map/ppermute | solution.py:1112
  33.6 31.3 %collective-permute-start.2 = (bf16[128,512]{1,0:T(8,128)(2,1)}, bf16[128,512]{1,0:T(8,128)(2,1)}, u32[]{:S(2)}, u32[]{:S(2)}) collective-permute-start(bf16[128,512]{1,0:T(8,128)(2,1)} %get-tuple-element.85), channel_id=1, source_target_pairs={{0,8},{4,12},{8,16},{12,20},{16,24},{20,28},{1,9},{5,13},{9,17},{1... | collective-permute-start | bytes 393224 | tf_op jit(solution)/shard_map/ppermute | solution.py:1112
  45.6 19.9 %collective-permute-start.3 = (bf16[128,512]{1,0:T(8,128)(2,1)}, bf16[128,512]{1,0:T(8,128)(2,1)S(1)}, u32[]{:S(2)}, u32[]{:S(2)}) collective-permute-start(bf16[128,512]{1,0:T(8,128)(2,1)} %get-tuple-element.85), channel_id=1, source_target_pairs={{0,16},{4,20},{8,24},{12,28},{1,17},{5,21},{9,25},{13,29},{2,18},{... | collective-permute-start | bytes 393224 | tf_op jit(solution)/shard_map/ppermute | solution.py:1112
  59.2 45.0 %copy-start.14 = (bf16[2,256,2048]{2,1,0:T(8,128)(2,1)}, bf16[2,256,2048]{2,1,0:T(8,128)(2,1)S(1)}, u32[]{:S(2)}) copy-start(bf16[2,256,2048]{2,1,0:T(8,128)(2,1)S(1)} %get-tuple-element.87.refs_13_.refs_14_) | copy-start | bytes 6291460
  59.2 13.7 %collective-permute-start.11 = (bf16[256,256]{1,0:T(8,128)(2,1)S(1)}, bf16[256,256]{1,0:T(8,128)(2,1)S(1)}, u32[]{:S(2)}, u32[]{:S(2)}) collective-permute-start(bf16[256,256]{1,0:T(8,128)(2,1)S(1)} %get-tuple-element.86.refs_3_.refs_1_), channel_id=1, source_target_pairs={{0,2},{1,3},{2,0},{3,1},{4,6},{5,7},{6,4},{7,5},{8,10},{9,11},{10,... | collective-permute-start | bytes 393224 | tf_op jit(solution)/shard_map/ppermute | solution.py:1138
  60.7 40.0 %collective-permute-start = (bf16[256,256]{1,0:T(8,128)(2,1)S(1)}, bf16[256,256]{1,0:T(8,128)(2,1)S(1)}, u32[]{:S(2)}, u32[]{:S(2)}) collective-permute-start(bf16[256,256]{1,0:T(8,128)(2,1)S(1)} %get-tuple-element.84.refs_7_.refs_1_), channel_id=1, source_target_pairs={{0,2},{1,3},{2,0},{3,1},{4,6},{5,7},{6,4},{7,5},{8,10},{9,11},{10,... | collective-permute-start | bytes 393224 | tf_op jit(solution)/shard_map/ppermute | solution.py:1138
  63.4 65.2 %collective-permute-start.23 = (bf16[2,4,128,256]{3,2,1,0:T(8,128)(2,1)}, bf16[2,4,128,256]{3,2,1,0:T(8,128)(2,1)}, u32[]{:S(2)}, u32[]{:S(2)}) collective-permute-start(bf16[2,4,128,256]{3,2,1,0:T(8,128)(2,1)} %get-tuple-element.101), channel_id=1, source_target_pairs={{0,4},{4,0},{8,12},{12,8},{16,20},{20,16},{24,28},{28,24},{1,5},{5... | collective-permute-start | bytes 1572872 | tf_op jit(solution)/shard_map/ppermute | solution.py:979
  64.9 24.9 %collective-permute-start.16 = (bf16[4,128,512]{2,1,0:T(8,128)(2,1)}, bf16[4,128,512]{2,1,0:T(8,128)(2,1)}, u32[]{:S(2)}, u32[]{:S(2)}) collective-permute-start(bf16[4,128,512]{2,1,0:T(8,128)(2,1)} %get-tuple-element.183), channel_id=1, source_target_pairs={{0,4},{4,0},{8,12},{12,8},{16,20},{20,16},{24,28},{28,24},{1,5},{5... | collective-permute-start | bytes 1572872 | tf_op jit(solution)/shard_map/ppermute | solution.py:979
  67.5 31.2 %collective-permute-start.5 = (bf16[4,128,512]{2,1,0:T(8,128)(2,1)}, bf16[4,128,512]{2,1,0:T(8,128)(2,1)}, u32[]{:S(2)}, u32[]{:S(2)}) collective-permute-start(bf16[4,128,512]{2,1,0:T(8,128)(2,1)} %get-tuple-element.185), channel_id=1, source_target_pairs={{0,4},{4,0},{8,12},{12,8},{16,20},{20,16},{24,28},{28,24},{1,5},{5... | collective-permute-start | bytes 1572872 | tf_op jit(solution)/shard_map/ppermute | solution.py:979
  72.3 26.4 %copy-start.74 = (bf16[1,4,128,512]{3,2,1,0:T(8,128)(2,1)S(1)}, bf16[1,4,128,512]{3,2,1,0:T(8,128)(2,1)}, u32[]{:S(2)}) copy-start(bf16[1,4,128,512]{3,2,1,0:T(8,128)(2,1)} %get-tuple-element.184) | copy-start | bytes 1572868
  73.0 27.1 %copy-start.41 = (bf16[256,256]{1,0:T(8,128)(2,1)}, bf16[256,256]{1,0:T(8,128)(2,1)S(1)}, u32[]{:S(2)}) copy-start(bf16[256,256]{1,0:T(8,128)(2,1)S(1)} %collective-permute-done.11.refs_2_) | copy-start | bytes 393220
  91.2 12.6 %collective-permute-start.17 = (bf16[2,4,128,512]{3,2,1,0:T(8,128)(2,1)S(1)}, bf16[2,4,128,512]{3,2,1,0:T(8,128)(2,1)S(1)}, u32[]{:S(2)}, u32[]{:S(2)}) collective-permute-start(bf16[2,4,128,512]{3,2,1,0:T(8,128)(2,1)S(1)} %get-tuple-element.171), channel_id=1, source_target_pairs={{0,1},{1,0},{2,3},{3,2},{4,5},{5,4},{6,7},{7,6},{8,9},{9,8},{10,11... | collective-permute-start | bytes 3145736 | tf_op jit(solution)/shard_map/ppermute | solution.py:1118
  100.1 3.9 collective-permute-start.6
  100.2 3.0 collective-permute-start.12
  100.8 2.8 collective-permute-start.1
  103.9 14.0 %copy-start.5 = (bf16[2,2,4,128,512]{4,3,2,1,0:T(8,128)(2,1)}, bf16[2,2,4,128,512]{4,3,2,1,0:T(8,128)(2,1)S(1)}, u32[]{:S(2)}) copy-start(bf16[2,2,4,128,512]{4,3,2,1,0:T(8,128)(2,1)S(1)} %pad_maximum_fusion.1) | copy-start | bytes 6291460
  126.0 40.7 %copy-start.13 = (bf16[256,1024]{1,0:T(8,128)(2,1)}, bf16[256,1024]{1,0:T(8,128)(2,1)S(1)}, u32[]{:S(2)}) copy-start(bf16[256,1024]{1,0:T(8,128)(2,1)S(1)} %get-tuple-element.93.refs_7_.refs_28_.refs_26_) | copy-start | bytes 1572868
  126.0 2.8 collective-permute-start.18
  126.3 5.5 %collective-permute-start.7 = (bf16[128,2048]{1,0:T(8,128)(2,1)}, bf16[128,2048]{1,0:T(8,128)(2,1)S(1)}, u32[]{:S(2)}, u32[]{:S(2)}) collective-permute-start(bf16[128,2048]{1,0:T(8,128)(2,1)} %get-tuple-element.89), channel_id=1, source_target_pairs={{0,1},{1,0},{2,3},{3,2},{4,5},{5,4},{6,7},{7,6},{8,9},{9,8},{10,11... | collective-permute-start | bytes 1572872 | tf_op jit(solution)/shard_map/ppermute | solution.py:982
  128.7 94.0 %collective-permute-start.24 = (bf16[2,4,128,256]{3,2,1,0:T(8,128)(2,1)}, bf16[2,4,128,256]{3,2,1,0:T(8,128)(2,1)}, u32[]{:S(2)}, u32[]{:S(2)}) collective-permute-start(bf16[2,4,128,256]{3,2,1,0:T(8,128)(2,1)} %collective-permute-done.23.refs_4_), channel_id=1, source_target_pairs={{0,1},{1,0},{2,3},{3,2},{4,5},{5,4},{6,7},{7,6},{8,9},{9,8},{10,11... | collective-permute-start | bytes 1572872 | tf_op jit(solution)/shard_map/ppermute | solution.py:1010
  130.3 9.2 %collective-permute-start.19 = (bf16[64,2048]{1,0:T(8,128)(2,1)S(1)}, bf16[64,2048]{1,0:T(8,128)(2,1)S(1)}, u32[]{:S(2)}, u32[]{:S(2)}) collective-permute-start(bf16[64,2048]{1,0:T(8,128)(2,1)S(1)} %slice.159), channel_id=1, source_target_pairs={{0,2},{1,3},{2,0},{3,1},{4,6},{5,7},{6,4},{7,5},{8,10},{9,11},{10,... | collective-permute-start | bytes 786440 | tf_op jit(solution)/shard_map/ppermute | solution.py:983
  132.1 12.5 %collective-permute-start.8 = (bf16[64,2048]{1,0:T(8,128)(2,1)S(1)}, bf16[64,2048]{1,0:T(8,128)(2,1)S(1)}, u32[]{:S(2)}, u32[]{:S(2)}) collective-permute-start(bf16[64,2048]{1,0:T(8,128)(2,1)S(1)} %slice.160), channel_id=1, source_target_pairs={{0,2},{1,3},{2,0},{3,1},{4,6},{5,7},{6,4},{7,5},{8,10},{9,11},{10,... | collective-permute-start | bytes 786440 | tf_op jit(solution)/shard_map/ppermute | solution.py:983
  144.8 15.5 %copy-start.68 = (f32[64,2048]{1,0:T(8,128)}, f32[64,2048]{1,0:T(8,128)S(1)}, u32[]{:S(2)}) copy-start(f32[64,2048]{1,0:T(8,128)S(1)} %get-tuple-element.163) | copy-start | bytes 1572868
  145.9 35.5 %collective-permute-start.20 = (bf16[64,2048]{1,0:T(8,128)(2,1)}, bf16[64,2048]{1,0:T(8,128)(2,1)}, u32[]{:S(2)}, u32[]{:S(2)}) collective-permute-start(bf16[64,2048]{1,0:T(8,128)(2,1)} %get-tuple-element.177.refs_1_), channel_id=1, source_target_pairs={{0,2},{1,3},{2,0},{3,1},{4,6},{5,7},{6,4},{7,5},{8,10},{9,11},{10,... | collective-permute-start | bytes 786440 | tf_op jit(solution)/shard_map/ppermute | solution.py:987
  148.3 11.2 %collective-permute-start.9 = (bf16[64,2048]{1,0:T(8,128)(2,1)S(1)}, bf16[64,2048]{1,0:T(8,128)(2,1)S(1)}, u32[]{:S(2)}, u32[]{:S(2)}) collective-permute-start(bf16[64,2048]{1,0:T(8,128)(2,1)S(1)} %get-tuple-element.175.refs_1_), channel_id=1, source_target_pairs={{0,2},{1,3},{2,0},{3,1},{4,6},{5,7},{6,4},{7,5},{8,10},{9,11},{10,... | collective-permute-start | bytes 786440 | tf_op jit(solution)/shard_map/ppermute | solution.py:987
  159.5 26.1 %slice-start = ((s8[5767168]{0:T(1024)(128)(4,1)}), s8[1572864]{0:T(1024)(128)(4,1)S(1)}, s32[]{:S(2)}) async-start(s8[5767168]{0:T(1024)(128)(4,1)} %bitcast.99), calls=%async_computation | async-start | bytes 3145728
  160.4 5.5 %collective-permute-start.10 = (bf16[128,2048]{1,0:T(8,128)(2,1)}, bf16[128,2048]{1,0:T(8,128)(2,1)S(1)}, u32[]{:S(2)}, u32[]{:S(2)}) collective-permute-start(bf16[128,2048]{1,0:T(8,128)(2,1)} %pad_maximum_fusion.9), channel_id=1, source_target_pairs={{0,1},{1,0},{2,3},{3,2},{4,5},{5,4},{6,7},{7,6},{8,9},{9,8},{10,11... | collective-permute-start | bytes 1572872 | tf_op jit(solution)/shard_map/ppermute | solution.py:989
  172.2 13.5 %slice-start.1 = ((s8[5767168]{0:T(1024)(128)(4,1)}), s8[4194304]{0:T(1024)(128)(4,1)S(1)}, s32[]{:S(2)}) async-start(s8[5767168]{0:T(1024)(128)(4,1)} %bitcast.99), calls=%async_computation.1 | async-start | bytes 8388608
  179.8 13.1 %copy-start.16 = (bf16[256,1408]{1,0:T(8,128)(2,1)}, bf16[256,1408]{1,0:T(8,128)(2,1)S(1)}, u32[]{:S(2)}) copy-start(bf16[256,1408]{1,0:T(8,128)(2,1)S(1)} %get-tuple-element.94.refs_1_.refs_8_.refs_0_) | copy-start | bytes 2162692
  179.8 13.1 %copy-start.17 = (bf16[256,1408]{1,0:T(8,128)(2,1)}, bf16[256,1408]{1,0:T(8,128)(2,1)S(1)}, u32[]{:S(2)}) copy-start(bf16[256,1408]{1,0:T(8,128)(2,1)S(1)} %get-tuple-element.97.refs_7_.refs_5_.refs_0_) | copy-start | bytes 2162692
  179.8 13.1 %copy-start.20 = (bf16[256,1408]{1,0:T(8,128)(2,1)}, bf16[256,1408]{1,0:T(8,128)(2,1)S(1)}, u32[]{:S(2)}) copy-start(bf16[256,1408]{1,0:T(8,128)(2,1)S(1)} %get-tuple-element.104.refs_3_.refs_4_) | copy-start | bytes 2162692
  179.8 42.9 %collective-permute-start.22 = (bf16[256,1408]{1,0:T(8,128)(2,1)S(1)}, bf16[256,1408]{1,0:T(8,128)(2,1)S(1)}, u32[]{:S(2)}, u32[]{:S(2)}) collective-permute-start(bf16[256,1408]{1,0:T(8,128)(2,1)S(1)} %get-tuple-element.97.refs_7_.refs_5_.refs_0_), channel_id=1, source_target_pairs={{0,4},{4,0},{8,12},{12,8},{16,20},{20,16},{24,28},{28,24},{1,5},{5... | collective-permute-start | bytes 2162696 | tf_op jit(solution)/shard_map/ppermute | solution.py:979
  182.5 3.2 collective-permute-start.21
  192.8 25.2 %copy-start.18 = (bf16[256,1408]{1,0:T(8,128)(2,1)}, bf16[256,1408]{1,0:T(8,128)(2,1)S(1)}, u32[]{:S(2)}) copy-start(bf16[256,1408]{1,0:T(8,128)(2,1)S(1)} %get-tuple-element.98.refs_2_.refs_9_.refs_1_) | copy-start | bytes 2162692
  192.9 25.2 %copy-start.19 = (bf16[256,1408]{1,0:T(8,128)(2,1)}, bf16[256,1408]{1,0:T(8,128)(2,1)S(1)}, u32[]{:S(2)}) copy-start(bf16[256,1408]{1,0:T(8,128)(2,1)S(1)} %get-tuple-element.99.refs_6_.refs_10_.refs_1_) | copy-start | bytes 2162692
  192.9 25.2 %copy-start.21 = (bf16[256,1408]{1,0:T(8,128)(2,1)}, bf16[256,1408]{1,0:T(8,128)(2,1)S(1)}, u32[]{:S(2)}) copy-start(bf16[256,1408]{1,0:T(8,128)(2,1)S(1)} %get-tuple-element.105.refs_4_.refs_5_) | copy-start | bytes 2162692
  192.9 25.2 %copy-start.52 = (bf16[4,256,256]{2,1,0:T(8,128)(2,1)}, bf16[4,256,256]{2,1,0:T(8,128)(2,1)S(1)}, u32[]{:S(2)}) copy-start(bf16[4,256,256]{2,1,0:T(8,128)(2,1)S(1)} %get-tuple-element.115.refs_7_) | copy-start | bytes 1572868
  192.9 25.2 %copy-start.58 = (bf16[4,128,256]{2,1,0:T(8,128)(2,1)}, bf16[4,128,256]{2,1,0:T(8,128)(2,1)S(1)}, u32[]{:S(2)}) copy-start(bf16[4,128,256]{2,1,0:T(8,128)(2,1)S(1)} %get-tuple-element.103.refs_7_) | copy-start | bytes 786436
  430.9 85.7 %copy-start.72 = (bf16[2,256,2048]{2,1,0:T(8,128)(2,1)S(1)}, bf16[2,256,2048]{2,1,0:T(8,128)(2,1)}, u32[]{:S(2)}) copy-start(bf16[2,256,2048]{2,1,0:T(8,128)(2,1)} %get-tuple-element.242) | copy-start | bytes 6291460
  (73 other events, 315.3 us)
